TPU v7x, 32 devices: a whole 2x2x4 slice. The times are simulated.
32 devices in a mesh: aux: 4 (over z), bas: 8 (over y, x, core).
Axes of the slice: x: 2, y: 2, z: 4, core: 2. Of those that a mesh axis runs over, the one named last changes fastest.
Arguments:
- coefficients: bfloat16 [4096, 256], P('bas'), may hold values from -0.5 to 0.5
- tensor: bfloat16 [32, 32, 3, 128, 128], P('aux', 'bas'), may hold values from -0.62890625 to 0.62890625
- pattern: int32 [32, 3], replicated, may hold values from -1 to 31, as said below
Outputs:
- exchange_tiles: float32 [32, 3, 128, 128], P('bas')
Inputs may be any that keep to these rules, and one draw needn't show every extreme that they name: `pattern`: row m lists distinct basis blocks that lie in [(4 * (m // 4) - 4), (4 * (m // 4) + 8)); its filled slots come first and its empty slots (-1) last. Rows hold from 1 to 3 filled slots; some row is full.
All inputs are finite; a program needn't handle non-finite values.
Results may differ from a plain program's by a relative error of at most 0.0012.
Values may be sent and summed in bfloat16 or wider, within the bound.
No kernel may reach another device: no remote copies, remote signals or barrier semaphores. Data moves between devices by JAX's collectives and lax.ppermute only.
A program may use at most 64 MiB of HBM per device.

v0:
```python
import jax
import jax.numpy as jnp
from jax import lax
from jax.sharding import PartitionSpec as P


def with_halo(value, sides, width):
    for axis, dim in sides:
        devices, length = (lax.axis_size(axis), value.shape[dim])
        up = [(i, (i + 1) % devices) for i in range(devices - 1)]
        down = [(j, i) for i, j in up]
        last = lax.slice_in_dim(value, length - width, length, axis=dim)
        leading = lax.slice_in_dim(value, 0, width, axis=dim)
        before = lax.ppermute(last, axis, up)
        after = lax.ppermute(leading, axis, down)
        value = jnp.concatenate([before, value, after], axis=dim)
    return value


def pick_rows(picker, source):
    return jnp.einsum("mjr,prci->pmjci", picker, source, preferred_element_type=jnp.float32).astype(
        jnp.bfloat16
    )


def pair_tiles(first_half, partner):
    return jnp.einsum("pmai,pmjci->mjac", first_half, partner, preferred_element_type=jnp.float32)


def body(coefficients, tensor, pattern):
    blocks = tensor.shape[1]
    block_width = tensor.shape[3]
    occupied = coefficients.shape[1]
    device = lax.axis_index("bas")
    owned_rows = lax.dynamic_slice_in_dim(pattern, device * blocks, blocks, 0)
    window = with_halo(coefficients, (("bas", 0),), blocks * block_width)
    window = window.reshape(3 * blocks, block_width, occupied)
    offset = (device - 1) * blocks
    places = jnp.arange(3 * blocks, dtype=jnp.int32)
    local_index = jnp.where(owned_rows >= 0, owned_rows - offset, -1)
    picker = (local_index[:, :, None] == places[None, None, :]).astype(jnp.bfloat16)
    chosen = jnp.einsum("mjr,rbi->mjbi", picker, window, preferred_element_type=jnp.float32).astype(
        jnp.bfloat16
    )
    half_form = jnp.einsum(
        "pmjab,mjbi->pmai", tensor, chosen, preferred_element_type=jnp.float32
    ).astype(jnp.bfloat16)
    beside_all = with_halo(half_form, (("bas", 1),), blocks)
    tile_sums = pair_tiles(half_form, pick_rows(picker, beside_all))
    return lax.psum(tile_sums, "aux")


def solution(mesh):
    return jax.shard_map(
        body,
        mesh=mesh,
        in_specs=(P("bas", None), P("aux", "bas", None, None, None), P()),
        out_specs=P("bas", None, None, None),
        check_vma=False,
    )
```

profile of v0, /device:TPU:0, one launch (start us, length us, event | category | flops | bytes accessed | tf_op | source)
XLA Modules:
  0.0 167.5 jit_solution(9758675051137600254)
XLA Ops:
  6.5 0.0 copy-start
  6.5 0.0 all-reduce.2.cloned.1.call-start
  6.5 2.6 %collective-permute-start = (bf16[512,256]{1,0:T(8,128)(2,1)}, bf16[512,256]{1,0:T(8,128)(2,1)S(1)}, u32[]{:S(2)}, u32[]{:S(2)}) collective-permute-start(bf16[512,256]{1,0:T(8,128)(2,1)} %param.3), channel_id=1, source_target_pairs={{0,1},{1,2},{2,3},{3,4},{4,5},{5,6},{6,7},{8,9},{9,10},{10,11},{11... | collective-permute-start | bytes 786440 | tf_op jit(solution)/shard_map/ppermute | solution.py:14
  9.2 1.3 collective-permute-start.1
  10.5 0.8 subtract_select_fusion
  11.2 0.1 copy.4
  11.3 0.0 collective-permute-done
  11.3 3.7 %collective-permute-done.1 = bf16[512,256]{1,0:T(8,128)(2,1)} collective-permute-done((bf16[512,256]{1,0:T(8,128)(2,1)}, bf16[512,256]{1,0:T(8,128)(2,1)}, u32[]{:S(2)}, u32[]{:S(2)}) %collective-permute-start.1) | collective-permute-done | bytes 262176 | tf_op jit(solution)/shard_map/ppermute | solution.py:15
  15.0 1.1 pad_maximum_fusion
  16.1 1.8 %fusion.13 = bf16[4,3,128,256]{3,1,2,0:T(4,128)(2,1)} fusion(bf16[12,128,256,1]{2,1,0,3:T(8,128)(2,1)S(1)} %bitcast.43, s32[4,3]{1,0:T(4,128)S(1)} %copy.4), kind=kOutput, calls=%fused_computation.9 | convolution fusion | flops 9437328 | bytes 1572912 | tf_op jit(solution)/shard_map/mjr,rbi->mjbi/dot_general | solution.py:42
  17.9 2.3 %copy.10 = bf16[4,3,128,256]{2,3,1,0:T(8,128)(2,1)} copy(bf16[4,3,128,256]{3,1,2,0:T(4,128)(2,1)} %fusion.13) | data formatting | bytes 1572864 | tf_op jit(solution)/shard_map/mjr,rbi->mjbi/dot_general | solution.py:42
  20.2 0.0 copy-done
  20.2 2.4 %bitcast_convert_fusion = bf16[4,256,8,128]{3,1,2,0:T(8,128)(2,1)S(1)} fusion(bf16[8,4,3,128,128]{4,3,2,1,0:T(8,128)(2,1)S(1)} %copy-done, bf16[4,3,128,256]{2,3,1,0:T(8,128)(2,1)} %copy.10), kind=kOutput, calls=%fused_computation.4 | convolution fusion | flops 806354944 | bytes 6029312 | tf_op jit(solution)/shard_map/pmjab,mjbi->pmai/dot_general | solution.py:45
  22.6 1.3 collective-permute-start.3
  23.9 7.5 %collective-permute-start.2 = (bf16[8,4,128,256]{2,3,0,1:T(8,128)(2,1)S(1)}, bf16[8,4,128,256]{2,3,0,1:T(8,128)(2,1)S(1)}, u32[]{:S(2)}, u32[]{:S(2)}) collective-permute-start(bf16[8,4,128,256]{2,3,0,1:T(8,128)(2,1)S(1)} %bitcast.45), channel_id=1, source_target_pairs={{0,1},{1,2},{2,3},{3,4},{4,5},{5,6},{6,7},{8,9},{9,10},{10,11},{11... | collective-permute-start | bytes 6291464 | tf_op jit(solution)/shard_map/ppermute | solution.py:14
  31.4 1.6 collective-permute-done.3
  33.0 2.1 %collective-permute-done.2 = bf16[8,4,128,256]{2,3,0,1:T(8,128)(2,1)S(1)} collective-permute-done((bf16[8,4,128,256]{2,3,0,1:T(8,128)(2,1)S(1)}, bf16[8,4,128,256]{2,3,0,1:T(8,128)(2,1)S(1)}, u32[]{:S(2)}, u32[]{:S(2)}) %collective-permute-start.2) | collective-permute-done | bytes 2097184 | tf_op jit(solution)/shard_map/ppermute | solution.py:14
  35.0 5.0 %maximum_bitcast_fusion = bf16[8,12,128,256,1]{2,3,0,1,4:T(8,128)(2,1)} fusion(bf16[8,4,128,256]{2,3,0,1:T(8,128)(2,1)S(1)} %collective-permute-done.3, bf16[8,4,128,256]{2,3,0,1:T(8,128)(2,1)S(1)} %bitcast.46, bf16[8,4,128,256]{2,3,0,1:T(8,128)(2,1)S(1)} %collective-permute-done.2), kind=kLoop, calls=%fused_computation.3 | loop fusion | flops 6291456 | bytes 12582912 | tf_op jit(solution)/shard_map/concatenate | solution.py:16
  40.0 11.5 %copy.13 = bf16[8,12,128,256,1]{3,1,4,2,0:T(8,128)(2,1)} copy(bf16[8,12,128,256,1]{2,3,0,1,4:T(8,128)(2,1)} %maximum_bitcast_fusion) | data formatting | bytes 12582912 | tf_op jit(solution)/shard_map/concatenate | solution.py:16
  51.5 10.2 %fusion.20 = bf16[8,128,256,4,3]{2,4,3,1,0:T(4,128)(2,1)} fusion(bf16[8,12,128,256,1]{3,1,4,2,0:T(8,128)(2,1)} %copy.13, s32[4,3]{1,0:T(4,128)S(1)} %copy.4), kind=kOutput, calls=%fused_computation.17 | convolution fusion | flops 75497616 | bytes 12582960 | tf_op jit(solution)/shard_map/mjr,prci->pmjci/dot_general | solution.py:21
  61.7 8.4 %fusion.8 = f32[4,3,128,128]{2,3,1,0:T(8,128)} fusion(bf16[4,256,8,128]{3,1,2,0:T(8,128)(2,1)} %copy-done.1, bf16[8,128,256,4,3]{2,4,3,1,0:T(4,128)(2,1)} %fusion.20), kind=kOutput, calls=%fused_computation.8 | convolution fusion | flops 805306368 | bytes 9175040 | tf_op jit(solution)/shard_map/pmai,pmjci->mjac/dot_general | solution.py:27
  70.2 0.0 all-reduce.2.cloned.1.call-update
  70.2 88.2 %all-reduce.2.cloned.1.call-done = f32[4,3,128,128]{2,3,1,0:T(8,128)} async-done(((f32[4,3,128,128]{2,3,1,0:T(8,128)}), f32[4,3,128,128]{2,3,1,0:T(8,128)}) %all-reduce.2.cloned.1.call-update) | async-done | bytes 786448 | tf_op jit(solution)/shard_map/psum | solution.py:50
  158.4 2.3 %copy.7 = f32[4,3,128,128]{3,2,1,0:T(8,128)} copy(f32[4,3,128,128]{2,3,1,0:T(8,128)} %all-reduce.2.cloned.1.call-done) | data formatting | bytes 1572864 | tf_op jit(solution)/shard_map/psum | solution.py:50
  (2 shorter events, 0.0 us)
Async XLA Ops:
  6.5 13.7 %copy-start = (bf16[8,4,3,128,128]{4,3,2,1,0:T(8,128)(2,1)S(1)}, bf16[8,4,3,128,128]{4,3,2,1,0:T(8,128)(2,1)}, u32[]{:S(2)}) copy-start(bf16[8,4,3,128,128]{4,3,2,1,0:T(8,128)(2,1)} %param.4) | copy-start | bytes 9437188
  6.5 151.9 %all-reduce.2.cloned.1.call-start = ((), (), s32[]{:S(2)}) async-start(), calls=%async_computation | async-start | bytes 1572864 | tf_op jit(solution)/shard_map/psum | solution.py:50
  6.5 4.8 %collective-permute-start = (bf16[512,256]{1,0:T(8,128)(2,1)}, bf16[512,256]{1,0:T(8,128)(2,1)S(1)}, u32[]{:S(2)}, u32[]{:S(2)}) collective-permute-start(bf16[512,256]{1,0:T(8,128)(2,1)} %param.3), channel_id=1, source_target_pairs={{0,1},{1,2},{2,3},{3,4},{4,5},{5,6},{6,7},{8,9},{9,10},{10,11},{11... | collective-permute-start | bytes 786440 | tf_op jit(solution)/shard_map/ppermute | solution.py:14
  9.2 5.9 %collective-permute-start.1 = (bf16[512,256]{1,0:T(8,128)(2,1)}, bf16[512,256]{1,0:T(8,128)(2,1)}, u32[]{:S(2)}, u32[]{:S(2)}) collective-permute-start(bf16[512,256]{1,0:T(8,128)(2,1)} %param.3), channel_id=1, source_target_pairs={{1,0},{2,1},{3,2},{4,3},{5,4},{6,5},{7,6},{9,8},{10,9},{11,10},{12... | collective-permute-start | bytes 786440 | tf_op jit(solution)/shard_map/ppermute | solution.py:15
  22.6 12.4 %copy-start.1 = (bf16[4,256,8,128]{3,1,2,0:T(8,128)(2,1)}, bf16[4,256,8,128]{3,1,2,0:T(8,128)(2,1)S(1)}, u32[]{:S(2)}) copy-start(bf16[4,256,8,128]{3,1,2,0:T(8,128)(2,1)S(1)} %bitcast_convert_fusion) | copy-start | bytes 6291460
  22.6 10.3 %collective-permute-start.3 = (bf16[8,4,128,256]{2,3,0,1:T(8,128)(2,1)S(1)}, bf16[8,4,128,256]{2,3,0,1:T(8,128)(2,1)S(1)}, u32[]{:S(2)}, u32[]{:S(2)}) collective-permute-start(bf16[8,4,128,256]{2,3,0,1:T(8,128)(2,1)S(1)} %bitcast.44), channel_id=1, source_target_pairs={{1,0},{2,1},{3,2},{4,3},{5,4},{6,5},{7,6},{9,8},{10,9},{11,10},{12... | collective-permute-start | bytes 6291464 | tf_op jit(solution)/shard_map/ppermute | solution.py:15
  23.9 11.1 %collective-permute-start.2 = (bf16[8,4,128,256]{2,3,0,1:T(8,128)(2,1)S(1)}, bf16[8,4,128,256]{2,3,0,1:T(8,128)(2,1)S(1)}, u32[]{:S(2)}, u32[]{:S(2)}) collective-permute-start(bf16[8,4,128,256]{2,3,0,1:T(8,128)(2,1)S(1)} %bitcast.45), channel_id=1, source_target_pairs={{0,1},{1,2},{2,3},{3,4},{4,5},{5,6},{6,7},{8,9},{9,10},{10,11},{11... | collective-permute-start | bytes 6291464 | tf_op jit(solution)/shard_map/ppermute | solution.py:14
Sparse Core Ops, SparseCore 0:
  70.3 88.0 all-reduce.1
where the time goes:
time: 168 us
  waiting for transfers between devices  95.6 us (57%)
  matrix products  22.8 us (14%)
  local copies, waits for them, and re-layouts  16.2 us (10%)
  between operations  13.5 us (8%)
  starting transfers between devices  12.7 us (8%)
  other arithmetic  6.84 us (4%)
    psum x1, waiting for transfers between devices, body(): return lax.psum(tile_sums, 'aux')  88.2 us
    concatenate x1, local copies, waits for them, and re-layouts, with_halo(): value = jnp.concatenate([before, value, after], axis=dim)  11.5 us
    dot_general x1, matrix products, pick_rows(): jnp.einsum('mjr,prci->pmjci', picker, source, preferred_element_type=jnp....  10.2 us
    ppermute x2, starting transfers between devices, with_halo(): before = lax.ppermute(last, axis, up)  10.1 us
    dot_general x1, matrix products, pair_tiles(): jnp.einsum('pmai,pmjci->mjac', first_half, partner, preferred_element_typ...  8.43 us
    concatenate x2, other arithmetic, with_halo(): value = jnp.concatenate([before, value, after], axis=dim)  6.08 us
    ppermute x2, waiting for transfers between devices, with_halo(): after = lax.ppermute(leading, axis, down)  5.28 us
  transfers between devices with their start and end apart: 5, of which 4 were waited for; matrix products, arithmetic and copies ran while one was open for 1% of the time, Pallas kernels for 0%

commit v1 on v0

v1 whole, which is shorter than its diff:
```python
import functools

import jax
import jax.numpy as jnp
from jax import lax
from jax.experimental import pallas as pl
from jax.experimental.pallas import tpu as pltpu
from jax.sharding import PartitionSpec as P

CHUNKS = 2
SCALE_ROWS = 16
VMEM = pl.BlockSpec(memory_space=pltpu.VMEM)
SMEM = pl.BlockSpec(memory_space=pltpu.SMEM)


def params(mib):
    return pltpu.CompilerParams(vmem_limit_bytes=mib << 20)


def half_kernel(pattern, own, beside, across, tensor, whole, *rest):
    parts, chosen = rest[:-1], rest[-1]
    aux, blocks, slots, width, _ = tensor.shape
    occupied = own.shape[1]
    rows, columns = parts[0].shape[1:]
    device = lax.axis_index("bas")
    for m in range(blocks):
        for j in range(slots):
            place = pattern[device * blocks + m, j]
            group, start = place // blocks, pl.multiple_of((place % blocks) * width, width)
            into = chosen.at[pl.ds(j * width, width)]

            @pl.when(place < 0)
            def _():
                into[...] = jnp.zeros((width, occupied), jnp.bfloat16)

            for source, held in (
                (own, group == device),
                (beside, group == device ^ 1),
                (across, (group != device) & (group != device ^ 1)),
            ):

                @pl.when((place >= 0) & held)
                def _():
                    into[...] = source[pl.ds(start, width), :]

        for p in range(aux):
            row = jnp.concatenate([tensor[p, m, j] for j in range(slots)], axis=1)
            half = jnp.dot(row, chosen[...], preferred_element_type=jnp.float32)
            half = half.astype(jnp.bfloat16)
            whole[m, :, p * occupied : (p + 1) * occupied] = half
            unit, column = divmod(p * occupied, columns)
            for k in range(width // rows):
                parts[2 * k + unit][m, :, column : column + occupied] = half[k * rows : (k + 1) * rows]


def half_forms(pattern, own, beside, across, tensor):
    aux, blocks, slots, width, _ = tensor.shape
    occupied = own.shape[1]
    part = jax.ShapeDtypeStruct((blocks, width // CHUNKS, aux * occupied // 2), jnp.bfloat16)
    out = [jax.ShapeDtypeStruct((blocks, width, aux * occupied), jnp.bfloat16)] + [part] * (2 * CHUNKS)
    return pl.pallas_call(
        half_kernel,
        out_shape=out,
        in_specs=[SMEM] + [VMEM] * 4,
        out_specs=[VMEM] * len(out),
        scratch_shapes=[pltpu.VMEM((slots * width, occupied), jnp.bfloat16)],
        compiler_params=params(24),
    )(pattern, own, beside, across, tensor)


def encode(tiles, coded, scales):
    rows = tiles[0].shape[0]
    scales[...] = jnp.zeros_like(scales)
    for t, tile in enumerate(tiles):
        most = jnp.max(jnp.abs(tile), axis=0, keepdims=True)
        power = jnp.ceil(jnp.log2(jnp.maximum(most, 2.0**-90)))
        scales[t : t + 1, :] = power
        whole = jnp.round(tile * jnp.exp2(14.0 - power))
        coded[t * rows : (t + 1) * rows, :] = whole.astype(jnp.int32).astype(jnp.int16)
    end = len(tiles) * rows
    coded[end : end + SCALE_ROWS, :] = scales[...].astype(jnp.int32).astype(jnp.int16)


def decode(coded, rows, count):
    end = count * rows
    scales = coded[end : end + SCALE_ROWS, :].astype(jnp.int32).astype(jnp.float32)
    scales = jnp.exp2(scales - 14.0)
    for t in range(count):
        value = coded[t * rows : (t + 1) * rows, :].astype(jnp.int32).astype(jnp.float32)
        yield value * scales[t : t + 1, :]


def tile_kernel(relays, chunk, pattern, whole, beside, first, second, third, kept, sent, partner, scales):
    blocks, width, depth = whole.shape
    rows = first.shape[1]
    slots = partner.shape[0] // rows
    device, layer = lax.axis_index("bas"), lax.axis_index("aux")
    at = chunk * rows
    relayed = device < 0
    for target in relays:
        relayed = relayed | (device == target)
    tiles = []
    for m in range(blocks):
        for j in range(slots):
            place = pattern[device * blocks + m, j]
            group, block = place // blocks, jnp.maximum(place, 0) % blocks
            into = partner.at[pl.ds(j * rows, rows)]
            across = (place >= 0) & (group != device) & (group != device ^ 1)

            @pl.when(place < 0)
            def _():
                into[...] = jnp.zeros((rows, depth), jnp.bfloat16)

            @pl.when((place >= 0) & (group == device))
            def _():
                into[...] = whole[block, at : at + rows, :]

            @pl.when((place >= 0) & (group == device ^ 1))
            def _():
                into[...] = beside[block, at : at + rows, :]

            @pl.when(across)
            def _():
                into[:, : depth // 2] = first[block]

            if relays:

                @pl.when(across & relayed)
                def _():
                    into[:, depth // 2 :] = third[block]

            @pl.when(across & jnp.logical_not(relayed))
            def _():
                into[:, depth // 2 :] = second[block]

        product = lax.dot_general(
            partner[...], whole[m], (((1,), (1,)), ((), ())), preferred_element_type=jnp.float32
        )
        tiles += [product[j * rows : (j + 1) * rows] for j in range(slots)]
    half = len(tiles) // 2
    for parity in range(2):

        @pl.when(layer % 2 == parity)
        def _():
            mine, other = tiles[parity * half :][:half], tiles[(1 - parity) * half :][:half]
            for t in range(half):
                kept[t * rows : (t + 1) * rows, :] = mine[t]
            encode(other, sent, scales)


def chunk_tiles(relays, chunk, pattern, whole, beside, first, second, third):
    blocks, width, depth = whole.shape
    rows, slots = first.shape[1], pattern.shape[1]
    half = blocks * slots // 2
    return pl.pallas_call(
        functools.partial(tile_kernel, relays, chunk),
        out_shape=[
            jax.ShapeDtypeStruct((half * rows, width), jnp.float32),
            jax.ShapeDtypeStruct((half * rows + SCALE_ROWS, width), jnp.int16),
        ],
        in_specs=[SMEM] + [VMEM] * 5,
        out_specs=[VMEM] * 2,
        scratch_shapes=[
            pltpu.VMEM((slots * rows, depth), jnp.bfloat16),
            pltpu.VMEM((SCALE_ROWS, width), jnp.float32),
        ],
        compiler_params=params(24),
    )(pattern, whole, beside, first, second, third)


def add_kernel(count, mine, other, coded, scales):
    rows = (coded.shape[0] - SCALE_ROWS) // count
    if mine.dtype == jnp.float32:
        held = [mine[t * rows : (t + 1) * rows, :] for t in range(count)]
    else:
        held = decode(mine, rows, count)
    encode([a + b for a, b in zip(held, decode(other, rows, count))], coded, scales)


def add_coded(count, mine, other):
    return pl.pallas_call(
        functools.partial(add_kernel, count),
        out_shape=jax.ShapeDtypeStruct(other.shape, other.dtype),
        in_specs=[VMEM] * 2,
        out_specs=VMEM,
        scratch_shapes=[pltpu.VMEM((SCALE_ROWS, other.shape[1]), jnp.float32)],
        compiler_params=params(8),
    )(mine, other)


def final_kernel(*refs):
    coded, out, turned = refs[:-2], refs[-2], refs[-1]
    blocks, slots, width, _ = out.shape
    half = blocks * slots // 2
    chunks = len(coded) // 2
    rows = width // chunks
    layer = lax.axis_index("aux")
    for parity in range(2):

        @pl.when(layer % 2 == parity)
        def _():
            for mine in range(2):
                base = (parity if mine == 0 else 1 - parity) * half
                for k in range(chunks):
                    for t, tile in enumerate(decode(coded[2 * k + mine], rows, half)):
                        turned[base + t, k * rows : (k + 1) * rows, :] = tile

    for t in range(2 * half):
        out[t // slots, t % slots] = turned[t].T


def final_tiles(shape, coded):
    blocks, slots, width, _ = shape
    return pl.pallas_call(
        final_kernel,
        out_shape=jax.ShapeDtypeStruct(shape, jnp.float32),
        in_specs=[VMEM] * len(coded),
        out_specs=VMEM,
        scratch_shapes=[pltpu.VMEM((blocks * slots, width, width), jnp.float32)],
        compiler_params=params(8),
    )(*coded)


def flipped(size, mask):
    return [(i, i ^ mask) for i in range(size)]


def body(coefficients, tensor, pattern):
    devices, layers = lax.axis_size("bas"), lax.axis_size("aux")
    _, blocks, slots, width, _ = tensor.shape
    chip = flipped(devices, 1)
    across = [pair for i in range(1, devices - 1, 2) for pair in ((i, i + 1), (i + 1, i))]
    detours = ((3, 4, 7), (4, 3, 0)) if devices == 8 else ()
    second_way = [pair for pair in across if pair not in [d[:2] for d in detours]]
    second_way += [(source, via) for source, _, via in detours]
    last_way = [(via, target) for _, target, via in detours]
    relays = tuple(target for _, target, _ in detours)

    beside = lax.ppermute(coefficients, "bas", chip)
    beyond = lax.ppermute(coefficients, "bas", across)
    whole, *parts = half_forms(pattern, coefficients, beside, beyond, tensor)
    arrived = []
    for k in range(CHUNKS):
        second = lax.ppermute(parts[2 * k + 1], "bas", second_way)
        first = lax.ppermute(parts[2 * k], "bas", across)
        third = lax.ppermute(second, "bas", last_way) if detours else second
        arrived.append((first, second, third))
    partner = lax.ppermute(whole, "bas", chip)
    half = blocks * slots // 2
    coded = []
    for k in range(CHUNKS):
        kept, sent = chunk_tiles(relays, k, pattern, whole, partner, *arrived[k])
        mine = add_coded(half, kept, lax.ppermute(sent, "aux", flipped(layers, 1)))
        mask = 2
        while mask < layers:
            mine = add_coded(half, mine, lax.ppermute(mine, "aux", flipped(layers, mask)))
            mask *= 2
        coded += [mine, lax.ppermute(mine, "aux", flipped(layers, 1))]
    return final_tiles((blocks, slots, width, width), coded)


def solution(mesh):
    return jax.shard_map(
        body,
        mesh=mesh,
        in_specs=(P("bas", None), P("aux", "bas", None, None, None), P()),
        out_specs=P("bas", None, None, None),
        check_vma=False,
    )
```

time: 168 us -> 79.2 us (0.47)
  waiting for transfers between devices: 95.6 us -> 34.6 us
  matrix products: 22.8 us -> 0 us
  starting transfers between devices: 12.7 us -> 28.8 us
  between operations: 13.5 us -> 0.14 us
  local copies, waits for them, and re-layouts: 16.2 us -> 3.6 us
  Pallas kernels: 0 us -> 11.7 us
  other arithmetic: 6.84 us -> 0 us
    psum x1 -> x0, waiting for transfers between devices: 88.2 us -> none  [body(): return lax.psum(tile_sums, 'aux')]
    ppermute x4 -> x15, waiting for transfers between devices: 7.34 us -> 34.6 us  [the longest x2 12.2 us: body(): third = lax.ppermute(second, 'bas', last_way) if detours else second]
    dot_general x4 -> x0, matrix products: 22.8 us -> none  [the longest x1 10.2 us: pick_rows(): jnp.einsum('mjr,prci->pmjci', picker, source, preferred_element_type=jnp....]
    ppermute x4 -> x15, starting transfers between devices: 12.7 us -> 28.8 us  [the longest x1 9.31 us: body(): partner = lax.ppermute(whole, 'bas', chip)]
    pallas_call x0 -> x8, Pallas kernels: none -> 11.7 us  [the longest x2 7.27 us: chunk_tiles(): pl.pallas_call(functools.partial(tile_kernel, relays, chunk), out_shape=[...]
    concatenate x1 -> x0, local copies, waits for them, and re-layouts: 11.5 us -> none  [with_halo(): value = jnp.concatenate([before, value, after], axis=dim)]
    concatenate x2 -> x0, other arithmetic: 6.08 us -> none  [with_halo(): value = jnp.concatenate([before, value, after], axis=dim)]
    unnamed x4 -> x5, local copies, waits for them, and re-layouts: 0.01 us -> 3.6 us
  transfers between devices with their start and end apart: 5 -> 15, of which waited for: 4 -> 8; matrix products, arithmetic and copies ran while one was open for 1% -> 1% of each run, Pallas kernels for 0% -> 10%
where the time goes in v1:
time: 79.2 us; the launch traced here: 78.9 us
  waiting for transfers between devices  34.6 us (44%)
  starting transfers between devices  28.8 us (36%)
  Pallas kernels  11.7 us (15%)
  local copies, waits for them, and re-layouts  3.6 us (5%)
    ppermute x2, waiting for transfers between devices, body(): third = lax.ppermute(second, 'bas', last_way) if detours else second  12.2 us
    ppermute x2, waiting for transfers between devices, body(): second = lax.ppermute(parts[2 * k + 1], 'bas', second_way)  10.5 us
    ppermute x1, starting transfers between devices, body(): partner = lax.ppermute(whole, 'bas', chip)  9.31 us
    pallas_call x2, Pallas kernels, chunk_tiles(): pl.pallas_call(functools.partial(tile_kernel, relays, chunk), out_shape=[...  7.27 us
    ppermute x2, waiting for transfers between devices, body(): lax.ppermute(mine, 'aux', flipped(layers, mask))  6.68 us
    ppermute x2, starting transfers between devices, body(): lax.ppermute(mine, 'aux', flipped(layers, mask))  5.66 us
    ppermute x2, waiting for transfers between devices, body(): coded += [mine, lax.ppermute(mine, 'aux', flipped(layers, 1))]  5.15 us
    ppermute x2, starting transfers between devices, body(): third = lax.ppermute(second, 'bas', last_way) if detours else second  4.27 us
  transfers between devices with their start and end apart: 15, of which 8 were waited for; matrix products, arithmetic and copies ran while one was open for 1% of the time, Pallas kernels for 10%

profile of v1, /device:TPU:0, one launch (start us, length us, event | category | flops | bytes accessed | tf_op | source)
XLA Modules:
  0.0 78.9 jit_solution(15383664242425744252)
XLA Ops:
  1.1 0.8 copy.5.pattern
  1.9 1.9 %copy-done = bf16[8,4,3,128,128]{4,3,2,1,0:T(8,128)(2,1)S(1)} copy-done((bf16[8,4,3,128,128]{4,3,2,1,0:T(8,128)(2,1)S(1)}, bf16[8,4,3,128,128]{4,3,2,1,0:T(8,128)(2,1)}, u32[]{:S(2)}) %copy-start) | copy-done | bytes 3145752
  3.8 0.9 %copy-done.1 = bf16[512,256]{1,0:T(8,128)(2,1)S(1)} copy-done((bf16[512,256]{1,0:T(8,128)(2,1)S(1)}, bf16[512,256]{1,0:T(8,128)(2,1)}, u32[]{:S(2)}) %copy-start.1) | copy-done | bytes 262168
  4.7 2.9 %shard_map.37 = (bf16[4,128,2048]{2,1,0:T(8,128)(2,1)S(1)}, bf16[4,64,1024]{2,1,0:T(8,128)(2,1)S(1)}, bf16[4,64,1024]{2,1,0:T(8,128)(2,1)S(1)}, bf16[4,64,1024]{2,1,0:T(8,128)(2,1)S(1)}, bf16[4,64,1024]{2,1,0:T(8,128)(2,1)S(1)}) custom-call(s32[32,3]{1,0:T(8,128)S(1)} %copy.5.pattern, bf16[512,256]{1,0:T(8,128)(2,1)S(1)} %copy-done.1, ...), custom_call_target="tpu_custom_call" | custom-call | tf_op jit(solution)/shard_map/pallas_call | solution.py:61
  7.6 9.3 %collective-permute-start.2 = (bf16[4,128,2048]{2,1,0:T(8,128)(2,1)S(1)}, bf16[4,128,2048]{2,1,0:T(8,128)(2,1)S(1)}, u32[]{:S(2)}, u32[]{:S(2)}) collective-permute-start(bf16[4,128,2048]{2,1,0:T(8,128)(2,1)S(1)} %get-tuple-element.14.whole), channel_id=1, source_target_pairs={{0,1},{1,0},{2,3},{3,2},{4,5},{5,4},{6,7},{7,6},{8,9},{9,8},{10,11... | collective-permute-start | bytes 6291464 | tf_op jit(solution)/shard_map/ppermute | solution.py:248
  16.9 1.3 %collective-permute-start.4 = (bf16[4,64,1024]{2,1,0:T(8,128)(2,1)S(1)}, bf16[4,64,1024]{2,1,0:T(8,128)(2,1)S(1)}, u32[]{:S(2)}, u32[]{:S(2)}) collective-permute-start(bf16[4,64,1024]{2,1,0:T(8,128)(2,1)S(1)} %get-tuple-element.16), channel_id=1, source_target_pairs={{1,2},{2,1},{5,6},{6,5},{3,7},{4,0},{9,10},{10,9},{13,14},{14,13},... | collective-permute-start | bytes 1572872 | tf_op jit(solution)/shard_map/ppermute | solution.py:244
  18.2 1.3 %collective-permute-start.10 = (bf16[4,64,1024]{2,1,0:T(8,128)(2,1)S(1)}, bf16[4,64,1024]{2,1,0:T(8,128)(2,1)S(1)}, u32[]{:S(2)}, u32[]{:S(2)}) collective-permute-start(bf16[4,64,1024]{2,1,0:T(8,128)(2,1)S(1)} %get-tuple-element.20), channel_id=1, source_target_pairs={{1,2},{2,1},{5,6},{6,5},{3,7},{4,0},{9,10},{10,9},{13,14},{14,13},... | collective-permute-start | bytes 1572872 | tf_op jit(solution)/shard_map/ppermute | solution.py:244
  20.2 7.8 %collective-permute-done.4.second = bf16[4,64,1024]{2,1,0:T(8,128)(2,1)S(1)} collective-permute-done((bf16[4,64,1024]{2,1,0:T(8,128)(2,1)S(1)}, bf16[4,64,1024]{2,1,0:T(8,128)(2,1)S(1)}, u32[]{:S(2)}, u32[]{:S(2)}) %collective-permute-start.4) | collective-permute-done | bytes 524320 | tf_op jit(solution)/shard_map/ppermute | solution.py:244
  28.0 2.1 %collective-permute-start.5 = (bf16[4,64,1024]{2,1,0:T(8,128)(2,1)S(1)}, bf16[4,64,1024]{2,1,0:T(8,128)(2,1)S(1)}, u32[]{:S(2)}, u32[]{:S(2)}) collective-permute-start(bf16[4,64,1024]{2,1,0:T(8,128)(2,1)S(1)} %collective-permute-done.4.second), channel_id=1, source_target_pairs={{7,4},{0,3},{15,12},{8,11},{23,20},{16,19},{31,28},{24,27}} | collective-permute-start | bytes 1572872 | tf_op jit(solution)/shard_map/ppermute | solution.py:246
  30.8 2.8 %collective-permute-done.10.second = bf16[4,64,1024]{2,1,0:T(8,128)(2,1)S(1)} collective-permute-done((bf16[4,64,1024]{2,1,0:T(8,128)(2,1)S(1)}, bf16[4,64,1024]{2,1,0:T(8,128)(2,1)S(1)}, u32[]{:S(2)}, u32[]{:S(2)}) %collective-permute-start.10) | collective-permute-done | bytes 524320 | tf_op jit(solution)/shard_map/ppermute | solution.py:244
  33.6 2.1 %collective-permute-start.11 = (bf16[4,64,1024]{2,1,0:T(8,128)(2,1)S(1)}, bf16[4,64,1024]{2,1,0:T(8,128)(2,1)S(1)}, u32[]{:S(2)}, u32[]{:S(2)}) collective-permute-start(bf16[4,64,1024]{2,1,0:T(8,128)(2,1)S(1)} %collective-permute-done.10.second), channel_id=1, source_target_pairs={{7,4},{0,3},{15,12},{8,11},{23,20},{16,19},{31,28},{24,27}} | collective-permute-start | bytes 1572872 | tf_op jit(solution)/shard_map/ppermute | solution.py:246
  35.8 6.7 %collective-permute-done.5.third = bf16[4,64,1024]{2,1,0:T(8,128)(2,1)S(1)} collective-permute-done((bf16[4,64,1024]{2,1,0:T(8,128)(2,1)S(1)}, bf16[4,64,1024]{2,1,0:T(8,128)(2,1)S(1)}, u32[]{:S(2)}, u32[]{:S(2)}) %collective-permute-start.5) | collective-permute-done | bytes 524320 | tf_op jit(solution)/shard_map/ppermute | solution.py:246
  42.5 3.6 %shard_map.38 = (f32[384,128]{1,0:T(8,128)S(1)}, s16[400,128]{1,0:T(8,128)(2,1)S(1)}) custom-call(s32[32,3]{1,0:T(8,128)S(1)} %copy.5.pattern, bf16[4,128,2048]{2,1,0:T(8,128)(2,1)S(1)} %get-tuple-element.14.whole, bf16[4,128,2048]{2,1,0:T(8,128)(2,1)S(1)} %collective-permute-done.2.beside, bf16[4,64,1024]{2,1,0:T(8,128)(2,1)S(1)} %collective-permute-done.3.first, ...), custom_call_target="tpu_custom_call" | custom-call | tf_op jit(solution)/shard_map/pallas_call | solution.py:155
  46.1 2.1 %collective-permute-start.6 = (s16[400,128]{1,0:T(8,128)(2,1)S(1)}, s16[400,128]{1,0:T(8,128)(2,1)S(1)}, u32[]{:S(2)}, u32[]{:S(2)}) collective-permute-start(s16[400,128]{1,0:T(8,128)(2,1)S(1)} %get-tuple-element.18), channel_id=1, source_target_pairs={{0,8},{8,0},{16,24},{24,16},{1,9},{9,1},{17,25},{25,17},{2,10},{10... | collective-permute-start | bytes 307208 | tf_op jit(solution)/shard_map/ppermute | solution.py:253
  48.2 5.5 %collective-permute-done.11.third = bf16[4,64,1024]{2,1,0:T(8,128)(2,1)S(1)} collective-permute-done((bf16[4,64,1024]{2,1,0:T(8,128)(2,1)S(1)}, bf16[4,64,1024]{2,1,0:T(8,128)(2,1)S(1)}, u32[]{:S(2)}, u32[]{:S(2)}) %collective-permute-start.11) | collective-permute-done | bytes 524320 | tf_op jit(solution)/shard_map/ppermute | solution.py:246
  53.7 3.6 %shard_map.41 = (f32[384,128]{1,0:T(8,128)S(1)}, s16[400,128]{1,0:T(8,128)(2,1)S(1)}) custom-call(s32[32,3]{1,0:T(8,128)S(1)} %copy.5.pattern, bf16[4,128,2048]{2,1,0:T(8,128)(2,1)S(1)} %get-tuple-element.14.whole, bf16[4,128,2048]{2,1,0:T(8,128)(2,1)S(1)} %collective-permute-done.2.beside, bf16[4,64,1024]{2,1,0:T(8,128)(2,1)S(1)} %collective-permute-done.9.first, ...), custom_call_target="tpu_custom_call" | custom-call | tf_op jit(solution)/shard_map/pallas_call | solution.py:155
  57.3 2.1 %collective-permute-start.12 = (s16[400,128]{1,0:T(8,128)(2,1)S(1)}, s16[400,128]{1,0:T(8,128)(2,1)S(1)}, u32[]{:S(2)}, u32[]{:S(2)}) collective-permute-start(s16[400,128]{1,0:T(8,128)(2,1)S(1)} %get-tuple-element.22), channel_id=1, source_target_pairs={{0,8},{8,0},{16,24},{24,16},{1,9},{9,1},{17,25},{25,17},{2,10},{10... | collective-permute-start | bytes 307208 | tf_op jit(solution)/shard_map/ppermute | solution.py:253
  59.5 2.7 %collective-permute-start.7 = (s16[400,128]{1,0:T(8,128)(2,1)S(1)}, s16[400,128]{1,0:T(8,128)(2,1)S(1)}, u32[]{:S(2)}, u32[]{:S(2)}) collective-permute-start(s16[400,128]{1,0:T(8,128)(2,1)S(1)} %shard_map.39.mine), channel_id=1, source_target_pairs={{0,16},{8,24},{16,0},{24,8},{1,17},{9,25},{17,1},{25,9},{2,18},{10... | collective-permute-start | bytes 307208 | tf_op jit(solution)/shard_map/ppermute | solution.py:256
  62.2 3.0 %collective-permute-start.13 = (s16[400,128]{1,0:T(8,128)(2,1)S(1)}, s16[400,128]{1,0:T(8,128)(2,1)S(1)}, u32[]{:S(2)}, u32[]{:S(2)}) collective-permute-start(s16[400,128]{1,0:T(8,128)(2,1)S(1)} %shard_map.42.mine), channel_id=1, source_target_pairs={{0,16},{8,24},{16,0},{24,8},{1,17},{9,25},{17,1},{25,9},{2,18},{10... | collective-permute-start | bytes 307208 | tf_op jit(solution)/shard_map/ppermute | solution.py:256
  65.2 1.3 %collective-permute-done.7.other = s16[400,128]{1,0:T(8,128)(2,1)S(1)} collective-permute-done((s16[400,128]{1,0:T(8,128)(2,1)S(1)}, s16[400,128]{1,0:T(8,128)(2,1)S(1)}, u32[]{:S(2)}, u32[]{:S(2)}) %collective-permute-start.7) | collective-permute-done | bytes 102432 | tf_op jit(solution)/shard_map/ppermute | solution.py:256
  67.0 5.4 %collective-permute-done.13.other = s16[400,128]{1,0:T(8,128)(2,1)S(1)} collective-permute-done((s16[400,128]{1,0:T(8,128)(2,1)S(1)}, s16[400,128]{1,0:T(8,128)(2,1)S(1)}, u32[]{:S(2)}, u32[]{:S(2)}) %collective-permute-start.13) | collective-permute-done | bytes 102432 | tf_op jit(solution)/shard_map/ppermute | solution.py:256
  72.5 1.0 %collective-permute-done.8.refs_1_ = s16[400,128]{1,0:T(8,128)(2,1)S(1)} collective-permute-done((s16[400,128]{1,0:T(8,128)(2,1)S(1)}, s16[400,128]{1,0:T(8,128)(2,1)S(1)}, u32[]{:S(2)}, u32[]{:S(2)}) %collective-permute-start.8) | collective-permute-done | bytes 102432 | tf_op jit(solution)/shard_map/ppermute | solution.py:258
  73.5 4.2 %collective-permute-done.14.refs_3_ = s16[400,128]{1,0:T(8,128)(2,1)S(1)} collective-permute-done((s16[400,128]{1,0:T(8,128)(2,1)S(1)}, s16[400,128]{1,0:T(8,128)(2,1)S(1)}, u32[]{:S(2)}, u32[]{:S(2)}) %collective-permute-start.14) | collective-permute-done | bytes 102432 | tf_op jit(solution)/shard_map/ppermute | solution.py:258
  77.7 1.2 %shard_map.44 = f32[4,3,128,128]{3,2,1,0:T(8,128)} custom-call(s16[400,128]{1,0:T(8,128)(2,1)S(1)} %shard_map.40.refs_0_, s16[400,128]{1,0:T(8,128)(2,1)S(1)} %collective-permute-done.8.refs_1_, s16[400,128]{1,0:T(8,128)(2,1)S(1)} %shard_map.43.refs_2_, s16[400,128]{1,0:T(8,128)(2,1)S(1)} %collective-permute-done.14.refs_3_), custom_call_target="tpu_custom_call" | custom-call | tf_op jit(solution)/shard_map/pallas_call | solution.py:214
  (19 shorter events, 3.3 us)
Async XLA Ops:
  0.0 1.9 %collective-permute-start = (bf16[512,256]{1,0:T(8,128)(2,1)}, bf16[512,256]{1,0:T(8,128)(2,1)S(1)}, u32[]{:S(2)}, u32[]{:S(2)}) collective-permute-start(bf16[512,256]{1,0:T(8,128)(2,1)} %own.1), channel_id=1, source_target_pairs={{0,1},{1,0},{2,3},{3,2},{4,5},{5,4},{6,7},{7,6},{8,9},{9,8},{10,11... | collective-permute-start | bytes 786440 | tf_op jit(solution)/shard_map/ppermute | solution.py:239
  0.5 1.4 %collective-permute-start.1 = (bf16[512,256]{1,0:T(8,128)(2,1)}, bf16[512,256]{1,0:T(8,128)(2,1)S(1)}, u32[]{:S(2)}, u32[]{:S(2)}) collective-permute-start(bf16[512,256]{1,0:T(8,128)(2,1)} %own.1), channel_id=1, source_target_pairs={{1,2},{2,1},{3,4},{4,3},{5,6},{6,5},{9,10},{10,9},{11,12},{12,11},... | collective-permute-start | bytes 786440 | tf_op jit(solution)/shard_map/ppermute | solution.py:240
  1.9 1.9 %copy-start = (bf16[8,4,3,128,128]{4,3,2,1,0:T(8,128)(2,1)S(1)}, bf16[8,4,3,128,128]{4,3,2,1,0:T(8,128)(2,1)}, u32[]{:S(2)}) copy-start(bf16[8,4,3,128,128]{4,3,2,1,0:T(8,128)(2,1)} %tensor.1) | copy-start | bytes 9437188
  3.8 0.9 %copy-start.1 = (bf16[512,256]{1,0:T(8,128)(2,1)S(1)}, bf16[512,256]{1,0:T(8,128)(2,1)}, u32[]{:S(2)}) copy-start(bf16[512,256]{1,0:T(8,128)(2,1)} %own.1) | copy-start | bytes 786436
  7.6 34.9 %collective-permute-start.2 = (bf16[4,128,2048]{2,1,0:T(8,128)(2,1)S(1)}, bf16[4,128,2048]{2,1,0:T(8,128)(2,1)S(1)}, u32[]{:S(2)}, u32[]{:S(2)}) collective-permute-start(bf16[4,128,2048]{2,1,0:T(8,128)(2,1)S(1)} %get-tuple-element.14.whole), channel_id=1, source_target_pairs={{0,1},{1,0},{2,3},{3,2},{4,5},{5,4},{6,7},{7,6},{8,9},{9,8},{10,11... | collective-permute-start | bytes 6291464 | tf_op jit(solution)/shard_map/ppermute | solution.py:248
  16.9 11.1 %collective-permute-start.4 = (bf16[4,64,1024]{2,1,0:T(8,128)(2,1)S(1)}, bf16[4,64,1024]{2,1,0:T(8,128)(2,1)S(1)}, u32[]{:S(2)}, u32[]{:S(2)}) collective-permute-start(bf16[4,64,1024]{2,1,0:T(8,128)(2,1)S(1)} %get-tuple-element.16), channel_id=1, source_target_pairs={{1,2},{2,1},{5,6},{6,5},{3,7},{4,0},{9,10},{10,9},{13,14},{14,13},... | collective-permute-start | bytes 1572872 | tf_op jit(solution)/shard_map/ppermute | solution.py:244
  18.2 15.4 %collective-permute-start.10 = (bf16[4,64,1024]{2,1,0:T(8,128)(2,1)S(1)}, bf16[4,64,1024]{2,1,0:T(8,128)(2,1)S(1)}, u32[]{:S(2)}, u32[]{:S(2)}) collective-permute-start(bf16[4,64,1024]{2,1,0:T(8,128)(2,1)S(1)} %get-tuple-element.20), channel_id=1, source_target_pairs={{1,2},{2,1},{5,6},{6,5},{3,7},{4,0},{9,10},{10,9},{13,14},{14,13},... | collective-permute-start | bytes 1572872 | tf_op jit(solution)/shard_map/ppermute | solution.py:244
  19.5 16.2 %collective-permute-start.3 = (bf16[4,64,1024]{2,1,0:T(8,128)(2,1)S(1)}, bf16[4,64,1024]{2,1,0:T(8,128)(2,1)S(1)}, u32[]{:S(2)}, u32[]{:S(2)}) collective-permute-start(bf16[4,64,1024]{2,1,0:T(8,128)(2,1)S(1)} %get-tuple-element.15), channel_id=1, source_target_pairs={{1,2},{2,1},{3,4},{4,3},{5,6},{6,5},{9,10},{10,9},{11,12},{12,11},... | collective-permute-start | bytes 1572872 | tf_op jit(solution)/shard_map/ppermute | solution.py:245
  28.0 14.5 %collective-permute-start.5 = (bf16[4,64,1024]{2,1,0:T(8,128)(2,1)S(1)}, bf16[4,64,1024]{2,1,0:T(8,128)(2,1)S(1)}, u32[]{:S(2)}, u32[]{:S(2)}) collective-permute-start(bf16[4,64,1024]{2,1,0:T(8,128)(2,1)S(1)} %collective-permute-done.4.second), channel_id=1, source_target_pairs={{7,4},{0,3},{15,12},{8,11},{23,20},{16,19},{31,28},{24,27}} | collective-permute-start | bytes 1572872 | tf_op jit(solution)/shard_map/ppermute | solution.py:246
  30.1 18.0 %collective-permute-start.9 = (bf16[4,64,1024]{2,1,0:T(8,128)(2,1)S(1)}, bf16[4,64,1024]{2,1,0:T(8,128)(2,1)S(1)}, u32[]{:S(2)}, u32[]{:S(2)}) collective-permute-start(bf16[4,64,1024]{2,1,0:T(8,128)(2,1)S(1)} %get-tuple-element.19), channel_id=1, source_target_pairs={{1,2},{2,1},{3,4},{4,3},{5,6},{6,5},{9,10},{10,9},{11,12},{12,11},... | collective-permute-start | bytes 1572872 | tf_op jit(solution)/shard_map/ppermute | solution.py:245
  33.6 20.1 %collective-permute-start.11 = (bf16[4,64,1024]{2,1,0:T(8,128)(2,1)S(1)}, bf16[4,64,1024]{2,1,0:T(8,128)(2,1)S(1)}, u32[]{:S(2)}, u32[]{:S(2)}) collective-permute-start(bf16[4,64,1024]{2,1,0:T(8,128)(2,1)S(1)} %collective-permute-done.10.second), channel_id=1, source_target_pairs={{7,4},{0,3},{15,12},{8,11},{23,20},{16,19},{31,28},{24,27}} | collective-permute-start | bytes 1572872 | tf_op jit(solution)/shard_map/ppermute | solution.py:246
  46.1 13.3 %collective-permute-start.6 = (s16[400,128]{1,0:T(8,128)(2,1)S(1)}, s16[400,128]{1,0:T(8,128)(2,1)S(1)}, u32[]{:S(2)}, u32[]{:S(2)}) collective-permute-start(s16[400,128]{1,0:T(8,128)(2,1)S(1)} %get-tuple-element.18), channel_id=1, source_target_pairs={{0,8},{8,0},{16,24},{24,16},{1,9},{9,1},{17,25},{25,17},{2,10},{10... | collective-permute-start | bytes 307208 | tf_op jit(solution)/shard_map/ppermute | solution.py:253
  57.3 4.8 %collective-permute-start.12 = (s16[400,128]{1,0:T(8,128)(2,1)S(1)}, s16[400,128]{1,0:T(8,128)(2,1)S(1)}, u32[]{:S(2)}, u32[]{:S(2)}) collective-permute-start(s16[400,128]{1,0:T(8,128)(2,1)S(1)} %get-tuple-element.22), channel_id=1, source_target_pairs={{0,8},{8,0},{16,24},{24,16},{1,9},{9,1},{17,25},{25,17},{2,10},{10... | collective-permute-start | bytes 307208 | tf_op jit(solution)/shard_map/ppermute | solution.py:253
  59.5 7.1 %collective-permute-start.7 = (s16[400,128]{1,0:T(8,128)(2,1)S(1)}, s16[400,128]{1,0:T(8,128)(2,1)S(1)}, u32[]{:S(2)}, u32[]{:S(2)}) collective-permute-start(s16[400,128]{1,0:T(8,128)(2,1)S(1)} %shard_map.39.mine), channel_id=1, source_target_pairs={{0,16},{8,24},{16,0},{24,8},{1,17},{9,25},{17,1},{25,9},{2,18},{10... | collective-permute-start | bytes 307208 | tf_op jit(solution)/shard_map/ppermute | solution.py:256
  62.2 10.1 %collective-permute-start.13 = (s16[400,128]{1,0:T(8,128)(2,1)S(1)}, s16[400,128]{1,0:T(8,128)(2,1)S(1)}, u32[]{:S(2)}, u32[]{:S(2)}) collective-permute-start(s16[400,128]{1,0:T(8,128)(2,1)S(1)} %shard_map.42.mine), channel_id=1, source_target_pairs={{0,16},{8,24},{16,0},{24,8},{1,17},{9,25},{17,1},{25,9},{2,18},{10... | collective-permute-start | bytes 307208 | tf_op jit(solution)/shard_map/ppermute | solution.py:256
  66.6 6.8 %collective-permute-start.8 = (s16[400,128]{1,0:T(8,128)(2,1)S(1)}, s16[400,128]{1,0:T(8,128)(2,1)S(1)}, u32[]{:S(2)}, u32[]{:S(2)}) collective-permute-start(s16[400,128]{1,0:T(8,128)(2,1)S(1)} %shard_map.40.refs_0_), channel_id=1, source_target_pairs={{0,8},{8,0},{16,24},{24,16},{1,9},{9,1},{17,25},{25,17},{2,10},{10... | collective-permute-start | bytes 307208 | tf_op jit(solution)/shard_map/ppermute | solution.py:258
  72.4 5.2 %collective-permute-start.14 = (s16[400,128]{1,0:T(8,128)(2,1)S(1)}, s16[400,128]{1,0:T(8,128)(2,1)S(1)}, u32[]{:S(2)}, u32[]{:S(2)}) collective-permute-start(s16[400,128]{1,0:T(8,128)(2,1)S(1)} %shard_map.43.refs_2_), channel_id=1, source_target_pairs={{0,8},{8,0},{16,24},{24,16},{1,9},{9,1},{17,25},{25,17},{2,10},{10... | collective-permute-start | bytes 307208 | tf_op jit(solution)/shard_map/ppermute | solution.py:258

commit v2 on v1

v2 whole, which is shorter than its diff:
```python
import functools

import jax
import jax.numpy as jnp
from jax import lax
from jax.experimental import pallas as pl
from jax.experimental.pallas import tpu as pltpu
from jax.sharding import PartitionSpec as P

CUTS = (0, 64, 128)
SCALE_ROWS = 16
FULL = 32752.0
VMEM = pl.BlockSpec(memory_space=pltpu.VMEM)
ANY = pl.BlockSpec(memory_space=pl.ANY)
SMEM = pl.BlockSpec(memory_space=pltpu.SMEM)


def params(mib):
    return pltpu.CompilerParams(vmem_limit_bytes=mib << 20)


def fetch_kernel(tensor, own, tensor_out, own_out, sems):
    copies = [
        pltpu.make_async_copy(own, own_out, sems.at[0]),
        pltpu.make_async_copy(tensor, tensor_out, sems.at[1]),
    ]
    for copy in copies:
        copy.start()
    for copy in copies:
        copy.wait()


def fetch(tensor, own):
    arrays = (tensor, own)
    return pl.pallas_call(
        fetch_kernel,
        out_shape=[jax.ShapeDtypeStruct(a.shape, a.dtype) for a in arrays],
        in_specs=[ANY] * 2,
        out_specs=[VMEM] * 2,
        scratch_shapes=[pltpu.SemaphoreType.DMA((2,))],
        compiler_params=params(8),
    )(*arrays)


def half_kernel(start, rows, earlier, pattern, own, beside, across, tensor, *rest):
    before, (out_0, out_1, *joined, chosen) = rest[:earlier], rest[earlier:]
    aux, blocks, slots, width, _ = tensor.shape
    occupied = own.shape[1]
    device = lax.axis_index("bas")
    for m in range(blocks):
        for j in range(slots):
            place = pattern[device * blocks + m, j]
            group, first = place // blocks, pl.multiple_of((place % blocks) * width, width)
            into = chosen.at[m, pl.ds(j * width, width)]

            @pl.when(place < 0)
            def _():
                into[...] = jnp.zeros((width, occupied), jnp.bfloat16)

            for source, held in (
                (own, group == device),
                (beside, group == device ^ 1),
                (across, (group != device) & (group != device ^ 1)),
            ):

                @pl.when((place >= 0) & held)
                def _():
                    into[...] = source[pl.ds(first, width), :]

        row = jnp.concatenate(
            [tensor[:, m, j, start : start + rows].reshape(aux * rows, width) for j in range(slots)], axis=1
        )
        half = jnp.dot(row, chosen[m], preferred_element_type=jnp.float32).astype(jnp.bfloat16)
        for p in range(aux):
            out, column = (out_0, p) if p < aux // 2 else (out_1, p - aux // 2)
            piece = half[p * rows : (p + 1) * rows]
            out[m, :, column * occupied : (column + 1) * occupied] = piece
            for whole in joined:
                whole[m, start : start + rows, p * occupied : (p + 1) * occupied] = piece
    for whole in joined:
        depth = aux * occupied // 2
        at = 0
        for one, other in zip(before[::2], before[1::2]):
            whole[:, at : at + one.shape[1], :depth] = one[...]
            whole[:, at : at + one.shape[1], depth:] = other[...]
            at += one.shape[1]


def half_forms(start, rows, pattern, own, beside, across, tensor, before=()):
    aux, blocks, slots, width, _ = tensor.shape
    occupied = own.shape[1]
    out = [jax.ShapeDtypeStruct((blocks, rows, aux * occupied // 2), jnp.bfloat16)] * 2
    if start + rows == width:
        out += [jax.ShapeDtypeStruct((blocks, width, aux * occupied), jnp.bfloat16)]
    return pl.pallas_call(
        functools.partial(half_kernel, start, rows, len(before)),
        out_shape=out,
        in_specs=[SMEM] + [VMEM] * (4 + len(before)),
        out_specs=[VMEM] * len(out),
        scratch_shapes=[pltpu.VMEM((blocks, slots * width, occupied), jnp.bfloat16)],
        compiler_params=params(24),
    )(pattern, own, beside, across, tensor, *before)


def encode(tiles, coded, scales):
    rows = tiles[0].shape[0]
    scales[...] = jnp.zeros_like(scales)
    for t, tile in enumerate(tiles):
        most = jnp.max(jnp.abs(tile), axis=0, keepdims=True)
        power = jnp.ceil(jnp.log2(jnp.maximum(most, 2.0**-90)))
        scales[t : t + 1, :] = power
        whole = jnp.round(tile * (FULL * jnp.exp2(-power)))
        coded[t * rows : (t + 1) * rows, :] = whole.astype(jnp.int32).astype(jnp.int16)
    end = len(tiles) * rows
    coded[end : end + SCALE_ROWS, :] = scales[...].astype(jnp.int32).astype(jnp.int16)


def decode(coded, rows, count):
    end = count * rows
    scales = coded[end : end + SCALE_ROWS, :].astype(jnp.int32).astype(jnp.float32)
    scales = jnp.exp2(scales) * (1.0 / FULL)
    for t in range(count):
        value = coded[t * rows : (t + 1) * rows, :].astype(jnp.int32).astype(jnp.float32)
        yield value * scales[t : t + 1, :]


def times(rows, whole):
    blocks, width, depth = whole.shape
    return lax.dot_general(
        rows, whole.reshape(blocks * width, depth), (((1,), (1,)), ((), ())), preferred_element_type=jnp.float32
    )


def near_kernel(cuts, whole, beside, *products):
    blocks, width, depth = whole.shape
    for k, product in enumerate(products):
        rows = cuts[k + 1] - cuts[k]
        for i, source in enumerate((whole, beside)):
            part = source[:, cuts[k] : cuts[k + 1], :].reshape(blocks * rows, depth)
            product[i * blocks * rows : (i + 1) * blocks * rows, :] = times(part, whole[...])


def near_products(cuts, whole, beside):
    blocks, width, _ = whole.shape
    return pl.pallas_call(
        functools.partial(near_kernel, cuts),
        out_shape=[
            jax.ShapeDtypeStruct((2 * blocks * (b - a), blocks * width), jnp.float32)
            for a, b in zip(cuts, cuts[1:])
        ],
        in_specs=[VMEM] * 2,
        out_specs=[VMEM] * (len(cuts) - 1),
        compiler_params=params(24),
    )(whole, beside)


def tile_kernel(relays, pattern, whole, near, first, second, third, kept, sent, far, scales):
    blocks, width, depth = whole.shape
    _, rows, cut = first.shape
    slots = pattern.shape[1]
    device, layer = lax.axis_index("bas"), lax.axis_index("aux")
    half = blocks * slots // 2
    far[...] = times(first[...].reshape(blocks * rows, cut), whole[:, :, :cut])

    def add(source):
        far[...] += times(source[...].reshape(blocks * rows, cut), whole[:, :, cut:])

    if relays:
        relayed = functools.reduce(jnp.logical_or, [device == target for target in relays])
        pl.when(relayed)(lambda: add(third))
        pl.when(jnp.logical_not(relayed))(lambda: add(second))
    else:
        add(second)

    def tile(t, parity):
        m = parity * (blocks // 2) + t // slots
        place = pattern[device * blocks + m, t % slots]
        group, block = place // blocks, jnp.maximum(place, 0) % blocks
        columns = pl.ds(pl.multiple_of(m * width, width), width)
        close = block + jnp.where(group == device, 0, blocks)
        inside = near[pl.ds(pl.multiple_of(close * rows, rows), rows), columns]
        outside = far[pl.ds(pl.multiple_of(block * rows, rows), rows), columns]
        value = jnp.where((group == device) | (group == device ^ 1), inside, outside)
        return jnp.where(place < 0, 0.0, value)

    for t in range(half):
        kept[t * rows : (t + 1) * rows, :] = tile(t, layer % 2)
    encode([tile(t, 1 - layer % 2) for t in range(half)], sent, scales)


def chunk_tiles(relays, pattern, whole, near, first, second, third):
    blocks, width, _ = whole.shape
    rows, slots = first.shape[1], pattern.shape[1]
    half = blocks * slots // 2
    return pl.pallas_call(
        functools.partial(tile_kernel, relays),
        out_shape=[
            jax.ShapeDtypeStruct((half * rows, width), jnp.float32),
            jax.ShapeDtypeStruct((half * rows + SCALE_ROWS, width), jnp.int16),
        ],
        in_specs=[SMEM] + [VMEM] * 5,
        out_specs=[VMEM] * 2,
        scratch_shapes=[
            pltpu.VMEM((blocks * rows, blocks * width), jnp.float32),
            pltpu.VMEM((SCALE_ROWS, width), jnp.float32),
        ],
        compiler_params=params(24),
    )(pattern, whole, near, first, second, third)


def add_kernel(count, mine, other, coded, scales):
    rows = (coded.shape[0] - SCALE_ROWS) // count
    if mine.dtype == jnp.float32:
        held = [mine[t * rows : (t + 1) * rows, :] for t in range(count)]
    else:
        held = decode(mine, rows, count)
    encode([a + b for a, b in zip(held, decode(other, rows, count))], coded, scales)


def add_coded(count, mine, other):
    return pl.pallas_call(
        functools.partial(add_kernel, count),
        out_shape=jax.ShapeDtypeStruct(other.shape, other.dtype),
        in_specs=[VMEM] * 2,
        out_specs=VMEM,
        scratch_shapes=[pltpu.VMEM((SCALE_ROWS, other.shape[1]), jnp.float32)],
        compiler_params=params(8),
    )(mine, other)


def final_kernel(*refs):
    coded, out, turned = refs[:-2], refs[-2], refs[-1]
    blocks, slots, width, _ = out.shape
    half = blocks * slots // 2
    layer = lax.axis_index("aux")
    for parity in range(2):

        @pl.when(layer % 2 == parity)
        def _():
            for mine in range(2):
                base = (parity if mine == 0 else 1 - parity) * half
                at = 0
                for part in coded[mine::2]:
                    rows = (part.shape[0] - SCALE_ROWS) // half
                    for t, tile in enumerate(decode(part, rows, half)):
                        turned[base + t, at : at + rows, :] = tile
                    at += rows

    for t in range(2 * half):
        out[t // slots, t % slots] = turned[t].T


def final_tiles(shape, coded):
    blocks, slots, width, _ = shape
    return pl.pallas_call(
        final_kernel,
        out_shape=jax.ShapeDtypeStruct(shape, jnp.float32),
        in_specs=[VMEM] * len(coded),
        out_specs=VMEM,
        scratch_shapes=[pltpu.VMEM((blocks * slots, width, width), jnp.float32)],
        compiler_params=params(8),
    )(*coded)


def flipped(size, mask):
    return [(i, i ^ mask) for i in range(size)]


def body(coefficients, tensor, pattern):
    devices, layers = lax.axis_size("bas"), lax.axis_size("aux")
    _, blocks, slots, width, _ = tensor.shape
    chip = flipped(devices, 1)
    across = [pair for i in range(1, devices - 1, 2) for pair in ((i, i + 1), (i + 1, i))]
    detours = ((3, 4, 7), (4, 3, 0)) if devices == 8 else ()
    second_way = [pair for pair in across if pair not in [d[:2] for d in detours]]
    second_way += [(source, via) for source, _, via in detours]
    last_way = [(via, target) for _, target, via in detours]
    relays = tuple(target for _, target, _ in detours)

    beyond = lax.ppermute(coefficients, "bas", across)
    beside = lax.ppermute(coefficients, "bas", chip)
    tensor, coefficients = fetch(tensor, coefficients)
    operands = (pattern, coefficients, beside, beyond, tensor)
    cuts = CUTS
    parts, arrived = [], []
    for a, b in zip(cuts, cuts[1:]):
        one, other, *joined = half_forms(a, b - a, *operands, before=parts if b == width else ())
        parts += [one, other]
        second = lax.ppermute(other, "bas", second_way)
        first = lax.ppermute(one, "bas", across)
        third = lax.ppermute(second, "bas", last_way) if detours else second
        arrived.append((first, second, third))
    (whole,) = joined
    near = near_products(cuts, whole, lax.ppermute(whole, "bas", chip))
    half = blocks * slots // 2
    coded = []
    for close, held in zip(near, arrived):
        kept, sent = chunk_tiles(relays, pattern, whole, close, *held)
        mine = add_coded(half, kept, lax.ppermute(sent, "aux", flipped(layers, 1)))
        mask = 2
        while mask < layers:
            mine = add_coded(half, mine, lax.ppermute(mine, "aux", flipped(layers, mask)))
            mask *= 2
        coded += [mine, lax.ppermute(mine, "aux", flipped(layers, 1))]
    return final_tiles((blocks, slots, width, width), coded)


def solution(mesh):
    return jax.shard_map(
        body,
        mesh=mesh,
        in_specs=(P("bas", None), P("aux", "bas", None, None, None), P()),
        out_specs=P("bas", None, None, None),
        check_vma=False,
    )
```

time: 79.2 us -> 77.4 us (0.977)
  starting transfers between devices: 28.8 us -> 25.7 us
  Pallas kernels: 11.7 us -> 13.6 us
    ppermute x5, starting transfers between devices: 13.3 us -> 10.1 us  [the longest x1 6.18 us: body(): near = near_products(cuts, whole, lax.ppermute(whole, 'bas', chip))]
    pallas_call x3 -> x6, Pallas kernels: 10.1 us -> 12 us  [the longest x2 5.54 us: half_forms(): pl.pallas_call(functools.partial(half_kernel, start, rows, len(before)),...]
  transfers between devices with their start and end apart: 15 -> 15, of which waited for: 8 -> 8; matrix products, arithmetic and copies ran while one was open for 1% -> 1% of each run, Pallas kernels for 10% -> 9%
where the time goes in v2:
time: 77.4 us; the launch traced here: 77.1 us
  waiting for transfers between devices  34 us (44%)
  starting transfers between devices  25.7 us (33%)
  Pallas kernels  13.6 us (18%)
  local copies, waits for them, and re-layouts  3.6 us (5%)
    ppermute x2, waiting for transfers between devices, body(): third = lax.ppermute(second, 'bas', last_way) if detours else second  11.6 us
    ppermute x2, waiting for transfers between devices, body(): second = lax.ppermute(other, 'bas', second_way)  10.5 us
    ppermute x2, waiting for transfers between devices, body(): lax.ppermute(mine, 'aux', flipped(layers, mask))  6.66 us
    ppermute x1, starting transfers between devices, body(): near = near_products(cuts, whole, lax.ppermute(whole, 'bas', chip))  6.18 us
    ppermute x2, starting transfers between devices, body(): lax.ppermute(mine, 'aux', flipped(layers, mask))  5.64 us
    pallas_call x2, Pallas kernels, half_forms(): pl.pallas_call(functools.partial(half_kernel, start, rows, len(before)),...  5.54 us
    ppermute x2, waiting for transfers between devices, body(): coded += [mine, lax.ppermute(mine, 'aux', flipped(layers, 1))]  5.2 us
    ppermute x2, starting transfers between devices, body(): third = lax.ppermute(second, 'bas', last_way) if detours else second  4.33 us
  transfers between devices with their start and end apart: 15, of which 8 were waited for; matrix products, arithmetic and copies ran while one was open for 1% of the time, Pallas kernels for 9%

profile of v2, /device:TPU:0, one launch (start us, length us, event | category | flops | bytes accessed | tf_op | source)
XLA Modules:
  0.0 77.1 jit_solution(7225778593374632976)
XLA Ops:
  1.9 1.9 %copy-done = bf16[8,4,3,128,128]{4,3,2,1,0:T(8,128)(2,1)S(1)} copy-done((bf16[8,4,3,128,128]{4,3,2,1,0:T(8,128)(2,1)S(1)}, bf16[8,4,3,128,128]{4,3,2,1,0:T(8,128)(2,1)}, u32[]{:S(2)}) %copy-start) | copy-done | bytes 3145752
  5.0 2.8 %shard_map.38 = (bf16[4,64,1024]{2,1,0:T(8,128)(2,1)S(1)}, bf16[4,64,1024]{2,1,0:T(8,128)(2,1)S(1)}) custom-call(s32[32,3]{1,0:T(8,128)S(1)} %copy.6.pattern, bf16[512,256]{1,0:T(8,128)(2,1)S(1)} %get-tuple-element.18.own, bf16[512,256]{1,0:T(8,128)(2,1)S(1)} %collective-permute-done.beside, bf16[512,256]{1,0:T(8,128)(2,1)S(1)} %collective-permute-done.1.across, ...), custom_call_target="tpu_custom_call" | custom-call | tf_op jit(solution)/shard_map/pallas_call | solution.py:95
  7.8 2.8 %shard_map.39 = (bf16[4,64,1024]{2,1,0:T(8,128)(2,1)S(1)}, bf16[4,64,1024]{2,1,0:T(8,128)(2,1)S(1)}, bf16[4,128,2048]{2,1,0:T(8,128)(2,1)S(1)}) custom-call(s32[32,3]{1,0:T(8,128)S(1)} %copy.6.pattern, bf16[512,256]{1,0:T(8,128)(2,1)S(1)} %get-tuple-element.18.own, bf16[512,256]{1,0:T(8,128)(2,1)S(1)} %collective-permute-done.beside, ...), custom_call_target="tpu_custom_call" | custom-call | tf_op jit(solution)/shard_map/pallas_call | solution.py:95
  10.6 6.2 %collective-permute-start.2 = (bf16[4,128,2048]{2,1,0:T(8,128)(2,1)S(1)}, bf16[4,128,2048]{2,1,0:T(8,128)(2,1)S(1)}, u32[]{:S(2)}, u32[]{:S(2)}) collective-permute-start(bf16[4,128,2048]{2,1,0:T(8,128)(2,1)S(1)} %get-tuple-element.22.whole), channel_id=1, source_target_pairs={{0,1},{1,0},{2,3},{3,2},{4,5},{5,4},{6,7},{7,6},{8,9},{9,8},{10,11... | collective-permute-start | bytes 6291464 | tf_op jit(solution)/shard_map/ppermute | solution.py:294
  16.7 1.3 %collective-permute-start.10 = (bf16[4,64,1024]{2,1,0:T(8,128)(2,1)S(1)}, bf16[4,64,1024]{2,1,0:T(8,128)(2,1)S(1)}, u32[]{:S(2)}, u32[]{:S(2)}) collective-permute-start(bf16[4,64,1024]{2,1,0:T(8,128)(2,1)S(1)} %get-tuple-element.28), channel_id=1, source_target_pairs={{1,2},{2,1},{5,6},{6,5},{3,7},{4,0},{9,10},{10,9},{13,14},{14,13},... | collective-permute-start | bytes 1572872 | tf_op jit(solution)/shard_map/ppermute | solution.py:289
  18.0 1.3 %collective-permute-start.4 = (bf16[4,64,1024]{2,1,0:T(8,128)(2,1)S(1)}, bf16[4,64,1024]{2,1,0:T(8,128)(2,1)S(1)}, u32[]{:S(2)}, u32[]{:S(2)}) collective-permute-start(bf16[4,64,1024]{2,1,0:T(8,128)(2,1)S(1)} %get-tuple-element.21.rest_1_), channel_id=1, source_target_pairs={{1,2},{2,1},{5,6},{6,5},{3,7},{4,0},{9,10},{10,9},{13,14},{14,13},... | collective-permute-start | bytes 1572872 | tf_op jit(solution)/shard_map/ppermute | solution.py:289
  20.0 7.8 %collective-permute-done.10.second = bf16[4,64,1024]{2,1,0:T(8,128)(2,1)S(1)} collective-permute-done((bf16[4,64,1024]{2,1,0:T(8,128)(2,1)S(1)}, bf16[4,64,1024]{2,1,0:T(8,128)(2,1)S(1)}, u32[]{:S(2)}, u32[]{:S(2)}) %collective-permute-start.10) | collective-permute-done | bytes 524320 | tf_op jit(solution)/shard_map/ppermute | solution.py:289
  27.8 2.2 %collective-permute-start.11 = (bf16[4,64,1024]{2,1,0:T(8,128)(2,1)S(1)}, bf16[4,64,1024]{2,1,0:T(8,128)(2,1)S(1)}, u32[]{:S(2)}, u32[]{:S(2)}) collective-permute-start(bf16[4,64,1024]{2,1,0:T(8,128)(2,1)S(1)} %collective-permute-done.10.second), channel_id=1, source_target_pairs={{7,4},{0,3},{15,12},{8,11},{23,20},{16,19},{31,28},{24,27}} | collective-permute-start | bytes 1572872 | tf_op jit(solution)/shard_map/ppermute | solution.py:291
  30.7 2.7 %collective-permute-done.4.second = bf16[4,64,1024]{2,1,0:T(8,128)(2,1)S(1)} collective-permute-done((bf16[4,64,1024]{2,1,0:T(8,128)(2,1)S(1)}, bf16[4,64,1024]{2,1,0:T(8,128)(2,1)S(1)}, u32[]{:S(2)}, u32[]{:S(2)}) %collective-permute-start.4) | collective-permute-done | bytes 524320 | tf_op jit(solution)/shard_map/ppermute | solution.py:289
  33.4 2.2 %collective-permute-start.5 = (bf16[4,64,1024]{2,1,0:T(8,128)(2,1)S(1)}, bf16[4,64,1024]{2,1,0:T(8,128)(2,1)S(1)}, u32[]{:S(2)}, u32[]{:S(2)}) collective-permute-start(bf16[4,64,1024]{2,1,0:T(8,128)(2,1)S(1)} %collective-permute-done.4.second), channel_id=1, source_target_pairs={{7,4},{0,3},{15,12},{8,11},{23,20},{16,19},{31,28},{24,27}} | collective-permute-start | bytes 1572872 | tf_op jit(solution)/shard_map/ppermute | solution.py:291
  35.6 2.4 %shard_map.40 = (f32[512,512]{1,0:T(8,128)S(1)}, f32[512,512]{1,0:T(8,128)S(1)}) custom-call(bf16[4,128,2048]{2,1,0:T(8,128)(2,1)S(1)} %get-tuple-element.22.whole, bf16[4,128,2048]{2,1,0:T(8,128)(2,1)S(1)} %collective-permute-done.2.beside), custom_call_target="tpu_custom_call" | custom-call | tf_op jit(solution)/shard_map/pallas_call | solution.py:145
  38.0 4.3 %collective-permute-done.11.third = bf16[4,64,1024]{2,1,0:T(8,128)(2,1)S(1)} collective-permute-done((bf16[4,64,1024]{2,1,0:T(8,128)(2,1)S(1)}, bf16[4,64,1024]{2,1,0:T(8,128)(2,1)S(1)}, u32[]{:S(2)}, u32[]{:S(2)}) %collective-permute-start.11) | collective-permute-done | bytes 524320 | tf_op jit(solution)/shard_map/ppermute | solution.py:291
  42.3 1.9 %shard_map.44 = (f32[384,128]{1,0:T(8,128)S(1)}, s16[400,128]{1,0:T(8,128)(2,1)S(1)}) custom-call(s32[32,3]{1,0:T(8,128)S(1)} %copy.6.pattern, bf16[4,128,2048]{2,1,0:T(8,128)(2,1)S(1)} %get-tuple-element.22.whole, f32[512,512]{1,0:T(8,128)S(1)} %get-tuple-element.26.near, bf16[4,64,1024]{2,1,0:T(8,128)(2,1)S(1)} %collective-permute-done.9.first, ...), custom_call_target="tpu_custom_call" | custom-call | tf_op jit(solution)/shard_map/pallas_call | solution.py:195
  44.2 2.0 %collective-permute-start.12 = (s16[400,128]{1,0:T(8,128)(2,1)S(1)}, s16[400,128]{1,0:T(8,128)(2,1)S(1)}, u32[]{:S(2)}, u32[]{:S(2)}) collective-permute-start(s16[400,128]{1,0:T(8,128)(2,1)S(1)} %get-tuple-element.30), channel_id=1, source_target_pairs={{0,8},{8,0},{16,24},{24,16},{1,9},{9,1},{17,25},{25,17},{2,10},{10... | collective-permute-start | bytes 307208 | tf_op jit(solution)/shard_map/ppermute | solution.py:299
  46.3 7.3 %collective-permute-done.5.third = bf16[4,64,1024]{2,1,0:T(8,128)(2,1)S(1)} collective-permute-done((bf16[4,64,1024]{2,1,0:T(8,128)(2,1)S(1)}, bf16[4,64,1024]{2,1,0:T(8,128)(2,1)S(1)}, u32[]{:S(2)}, u32[]{:S(2)}) %collective-permute-start.5) | collective-permute-done | bytes 524320 | tf_op jit(solution)/shard_map/ppermute | solution.py:291
  53.6 1.9 %shard_map.41 = (f32[384,128]{1,0:T(8,128)S(1)}, s16[400,128]{1,0:T(8,128)(2,1)S(1)}) custom-call(s32[32,3]{1,0:T(8,128)S(1)} %copy.6.pattern, bf16[4,128,2048]{2,1,0:T(8,128)(2,1)S(1)} %get-tuple-element.22.whole, f32[512,512]{1,0:T(8,128)S(1)} %get-tuple-element.23.near, bf16[4,64,1024]{2,1,0:T(8,128)(2,1)S(1)} %collective-permute-done.3.first, ...), custom_call_target="tpu_custom_call" | custom-call | tf_op jit(solution)/shard_map/pallas_call | solution.py:195
  55.5 2.0 %collective-permute-start.6 = (s16[400,128]{1,0:T(8,128)(2,1)S(1)}, s16[400,128]{1,0:T(8,128)(2,1)S(1)}, u32[]{:S(2)}, u32[]{:S(2)}) collective-permute-start(s16[400,128]{1,0:T(8,128)(2,1)S(1)} %get-tuple-element.25), channel_id=1, source_target_pairs={{0,8},{8,0},{16,24},{24,16},{1,9},{9,1},{17,25},{25,17},{2,10},{10... | collective-permute-start | bytes 307208 | tf_op jit(solution)/shard_map/ppermute | solution.py:299
  57.6 2.7 %collective-permute-start.13 = (s16[400,128]{1,0:T(8,128)(2,1)S(1)}, s16[400,128]{1,0:T(8,128)(2,1)S(1)}, u32[]{:S(2)}, u32[]{:S(2)}) collective-permute-start(s16[400,128]{1,0:T(8,128)(2,1)S(1)} %shard_map.45.mine), channel_id=1, source_target_pairs={{0,16},{8,24},{16,0},{24,8},{1,17},{9,25},{17,1},{25,9},{2,18},{10... | collective-permute-start | bytes 307208 | tf_op jit(solution)/shard_map/ppermute | solution.py:302
  60.4 3.0 %collective-permute-start.7 = (s16[400,128]{1,0:T(8,128)(2,1)S(1)}, s16[400,128]{1,0:T(8,128)(2,1)S(1)}, u32[]{:S(2)}, u32[]{:S(2)}) collective-permute-start(s16[400,128]{1,0:T(8,128)(2,1)S(1)} %shard_map.42.mine), channel_id=1, source_target_pairs={{0,16},{8,24},{16,0},{24,8},{1,17},{9,25},{17,1},{25,9},{2,18},{10... | collective-permute-start | bytes 307208 | tf_op jit(solution)/shard_map/ppermute | solution.py:302
  63.4 1.3 %collective-permute-done.13.other = s16[400,128]{1,0:T(8,128)(2,1)S(1)} collective-permute-done((s16[400,128]{1,0:T(8,128)(2,1)S(1)}, s16[400,128]{1,0:T(8,128)(2,1)S(1)}, u32[]{:S(2)}, u32[]{:S(2)}) %collective-permute-start.13) | collective-permute-done | bytes 102432 | tf_op jit(solution)/shard_map/ppermute | solution.py:302
  65.1 5.4 %collective-permute-done.7.other = s16[400,128]{1,0:T(8,128)(2,1)S(1)} collective-permute-done((s16[400,128]{1,0:T(8,128)(2,1)S(1)}, s16[400,128]{1,0:T(8,128)(2,1)S(1)}, u32[]{:S(2)}, u32[]{:S(2)}) %collective-permute-start.7) | collective-permute-done | bytes 102432 | tf_op jit(solution)/shard_map/ppermute | solution.py:302
  70.6 1.0 %collective-permute-done.14.refs_3_ = s16[400,128]{1,0:T(8,128)(2,1)S(1)} collective-permute-done((s16[400,128]{1,0:T(8,128)(2,1)S(1)}, s16[400,128]{1,0:T(8,128)(2,1)S(1)}, u32[]{:S(2)}, u32[]{:S(2)}) %collective-permute-start.14) | collective-permute-done | bytes 102432 | tf_op jit(solution)/shard_map/ppermute | solution.py:304
  71.6 4.2 %collective-permute-done.8.refs_1_ = s16[400,128]{1,0:T(8,128)(2,1)S(1)} collective-permute-done((s16[400,128]{1,0:T(8,128)(2,1)S(1)}, s16[400,128]{1,0:T(8,128)(2,1)S(1)}, u32[]{:S(2)}, u32[]{:S(2)}) %collective-permute-start.8) | collective-permute-done | bytes 102432 | tf_op jit(solution)/shard_map/ppermute | solution.py:304
  75.8 1.2 %shard_map.47 = f32[4,3,128,128]{3,2,1,0:T(8,128)} custom-call(s16[400,128]{1,0:T(8,128)(2,1)S(1)} %shard_map.43.refs_0_, s16[400,128]{1,0:T(8,128)(2,1)S(1)} %collective-permute-done.8.refs_1_, s16[400,128]{1,0:T(8,128)(2,1)S(1)} %shard_map.46.refs_2_, s16[400,128]{1,0:T(8,128)(2,1)S(1)} %collective-permute-done.14.refs_3_), custom_call_target="tpu_custom_call" | custom-call | tf_op jit(solution)/shard_map/pallas_call | solution.py:255
  (22 shorter events, 5.3 us)
Async XLA Ops:
  0.0 5.0 %collective-permute-start = (bf16[512,256]{1,0:T(8,128)(2,1)}, bf16[512,256]{1,0:T(8,128)(2,1)S(1)}, u32[]{:S(2)}, u32[]{:S(2)}) collective-permute-start(bf16[512,256]{1,0:T(8,128)(2,1)} %own.1), channel_id=1, source_target_pairs={{0,1},{1,0},{2,3},{3,2},{4,5},{5,4},{6,7},{7,6},{8,9},{9,8},{10,11... | collective-permute-start | bytes 786440 | tf_op jit(solution)/shard_map/ppermute | solution.py:281
  0.5 4.5 %collective-permute-start.1 = (bf16[512,256]{1,0:T(8,128)(2,1)}, bf16[512,256]{1,0:T(8,128)(2,1)S(1)}, u32[]{:S(2)}, u32[]{:S(2)}) collective-permute-start(bf16[512,256]{1,0:T(8,128)(2,1)} %own.1), channel_id=1, source_target_pairs={{1,2},{2,1},{3,4},{4,3},{5,6},{6,5},{9,10},{10,9},{11,12},{12,11},... | collective-permute-start | bytes 786440 | tf_op jit(solution)/shard_map/ppermute | solution.py:280
  1.9 1.9 %copy-start = (bf16[8,4,3,128,128]{4,3,2,1,0:T(8,128)(2,1)S(1)}, bf16[8,4,3,128,128]{4,3,2,1,0:T(8,128)(2,1)}, u32[]{:S(2)}) copy-start(bf16[8,4,3,128,128]{4,3,2,1,0:T(8,128)(2,1)} %tensor.1) | copy-start | bytes 9437188
  3.8 0.9 %copy-start.1 = (bf16[512,256]{1,0:T(8,128)(2,1)S(1)}, bf16[512,256]{1,0:T(8,128)(2,1)}, u32[]{:S(2)}) copy-start(bf16[512,256]{1,0:T(8,128)(2,1)} %own.1) | copy-start | bytes 786436
  10.6 25.0 %collective-permute-start.2 = (bf16[4,128,2048]{2,1,0:T(8,128)(2,1)S(1)}, bf16[4,128,2048]{2,1,0:T(8,128)(2,1)S(1)}, u32[]{:S(2)}, u32[]{:S(2)}) collective-permute-start(bf16[4,128,2048]{2,1,0:T(8,128)(2,1)S(1)} %get-tuple-element.22.whole), channel_id=1, source_target_pairs={{0,1},{1,0},{2,3},{3,2},{4,5},{5,4},{6,7},{7,6},{8,9},{9,8},{10,11... | collective-permute-start | bytes 6291464 | tf_op jit(solution)/shard_map/ppermute | solution.py:294
  16.7 11.1 %collective-permute-start.10 = (bf16[4,64,1024]{2,1,0:T(8,128)(2,1)S(1)}, bf16[4,64,1024]{2,1,0:T(8,128)(2,1)S(1)}, u32[]{:S(2)}, u32[]{:S(2)}) collective-permute-start(bf16[4,64,1024]{2,1,0:T(8,128)(2,1)S(1)} %get-tuple-element.28), channel_id=1, source_target_pairs={{1,2},{2,1},{5,6},{6,5},{3,7},{4,0},{9,10},{10,9},{13,14},{14,13},... | collective-permute-start | bytes 1572872 | tf_op jit(solution)/shard_map/ppermute | solution.py:289
  18.0 15.4 %collective-permute-start.4 = (bf16[4,64,1024]{2,1,0:T(8,128)(2,1)S(1)}, bf16[4,64,1024]{2,1,0:T(8,128)(2,1)S(1)}, u32[]{:S(2)}, u32[]{:S(2)}) collective-permute-start(bf16[4,64,1024]{2,1,0:T(8,128)(2,1)S(1)} %get-tuple-element.21.rest_1_), channel_id=1, source_target_pairs={{1,2},{2,1},{5,6},{6,5},{3,7},{4,0},{9,10},{10,9},{13,14},{14,13},... | collective-permute-start | bytes 1572872 | tf_op jit(solution)/shard_map/ppermute | solution.py:289
  19.3 18.6 %collective-permute-start.9 = (bf16[4,64,1024]{2,1,0:T(8,128)(2,1)S(1)}, bf16[4,64,1024]{2,1,0:T(8,128)(2,1)S(1)}, u32[]{:S(2)}, u32[]{:S(2)}) collective-permute-start(bf16[4,64,1024]{2,1,0:T(8,128)(2,1)S(1)} %get-tuple-element.27), channel_id=1, source_target_pairs={{1,2},{2,1},{3,4},{4,3},{5,6},{6,5},{9,10},{10,9},{11,12},{12,11},... | collective-permute-start | bytes 1572872 | tf_op jit(solution)/shard_map/ppermute | solution.py:290
  27.8 14.5 %collective-permute-start.11 = (bf16[4,64,1024]{2,1,0:T(8,128)(2,1)S(1)}, bf16[4,64,1024]{2,1,0:T(8,128)(2,1)S(1)}, u32[]{:S(2)}, u32[]{:S(2)}) collective-permute-start(bf16[4,64,1024]{2,1,0:T(8,128)(2,1)S(1)} %collective-permute-done.10.second), channel_id=1, source_target_pairs={{7,4},{0,3},{15,12},{8,11},{23,20},{16,19},{31,28},{24,27}} | collective-permute-start | bytes 1572872 | tf_op jit(solution)/shard_map/ppermute | solution.py:291
  30.0 16.3 %collective-permute-start.3 = (bf16[4,64,1024]{2,1,0:T(8,128)(2,1)S(1)}, bf16[4,64,1024]{2,1,0:T(8,128)(2,1)S(1)}, u32[]{:S(2)}, u32[]{:S(2)}) collective-permute-start(bf16[4,64,1024]{2,1,0:T(8,128)(2,1)S(1)} %get-tuple-element.20.rest_0_), channel_id=1, source_target_pairs={{1,2},{2,1},{3,4},{4,3},{5,6},{6,5},{9,10},{10,9},{11,12},{12,11},... | collective-permute-start | bytes 1572872 | tf_op jit(solution)/shard_map/ppermute | solution.py:290
  33.4 20.1 %collective-permute-start.5 = (bf16[4,64,1024]{2,1,0:T(8,128)(2,1)S(1)}, bf16[4,64,1024]{2,1,0:T(8,128)(2,1)S(1)}, u32[]{:S(2)}, u32[]{:S(2)}) collective-permute-start(bf16[4,64,1024]{2,1,0:T(8,128)(2,1)S(1)} %collective-permute-done.4.second), channel_id=1, source_target_pairs={{7,4},{0,3},{15,12},{8,11},{23,20},{16,19},{31,28},{24,27}} | collective-permute-start | bytes 1572872 | tf_op jit(solution)/shard_map/ppermute | solution.py:291
  44.2 13.3 %collective-permute-start.12 = (s16[400,128]{1,0:T(8,128)(2,1)S(1)}, s16[400,128]{1,0:T(8,128)(2,1)S(1)}, u32[]{:S(2)}, u32[]{:S(2)}) collective-permute-start(s16[400,128]{1,0:T(8,128)(2,1)S(1)} %get-tuple-element.30), channel_id=1, source_target_pairs={{0,8},{8,0},{16,24},{24,16},{1,9},{9,1},{17,25},{25,17},{2,10},{10... | collective-permute-start | bytes 307208 | tf_op jit(solution)/shard_map/ppermute | solution.py:299
  55.5 4.8 %collective-permute-start.6 = (s16[400,128]{1,0:T(8,128)(2,1)S(1)}, s16[400,128]{1,0:T(8,128)(2,1)S(1)}, u32[]{:S(2)}, u32[]{:S(2)}) collective-permute-start(s16[400,128]{1,0:T(8,128)(2,1)S(1)} %get-tuple-element.25), channel_id=1, source_target_pairs={{0,8},{8,0},{16,24},{24,16},{1,9},{9,1},{17,25},{25,17},{2,10},{10... | collective-permute-start | bytes 307208 | tf_op jit(solution)/shard_map/ppermute | solution.py:299
  57.6 7.0 %collective-permute-start.13 = (s16[400,128]{1,0:T(8,128)(2,1)S(1)}, s16[400,128]{1,0:T(8,128)(2,1)S(1)}, u32[]{:S(2)}, u32[]{:S(2)}) collective-permute-start(s16[400,128]{1,0:T(8,128)(2,1)S(1)} %shard_map.45.mine), channel_id=1, source_target_pairs={{0,16},{8,24},{16,0},{24,8},{1,17},{9,25},{17,1},{25,9},{2,18},{10... | collective-permute-start | bytes 307208 | tf_op jit(solution)/shard_map/ppermute | solution.py:302
  60.4 10.1 %collective-permute-start.7 = (s16[400,128]{1,0:T(8,128)(2,1)S(1)}, s16[400,128]{1,0:T(8,128)(2,1)S(1)}, u32[]{:S(2)}, u32[]{:S(2)}) collective-permute-start(s16[400,128]{1,0:T(8,128)(2,1)S(1)} %shard_map.42.mine), channel_id=1, source_target_pairs={{0,16},{8,24},{16,0},{24,8},{1,17},{9,25},{17,1},{25,9},{2,18},{10... | collective-permute-start | bytes 307208 | tf_op jit(solution)/shard_map/ppermute | solution.py:302
  64.8 6.8 %collective-permute-start.14 = (s16[400,128]{1,0:T(8,128)(2,1)S(1)}, s16[400,128]{1,0:T(8,128)(2,1)S(1)}, u32[]{:S(2)}, u32[]{:S(2)}) collective-permute-start(s16[400,128]{1,0:T(8,128)(2,1)S(1)} %shard_map.46.refs_2_), channel_id=1, source_target_pairs={{0,8},{8,0},{16,24},{24,16},{1,9},{9,1},{17,25},{25,17},{2,10},{10... | collective-permute-start | bytes 307208 | tf_op jit(solution)/shard_map/ppermute | solution.py:304
  70.6 5.3 %collective-permute-start.8 = (s16[400,128]{1,0:T(8,128)(2,1)S(1)}, s16[400,128]{1,0:T(8,128)(2,1)S(1)}, u32[]{:S(2)}, u32[]{:S(2)}) collective-permute-start(s16[400,128]{1,0:T(8,128)(2,1)S(1)} %shard_map.43.refs_0_), channel_id=1, source_target_pairs={{0,8},{8,0},{16,24},{24,16},{1,9},{9,1},{17,25},{25,17},{2,10},{10... | collective-permute-start | bytes 307208 | tf_op jit(solution)/shard_map/ppermute | solution.py:304

commit v3 on v2

v3 whole, which is shorter than its diff:
```python
import functools

import jax
import jax.numpy as jnp
from jax import lax
from jax.experimental import pallas as pl
from jax.experimental.pallas import tpu as pltpu
from jax.sharding import PartitionSpec as P

CUT = 64
PIECES = 2
SCALE_ROWS = 16
FULL = 32752.0
VMEM = pl.BlockSpec(memory_space=pltpu.VMEM)
ANY = pl.BlockSpec(memory_space=pl.ANY)
SMEM = pl.BlockSpec(memory_space=pltpu.SMEM)


def params(mib):
    return pltpu.CompilerParams(vmem_limit_bytes=mib << 20)


NO_COST = pl.CostEstimate(flops=0, bytes_accessed=0, transcendentals=0)


def fetch_kernel(tensor, own, tensor_out, own_out, sems):
    copies = [
        pltpu.make_async_copy(own, own_out, sems.at[0]),
        pltpu.make_async_copy(tensor, tensor_out, sems.at[1]),
    ]
    for copy in copies:
        copy.start()
    for copy in copies:
        copy.wait()


def fetch(tensor, own):
    arrays = (tensor, own)
    return pl.pallas_call(
        fetch_kernel,
        out_shape=[jax.ShapeDtypeStruct(a.shape, a.dtype) for a in arrays],
        in_specs=[ANY] * 2,
        out_specs=[VMEM] * 2,
        scratch_shapes=[pltpu.SemaphoreType.DMA((2,))],
        compiler_params=params(8),
        cost_estimate=NO_COST,
    )(*arrays)


def half_kernel(cuts, pattern, own, beside, across, tensor, *outs):
    parts, pieces = outs[: len(cuts) - 1], outs[len(cuts) - 1 :]
    aux, blocks, slots, width, _ = tensor.shape
    occupied = own.shape[1]
    device = lax.axis_index("bas")
    for m in range(blocks):
        chosen = []
        for j in range(slots):
            place = pattern[(device * blocks + m) * slots + j]
            group = place // blocks
            rows = pl.ds(pl.multiple_of(jnp.maximum(place, 0) % blocks * width, width), width)
            value = jnp.where(group == device ^ 1, beside[rows, :], across[rows, :])
            value = jnp.where(group == device, own[rows, :], value)
            chosen.append(jnp.where(place < 0, jnp.zeros_like(value), value))
        chosen = jnp.concatenate(chosen, axis=0)
        for p in range(aux):
            row = jnp.concatenate([tensor[p, m, j] for j in range(slots)], axis=1)
            half = jnp.dot(row, chosen, preferred_element_type=jnp.float32).astype(jnp.bfloat16)
            piece, column = divmod(p, aux // len(pieces))
            pieces[piece][m, :, column * occupied : (column + 1) * occupied] = half
            for part, start, stop in zip(parts, cuts, cuts[1:]):
                part[m, :, p * occupied : (p + 1) * occupied] = half[start:stop]


def half_forms(cuts, pattern, own, beside, across, tensor):
    aux, blocks, slots, width, _ = tensor.shape
    depth = aux * own.shape[1]
    shapes = [(blocks, b - a, depth) for a, b in zip(cuts, cuts[1:])]
    shapes += [(blocks, width, depth // PIECES)] * PIECES
    outs = pl.pallas_call(
        functools.partial(half_kernel, cuts),
        out_shape=[jax.ShapeDtypeStruct(shape, jnp.bfloat16) for shape in shapes],
        in_specs=[SMEM] + [VMEM] * 4,
        out_specs=[VMEM] * len(shapes),
        compiler_params=params(24),
        cost_estimate=NO_COST,
    )(pattern, own, beside, across, tensor)
    return outs[:-PIECES], outs[-PIECES:]


def encode(tiles, coded, scales):
    rows = tiles[0].shape[0]
    scales[...] = jnp.zeros_like(scales)
    for t, tile in enumerate(tiles):
        most = jnp.max(jnp.abs(tile), axis=0, keepdims=True)
        power = jnp.ceil(jnp.log2(jnp.maximum(most, 2.0**-90)))
        scales[t : t + 1, :] = power
        whole = jnp.round(tile * (FULL * jnp.exp2(-power)))
        coded[t * rows : (t + 1) * rows, :] = whole.astype(jnp.int32).astype(jnp.int16)
    end = len(tiles) * rows
    coded[end : end + SCALE_ROWS, :] = scales[...].astype(jnp.int32).astype(jnp.int16)


def decode(coded, rows, count):
    end = count * rows
    scales = coded[end : end + SCALE_ROWS, :].astype(jnp.int32).astype(jnp.float32)
    scales = jnp.exp2(scales) * (1.0 / FULL)
    for t in range(count):
        value = coded[t * rows : (t + 1) * rows, :].astype(jnp.int32).astype(jnp.float32)
        yield value * scales[t : t + 1, :]


def times(rows, pieces):
    total = 0.0
    for k, piece in enumerate(pieces):
        left, right = rows(k), piece[...]
        total += lax.dot_general(
            left.reshape(-1, left.shape[2]),
            right.reshape(-1, right.shape[2]),
            (((1,), (1,)), ((), ())),
            preferred_element_type=jnp.float32,
        )
    return total


def near_kernel(start, stop, *refs):
    whole, beside, product = refs[:PIECES], refs[PIECES : 2 * PIECES], refs[-1]
    half = product.shape[0] // 2
    product[:half, :] = times(lambda k: whole[k][:, start:stop, :], whole)
    product[half:, :] = times(lambda k: beside[k][:, start:stop, :], whole)


def near_products(start, stop, whole, beside, *earlier):
    blocks, width, _ = whole[0].shape
    return pl.pallas_call(
        functools.partial(near_kernel, start, stop),
        out_shape=jax.ShapeDtypeStruct((2 * blocks * (stop - start), blocks * width), jnp.float32),
        in_specs=[VMEM] * (2 * PIECES) + [ANY] * len(earlier),
        out_specs=VMEM,
        compiler_params=params(24),
        cost_estimate=NO_COST,
    )(*whole, *beside, *earlier)


def gate_kernel(_, out):
    out[...] = jnp.zeros_like(out)


def gate(earlier):
    return pl.pallas_call(
        gate_kernel,
        out_shape=jax.ShapeDtypeStruct((8, 128), jnp.float32),
        in_specs=[ANY],
        out_specs=VMEM,
        compiler_params=params(4),
        cost_estimate=NO_COST,
    )(earlier)


def tile_kernel(relays, count, pattern, near, *refs):
    whole, across, (kept, sent, far, scales, places, sem) = refs[:PIECES], refs[PIECES : PIECES + count], refs[-6:]
    blocks, width, depth = whole[0].shape
    rows = across[0].shape[1]
    slots = pattern.shape[0] // (blocks * lax.axis_size("bas"))
    device, layer = lax.axis_index("bas"), lax.axis_index("aux")
    half = blocks * slots // 2
    copy = pltpu.make_async_copy(pattern, places, sem)
    copy.start()

    def multiply(source):
        far[...] = times(lambda k: source[:, :, k * depth : (k + 1) * depth], whole)

    if count > 1:
        relayed = functools.reduce(jnp.logical_or, [device == target for target in relays])
        pl.when(relayed)(lambda: multiply(across[1]))
        pl.when(jnp.logical_not(relayed))(lambda: multiply(across[0]))
    else:
        multiply(across[0])
    copy.wait()

    def tile(t, parity):
        m = parity * (blocks // 2) + t // slots
        place = places[(device * blocks + m) * slots + t % slots]
        group, block = place // blocks, jnp.maximum(place, 0) % blocks
        columns = pl.ds(pl.multiple_of(m * width, width), width)
        close = block + jnp.where(group == device, 0, blocks)
        inside = near[pl.ds(pl.multiple_of(close * rows, rows), rows), columns]
        outside = far[pl.ds(pl.multiple_of(block * rows, rows), rows), columns]
        value = jnp.where((group == device) | (group == device ^ 1), inside, outside)
        return jnp.where(place < 0, 0.0, value)

    for t in range(half):
        kept[t * rows : (t + 1) * rows, :] = tile(t, layer % 2)
    encode([tile(t, 1 - layer % 2) for t in range(half)], sent, scales)


def chunk_tiles(relays, pattern, near, whole, across, *earlier):
    blocks, width, _ = whole[0].shape
    rows, slots = across[0].shape[1], pattern.shape[0] // (blocks * lax.axis_size("bas"))
    half = blocks * slots // 2
    return pl.pallas_call(
        functools.partial(tile_kernel, relays, len(across)),
        out_shape=[
            jax.ShapeDtypeStruct((half * rows, width), jnp.float32),
            jax.ShapeDtypeStruct((half * rows + SCALE_ROWS, width), jnp.int16),
        ],
        in_specs=[ANY] + [VMEM] * (1 + PIECES + len(across)) + [ANY] * len(earlier),
        out_specs=[VMEM] * 2,
        scratch_shapes=[
            pltpu.VMEM((blocks * rows, blocks * width), jnp.float32),
            pltpu.VMEM((SCALE_ROWS, width), jnp.float32),
            pltpu.SMEM(pattern.shape, pattern.dtype),
            pltpu.SemaphoreType.DMA,
        ],
        compiler_params=params(24),
        cost_estimate=NO_COST,
    )(pattern, near, *whole, *across, *earlier)


def add_kernel(count, mine, other, coded, scales):
    rows = (coded.shape[0] - SCALE_ROWS) // count
    if mine.dtype == jnp.float32:
        held = [mine[t * rows : (t + 1) * rows, :] for t in range(count)]
    else:
        held = decode(mine, rows, count)
    encode([a + b for a, b in zip(held, decode(other, rows, count))], coded, scales)


def add_coded(count, mine, other):
    return pl.pallas_call(
        functools.partial(add_kernel, count),
        out_shape=jax.ShapeDtypeStruct(other.shape, other.dtype),
        in_specs=[VMEM] * 2,
        out_specs=VMEM,
        scratch_shapes=[pltpu.VMEM((SCALE_ROWS, other.shape[1]), jnp.float32)],
        compiler_params=params(8),
        cost_estimate=NO_COST,
    )(mine, other)


def final_kernel(*refs):
    coded, (out, turned, sems) = refs[:-3], refs[-3:]
    blocks, slots, width, _ = out.shape
    half = blocks * slots // 2
    layer = lax.axis_index("aux")
    copies = []
    for mine in range(2):
        base = jnp.where(layer % 2 == mine, 0, half)
        chunks = [list(decode(part, (part.shape[0] - SCALE_ROWS) // half, half)) for part in coded[mine::2]]
        for t in range(half):
            at = mine * half + t
            turned[at] = jnp.concatenate([chunk[t] for chunk in chunks], axis=0).T
            place = base + t
            copies.append(
                pltpu.make_async_copy(turned.at[at], out.at[place // slots, place % slots], sems.at[at])
            )
            copies[-1].start()
    for copy in copies:
        copy.wait()


def final_tiles(shape, coded):
    blocks, slots, width, _ = shape
    return pl.pallas_call(
        final_kernel,
        out_shape=jax.ShapeDtypeStruct(shape, jnp.float32),
        in_specs=[VMEM] * len(coded),
        out_specs=ANY,
        scratch_shapes=[
            pltpu.VMEM((blocks * slots, width, width), jnp.float32),
            pltpu.SemaphoreType.DMA((blocks * slots,)),
        ],
        compiler_params=params(8),
        cost_estimate=NO_COST,
    )(*coded)


def flipped(size, mask):
    return [(i, i ^ mask) for i in range(size)]


def body(coefficients, tensor, pattern):
    devices, layers = lax.axis_size("bas"), lax.axis_size("aux")
    _, blocks, slots, width, _ = tensor.shape
    chip = flipped(devices, 1)
    across = [pair for i in range(1, devices - 1, 2) for pair in ((i, i + 1), (i + 1, i))]
    detours = ((3, 4, 7), (4, 3, 0)) if devices == 8 else ()
    direct = [pair for pair in across if pair not in [d[:2] for d in detours]]
    there = [(source, via) for source, _, via in detours]
    onward = [(via, target) for _, target, via in detours]
    relays = tuple(target for _, target, _ in detours)

    beyond = lax.ppermute(coefficients, "bas", across)
    beside = lax.ppermute(coefficients, "bas", chip)
    tensor, coefficients = fetch(tensor, coefficients)
    cuts = (0, CUT, width)
    pattern = pattern.reshape(-1)
    (early, late), whole = half_forms(cuts, pattern, coefficients, beside, beyond, tensor)
    arrived = [[lax.ppermute(early, "bas", across)], [lax.ppermute(late, "bas", direct)]]
    if detours:
        arrived[1].append(lax.ppermute(lax.ppermute(late, "bas", there), "bas", onward))
    beside = [lax.ppermute(piece, "bas", chip) for piece in whole]
    half = blocks * slots // 2
    coded, earlier, opened = [], (), gate(arrived[0][0])
    for start, stop, held in zip(cuts, cuts[1:], arrived):
        near = near_products(start, stop, whole, beside, opened)
        kept, sent = chunk_tiles(relays, pattern, near, whole, held, *earlier)
        mine = add_coded(half, kept, lax.ppermute(sent, "aux", flipped(layers, 1)))
        earlier = (mine,)
        mask = 2
        while mask < layers:
            mine = add_coded(half, mine, lax.ppermute(mine, "aux", flipped(layers, mask)))
            mask *= 2
        coded += [mine, lax.ppermute(mine, "aux", flipped(layers, 1))]
    return final_tiles((blocks, slots, width, width), coded)


def solution(mesh):
    return jax.shard_map(
        body,
        mesh=mesh,
        in_specs=(P("bas", None), P("aux", "bas", None, None, None), P()),
        out_specs=P("bas", None, None, None),
        check_vma=False,
    )
```

time: 77.4 us -> 73 us (0.943)
  Pallas kernels: 13.6 us -> 7.97 us
  waiting for transfers between devices: 34 us -> 37.5 us
  starting transfers between devices: 25.7 us -> 23.4 us
    pallas_call x5 -> x6, Pallas kernels: 11.8 us -> 6.28 us  [the longest x2 2.55 us: near_products(): pl.pallas_call(functools.partial(near_kernel, start, stop), out_shape=jax...]
    ppermute x7 -> x6, starting transfers between devices: 14.5 us -> 10.9 us  [the longest x2 6.79 us: body(): beside = [lax.ppermute(piece, 'bas', chip) for piece in whole]]
    ppermute x7 -> x6, waiting for transfers between devices: 22.1 us -> 24.6 us  [the longest x1 13 us: body(): lax.ppermute(late, 'bas', there)]
    ppermute x2, waiting for transfers between devices: 0.01 us -> 1.41 us  [body(): mine = add_coded(half, kept, lax.ppermute(sent, 'aux', flipped(layers, 1)))]
    ppermute x2, starting transfers between devices: 4.08 us -> 5.17 us  [body(): mine = add_coded(half, kept, lax.ppermute(sent, 'aux', flipped(layers, 1)))]
  transfers between devices with their start and end apart: 15 -> 14, of which waited for: 8 -> 7; matrix products, arithmetic and copies ran while one was open for 1% -> 1% of each run, Pallas kernels for 9% -> 6%
where the time goes in v3:
time: 73 us; the launch traced here: 72.8 us
  waiting for transfers between devices  37.5 us (51%)
  starting transfers between devices  23.4 us (32%)
  Pallas kernels  7.97 us (11%)
  local copies, waits for them, and re-layouts  3.7 us (5%)
    ppermute x1, waiting for transfers between devices, body(): lax.ppermute(late, 'bas', there)  13 us
    ppermute x1, waiting for transfers between devices, body(): lax.ppermute(lax.ppermute(late, 'bas', there), 'bas', onward)  11.5 us
    ppermute x2, starting transfers between devices, body(): beside = [lax.ppermute(piece, 'bas', chip) for piece in whole]  6.79 us
    ppermute x2, waiting for transfers between devices, body(): lax.ppermute(mine, 'aux', flipped(layers, mask))  6.57 us
    ppermute x2, starting transfers between devices, body(): lax.ppermute(mine, 'aux', flipped(layers, mask))  5.69 us
    ppermute x2, starting transfers between devices, body(): mine = add_coded(half, kept, lax.ppermute(sent, 'aux', flipped(layers, 1)))  5.17 us
    ppermute x2, waiting for transfers between devices, body(): coded += [mine, lax.ppermute(mine, 'aux', flipped(layers, 1))]  4.94 us
    unnamed x5, local copies, waits for them, and re-layouts  3.6 us
  transfers between devices with their start and end apart: 14, of which 7 were waited for; matrix products, arithmetic and copies ran while one was open for 1% of the time, Pallas kernels for 6%

profile of v3, /device:TPU:0, one launch (start us, length us, event | category | flops | bytes accessed | tf_op | source)
XLA Modules:
  0.0 72.8 jit_solution(9603719149400675772)
XLA Ops:
  1.1 0.8 %copy.5 = s32[32,3]{1,0:T(8,128)S(1)} copy(s32[32,3]{0,1:T(4,128)} %param.5) | data formatting | bytes 768 | tf_op args[2]
  2.0 1.9 %copy-done = bf16[8,4,3,128,128]{4,3,2,1,0:T(8,128)(2,1)S(1)} copy-done((bf16[8,4,3,128,128]{4,3,2,1,0:T(8,128)(2,1)S(1)}, bf16[8,4,3,128,128]{4,3,2,1,0:T(8,128)(2,1)}, u32[]{:S(2)}) %copy-start) | copy-done | bytes 3145752
  3.9 0.9 %copy-done.1 = bf16[512,256]{1,0:T(8,128)(2,1)S(1)} copy-done((bf16[512,256]{1,0:T(8,128)(2,1)S(1)}, bf16[512,256]{1,0:T(8,128)(2,1)}, u32[]{:S(2)}) %copy-start.1) | copy-done | bytes 262168
  5.1 1.8 %shard_map.38 = (bf16[4,64,2048]{2,1,0:T(8,128)(2,1)S(1)}, bf16[4,64,2048]{2,1,0:T(8,128)(2,1)S(1)}, bf16[4,128,1024]{2,1,0:T(8,128)(2,1)S(1)}, bf16[4,128,1024]{2,1,0:T(8,128)(2,1)S(1)}) custom-call(s32[96]{0:T(128)S(1)} %reshape.3.pattern, bf16[512,256]{1,0:T(8,128)(2,1)S(1)} %get-tuple-element.15.own, bf16[512,256]{1,0:T(8,128)(2,1)S(1)} %collective-permute-done.beside, ...), custom_call_target="tpu_custom_call" | custom-call | tf_op jit(solution)/shard_map/pallas_call | solution.py:79
  6.9 1.3 %collective-permute-start.9 = (bf16[4,64,2048]{2,1,0:T(8,128)(2,1)S(1)}, bf16[4,64,2048]{2,1,0:T(8,128)(2,1)S(1)}, u32[]{:S(2)}, u32[]{:S(2)}) collective-permute-start(bf16[4,64,2048]{2,1,0:T(8,128)(2,1)S(1)} %get-tuple-element.22), channel_id=1, source_target_pairs={{3,7},{4,0},{11,15},{12,8},{19,23},{20,16},{27,31},{28,24}} | collective-permute-start | bytes 3145736 | tf_op jit(solution)/shard_map/ppermute | solution.py:300
  8.2 0.7 %collective-permute-start.4 = (bf16[4,64,2048]{2,1,0:T(8,128)(2,1)S(1)}, bf16[4,64,2048]{2,1,0:T(8,128)(2,1)S(1)}, u32[]{:S(2)}, u32[]{:S(2)}) collective-permute-start(bf16[4,64,2048]{2,1,0:T(8,128)(2,1)S(1)} %get-tuple-element.19), channel_id=1, source_target_pairs={{1,2},{2,1},{3,4},{4,3},{5,6},{6,5},{9,10},{10,9},{11,12},{12,11},... | collective-permute-start | bytes 3145736 | tf_op jit(solution)/shard_map/ppermute | solution.py:298
  9.0 6.7 %collective-permute-start.2 = (bf16[4,128,1024]{2,1,0:T(8,128)(2,1)S(1)}, bf16[4,128,1024]{2,1,0:T(8,128)(2,1)S(1)}, u32[]{:S(2)}, u32[]{:S(2)}) collective-permute-start(bf16[4,128,1024]{2,1,0:T(8,128)(2,1)S(1)} %get-tuple-element.17.refs_0_), channel_id=1, source_target_pairs={{0,1},{1,0},{2,3},{3,2},{4,5},{5,4},{6,7},{7,6},{8,9},{9,8},{10,11... | collective-permute-start | bytes 3145736 | tf_op jit(solution)/shard_map/ppermute | solution.py:301
  16.5 13.0 %collective-permute-done.9 = bf16[4,64,2048]{2,1,0:T(8,128)(2,1)S(1)} collective-permute-done((bf16[4,64,2048]{2,1,0:T(8,128)(2,1)S(1)}, bf16[4,64,2048]{2,1,0:T(8,128)(2,1)S(1)}, u32[]{:S(2)}, u32[]{:S(2)}) %collective-permute-start.9) | collective-permute-done | bytes 1048608 | tf_op jit(solution)/shard_map/ppermute | solution.py:300
  29.5 1.3 %collective-permute-start.10 = (bf16[4,64,2048]{2,1,0:T(8,128)(2,1)S(1)}, bf16[4,64,2048]{2,1,0:T(8,128)(2,1)S(1)}, u32[]{:S(2)}, u32[]{:S(2)}) collective-permute-start(bf16[4,64,2048]{2,1,0:T(8,128)(2,1)S(1)} %collective-permute-done.9), channel_id=1, source_target_pairs={{7,4},{0,3},{15,12},{8,11},{23,20},{16,19},{31,28},{24,27}} | collective-permute-start | bytes 3145736 | tf_op jit(solution)/shard_map/ppermute | solution.py:300
  30.9 1.3 %shard_map.40.near = f32[512,512]{1,0:T(8,128)S(1)} custom-call(bf16[4,128,1024]{2,1,0:T(8,128)(2,1)S(1)} %get-tuple-element.17.refs_0_, bf16[4,128,1024]{2,1,0:T(8,128)(2,1)S(1)} %get-tuple-element.18.refs_1_, bf16[4,128,1024]{2,1,0:T(8,128)(2,1)S(1)} %collective-permute-done.2.refs_2_, bf16[4,128,1024]{2,1,0:T(8,128)(2,1)S(1)} %collective-permute-done.3.refs_3_, ...), custom_call_target="tpu_custom_call" | custom-call | tf_op jit(solution)/shard_map/pallas_call | solution.py:134
  32.2 1.0 %shard_map.41 = (f32[384,128]{1,0:T(8,128)S(1)}, s16[400,128]{1,0:T(8,128)(2,1)S(1)}) custom-call(s32[96]{0:T(128)S(1)} %reshape.3.pattern, f32[512,512]{1,0:T(8,128)S(1)} %shard_map.40.near, bf16[4,128,1024]{2,1,0:T(8,128)(2,1)S(1)} %get-tuple-element.17.refs_0_, bf16[4,128,1024]{2,1,0:T(8,128)(2,1)S(1)} %get-tuple-element.18.refs_1_, ...), custom_call_target="tpu_custom_call" | custom-call | tf_op jit(solution)/shard_map/pallas_call | solution.py:200
  33.2 2.3 %collective-permute-start.5 = (s16[400,128]{1,0:T(8,128)(2,1)S(1)}, s16[400,128]{1,0:T(8,128)(2,1)S(1)}, u32[]{:S(2)}, u32[]{:S(2)}) collective-permute-start(s16[400,128]{1,0:T(8,128)(2,1)S(1)} %get-tuple-element.21), channel_id=1, source_target_pairs={{0,8},{8,0},{16,24},{24,16},{1,9},{9,1},{17,25},{25,17},{2,10},{10... | collective-permute-start | bytes 307208 | tf_op jit(solution)/shard_map/ppermute | solution.py:307
  35.5 1.3 %shard_map.44.near = f32[512,512]{1,0:T(8,128)S(1)} custom-call(bf16[4,128,1024]{2,1,0:T(8,128)(2,1)S(1)} %get-tuple-element.17.refs_0_, bf16[4,128,1024]{2,1,0:T(8,128)(2,1)S(1)} %get-tuple-element.18.refs_1_, bf16[4,128,1024]{2,1,0:T(8,128)(2,1)S(1)} %collective-permute-done.2.refs_2_, bf16[4,128,1024]{2,1,0:T(8,128)(2,1)S(1)} %collective-permute-done.3.refs_3_, ...), custom_call_target="tpu_custom_call" | custom-call | tf_op jit(solution)/shard_map/pallas_call | solution.py:134
  36.7 1.4 %collective-permute-done.5.other = s16[400,128]{1,0:T(8,128)(2,1)S(1)} collective-permute-done((s16[400,128]{1,0:T(8,128)(2,1)S(1)}, s16[400,128]{1,0:T(8,128)(2,1)S(1)}, u32[]{:S(2)}, u32[]{:S(2)}) %collective-permute-start.5) | collective-permute-done | bytes 102432 | tf_op jit(solution)/shard_map/ppermute | solution.py:307
  38.2 11.5 %collective-permute-done.10.refs_3_ = bf16[4,64,2048]{2,1,0:T(8,128)(2,1)S(1)} collective-permute-done((bf16[4,64,2048]{2,1,0:T(8,128)(2,1)S(1)}, bf16[4,64,2048]{2,1,0:T(8,128)(2,1)S(1)}, u32[]{:S(2)}, u32[]{:S(2)}) %collective-permute-start.10) | collective-permute-done | bytes 1048608 | tf_op jit(solution)/shard_map/ppermute | solution.py:300
  49.7 1.0 %shard_map.45 = (f32[384,128]{1,0:T(8,128)S(1)}, s16[400,128]{1,0:T(8,128)(2,1)S(1)}) custom-call(s32[96]{0:T(128)S(1)} %reshape.3.pattern, f32[512,512]{1,0:T(8,128)S(1)} %shard_map.44.near, bf16[4,128,1024]{2,1,0:T(8,128)(2,1)S(1)} %get-tuple-element.17.refs_0_, bf16[4,128,1024]{2,1,0:T(8,128)(2,1)S(1)} %get-tuple-element.18.refs_1_, ...), custom_call_target="tpu_custom_call" | custom-call | tf_op jit(solution)/shard_map/pallas_call | solution.py:200
  50.7 2.9 %collective-permute-start.11 = (s16[400,128]{1,0:T(8,128)(2,1)S(1)}, s16[400,128]{1,0:T(8,128)(2,1)S(1)}, u32[]{:S(2)}, u32[]{:S(2)}) collective-permute-start(s16[400,128]{1,0:T(8,128)(2,1)S(1)} %get-tuple-element.24), channel_id=1, source_target_pairs={{0,8},{8,0},{16,24},{24,16},{1,9},{9,1},{17,25},{25,17},{2,10},{10... | collective-permute-start | bytes 307208 | tf_op jit(solution)/shard_map/ppermute | solution.py:307
  53.6 2.6 %collective-permute-start.6 = (s16[400,128]{1,0:T(8,128)(2,1)S(1)}, s16[400,128]{1,0:T(8,128)(2,1)S(1)}, u32[]{:S(2)}, u32[]{:S(2)}) collective-permute-start(s16[400,128]{1,0:T(8,128)(2,1)S(1)} %shard_map.42.mine.refs_4_), channel_id=1, source_target_pairs={{0,16},{8,24},{16,0},{24,8},{1,17},{9,25},{17,1},{25,9},{2,18},{10... | collective-permute-start | bytes 307208 | tf_op jit(solution)/shard_map/ppermute | solution.py:311
  56.3 3.1 %collective-permute-start.12 = (s16[400,128]{1,0:T(8,128)(2,1)S(1)}, s16[400,128]{1,0:T(8,128)(2,1)S(1)}, u32[]{:S(2)}, u32[]{:S(2)}) collective-permute-start(s16[400,128]{1,0:T(8,128)(2,1)S(1)} %shard_map.46.mine), channel_id=1, source_target_pairs={{0,16},{8,24},{16,0},{24,8},{1,17},{9,25},{17,1},{25,9},{2,18},{10... | collective-permute-start | bytes 307208 | tf_op jit(solution)/shard_map/ppermute | solution.py:311
  59.4 1.1 %collective-permute-done.6.other = s16[400,128]{1,0:T(8,128)(2,1)S(1)} collective-permute-done((s16[400,128]{1,0:T(8,128)(2,1)S(1)}, s16[400,128]{1,0:T(8,128)(2,1)S(1)}, u32[]{:S(2)}, u32[]{:S(2)}) %collective-permute-start.6) | collective-permute-done | bytes 102432 | tf_op jit(solution)/shard_map/ppermute | solution.py:311
  61.1 5.4 %collective-permute-done.12.other = s16[400,128]{1,0:T(8,128)(2,1)S(1)} collective-permute-done((s16[400,128]{1,0:T(8,128)(2,1)S(1)}, s16[400,128]{1,0:T(8,128)(2,1)S(1)}, u32[]{:S(2)}, u32[]{:S(2)}) %collective-permute-start.12) | collective-permute-done | bytes 102432 | tf_op jit(solution)/shard_map/ppermute | solution.py:311
  66.7 0.8 %collective-permute-done.7.refs_1_ = s16[400,128]{1,0:T(8,128)(2,1)S(1)} collective-permute-done((s16[400,128]{1,0:T(8,128)(2,1)S(1)}, s16[400,128]{1,0:T(8,128)(2,1)S(1)}, u32[]{:S(2)}, u32[]{:S(2)}) %collective-permute-start.7) | collective-permute-done | bytes 102432 | tf_op jit(solution)/shard_map/ppermute | solution.py:313
  67.5 4.2 %collective-permute-done.13.refs_3_ = s16[400,128]{1,0:T(8,128)(2,1)S(1)} collective-permute-done((s16[400,128]{1,0:T(8,128)(2,1)S(1)}, s16[400,128]{1,0:T(8,128)(2,1)S(1)}, u32[]{:S(2)}, u32[]{:S(2)}) %collective-permute-start.13) | collective-permute-done | bytes 102432 | tf_op jit(solution)/shard_map/ppermute | solution.py:313
  71.7 1.1 %shard_map.48 = f32[4,3,128,128]{3,2,1,0:T(8,128)} custom-call(s16[400,128]{1,0:T(8,128)(2,1)S(1)} %shard_map.43.refs_0_, s16[400,128]{1,0:T(8,128)(2,1)S(1)} %collective-permute-done.7.refs_1_, s16[400,128]{1,0:T(8,128)(2,1)S(1)} %shard_map.47.refs_2_, s16[400,128]{1,0:T(8,128)(2,1)S(1)} %collective-permute-done.13.refs_3_), custom_call_target="tpu_custom_call" | custom-call | tf_op jit(solution)/shard_map/pallas_call | solution.py:263
  (22 shorter events, 3.3 us)
Async XLA Ops:
  0.0 5.1 %collective-permute-start = (bf16[512,256]{1,0:T(8,128)(2,1)}, bf16[512,256]{1,0:T(8,128)(2,1)S(1)}, u32[]{:S(2)}, u32[]{:S(2)}) collective-permute-start(bf16[512,256]{1,0:T(8,128)(2,1)} %own.1), channel_id=1, source_target_pairs={{0,1},{1,0},{2,3},{3,2},{4,5},{5,4},{6,7},{7,6},{8,9},{9,8},{10,11... | collective-permute-start | bytes 786440 | tf_op jit(solution)/shard_map/ppermute | solution.py:293
  0.5 4.7 %collective-permute-start.1 = (bf16[512,256]{1,0:T(8,128)(2,1)}, bf16[512,256]{1,0:T(8,128)(2,1)S(1)}, u32[]{:S(2)}, u32[]{:S(2)}) collective-permute-start(bf16[512,256]{1,0:T(8,128)(2,1)} %own.1), channel_id=1, source_target_pairs={{1,2},{2,1},{3,4},{4,3},{5,6},{6,5},{9,10},{10,9},{11,12},{12,11},... | collective-permute-start | bytes 786440 | tf_op jit(solution)/shard_map/ppermute | solution.py:292
  2.0 1.9 %copy-start = (bf16[8,4,3,128,128]{4,3,2,1,0:T(8,128)(2,1)S(1)}, bf16[8,4,3,128,128]{4,3,2,1,0:T(8,128)(2,1)}, u32[]{:S(2)}) copy-start(bf16[8,4,3,128,128]{4,3,2,1,0:T(8,128)(2,1)} %tensor.1) | copy-start | bytes 9437188
  3.9 0.9 %copy-start.1 = (bf16[512,256]{1,0:T(8,128)(2,1)S(1)}, bf16[512,256]{1,0:T(8,128)(2,1)}, u32[]{:S(2)}) copy-start(bf16[512,256]{1,0:T(8,128)(2,1)} %own.1) | copy-start | bytes 786436
  6.9 22.6 %collective-permute-start.9 = (bf16[4,64,2048]{2,1,0:T(8,128)(2,1)S(1)}, bf16[4,64,2048]{2,1,0:T(8,128)(2,1)S(1)}, u32[]{:S(2)}, u32[]{:S(2)}) collective-permute-start(bf16[4,64,2048]{2,1,0:T(8,128)(2,1)S(1)} %get-tuple-element.22), channel_id=1, source_target_pairs={{3,7},{4,0},{11,15},{12,8},{19,23},{20,16},{27,31},{28,24}} | collective-permute-start | bytes 3145736 | tf_op jit(solution)/shard_map/ppermute | solution.py:300
  8.2 22.7 %collective-permute-start.4 = (bf16[4,64,2048]{2,1,0:T(8,128)(2,1)S(1)}, bf16[4,64,2048]{2,1,0:T(8,128)(2,1)S(1)}, u32[]{:S(2)}, u32[]{:S(2)}) collective-permute-start(bf16[4,64,2048]{2,1,0:T(8,128)(2,1)S(1)} %get-tuple-element.19), channel_id=1, source_target_pairs={{1,2},{2,1},{3,4},{4,3},{5,6},{6,5},{9,10},{10,9},{11,12},{12,11},... | collective-permute-start | bytes 3145736 | tf_op jit(solution)/shard_map/ppermute | solution.py:298
  9.0 21.9 %collective-permute-start.2 = (bf16[4,128,1024]{2,1,0:T(8,128)(2,1)S(1)}, bf16[4,128,1024]{2,1,0:T(8,128)(2,1)S(1)}, u32[]{:S(2)}, u32[]{:S(2)}) collective-permute-start(bf16[4,128,1024]{2,1,0:T(8,128)(2,1)S(1)} %get-tuple-element.17.refs_0_), channel_id=1, source_target_pairs={{0,1},{1,0},{2,3},{3,2},{4,5},{5,4},{6,7},{7,6},{8,9},{9,8},{10,11... | collective-permute-start | bytes 3145736 | tf_op jit(solution)/shard_map/ppermute | solution.py:301
  15.7 15.2 %collective-permute-start.3 = (bf16[4,128,1024]{2,1,0:T(8,128)(2,1)S(1)}, bf16[4,128,1024]{2,1,0:T(8,128)(2,1)S(1)}, u32[]{:S(2)}, u32[]{:S(2)}) collective-permute-start(bf16[4,128,1024]{2,1,0:T(8,128)(2,1)S(1)} %get-tuple-element.18.refs_1_), channel_id=1, source_target_pairs={{0,1},{1,0},{2,3},{3,2},{4,5},{5,4},{6,7},{7,6},{8,9},{9,8},{10,11... | collective-permute-start | bytes 3145736 | tf_op jit(solution)/shard_map/ppermute | solution.py:301
  15.8 22.4 %collective-permute-start.8 = (bf16[4,64,2048]{2,1,0:T(8,128)(2,1)S(1)}, bf16[4,64,2048]{2,1,0:T(8,128)(2,1)S(1)}, u32[]{:S(2)}, u32[]{:S(2)}) collective-permute-start(bf16[4,64,2048]{2,1,0:T(8,128)(2,1)S(1)} %get-tuple-element.22), channel_id=1, source_target_pairs={{1,2},{2,1},{5,6},{6,5},{9,10},{10,9},{13,14},{14,13},{17,18},{18,... | collective-permute-start | bytes 3145736 | tf_op jit(solution)/shard_map/ppermute | solution.py:298
  29.5 20.2 %collective-permute-start.10 = (bf16[4,64,2048]{2,1,0:T(8,128)(2,1)S(1)}, bf16[4,64,2048]{2,1,0:T(8,128)(2,1)S(1)}, u32[]{:S(2)}, u32[]{:S(2)}) collective-permute-start(bf16[4,64,2048]{2,1,0:T(8,128)(2,1)S(1)} %collective-permute-done.9), channel_id=1, source_target_pairs={{7,4},{0,3},{15,12},{8,11},{23,20},{16,19},{31,28},{24,27}} | collective-permute-start | bytes 3145736 | tf_op jit(solution)/shard_map/ppermute | solution.py:300
  33.2 4.9 %collective-permute-start.5 = (s16[400,128]{1,0:T(8,128)(2,1)S(1)}, s16[400,128]{1,0:T(8,128)(2,1)S(1)}, u32[]{:S(2)}, u32[]{:S(2)}) collective-permute-start(s16[400,128]{1,0:T(8,128)(2,1)S(1)} %get-tuple-element.21), channel_id=1, source_target_pairs={{0,8},{8,0},{16,24},{24,16},{1,9},{9,1},{17,25},{25,17},{2,10},{10... | collective-permute-start | bytes 307208 | tf_op jit(solution)/shard_map/ppermute | solution.py:307
  50.7 5.5 %collective-permute-start.11 = (s16[400,128]{1,0:T(8,128)(2,1)S(1)}, s16[400,128]{1,0:T(8,128)(2,1)S(1)}, u32[]{:S(2)}, u32[]{:S(2)}) collective-permute-start(s16[400,128]{1,0:T(8,128)(2,1)S(1)} %get-tuple-element.24), channel_id=1, source_target_pairs={{0,8},{8,0},{16,24},{24,16},{1,9},{9,1},{17,25},{25,17},{2,10},{10... | collective-permute-start | bytes 307208 | tf_op jit(solution)/shard_map/ppermute | solution.py:307
  53.6 7.0 %collective-permute-start.6 = (s16[400,128]{1,0:T(8,128)(2,1)S(1)}, s16[400,128]{1,0:T(8,128)(2,1)S(1)}, u32[]{:S(2)}, u32[]{:S(2)}) collective-permute-start(s16[400,128]{1,0:T(8,128)(2,1)S(1)} %shard_map.42.mine.refs_4_), channel_id=1, source_target_pairs={{0,16},{8,24},{16,0},{24,8},{1,17},{9,25},{17,1},{25,9},{2,18},{10... | collective-permute-start | bytes 307208 | tf_op jit(solution)/shard_map/ppermute | solution.py:311
  56.3 10.3 %collective-permute-start.12 = (s16[400,128]{1,0:T(8,128)(2,1)S(1)}, s16[400,128]{1,0:T(8,128)(2,1)S(1)}, u32[]{:S(2)}, u32[]{:S(2)}) collective-permute-start(s16[400,128]{1,0:T(8,128)(2,1)S(1)} %shard_map.46.mine), channel_id=1, source_target_pairs={{0,16},{8,24},{16,0},{24,8},{1,17},{9,25},{17,1},{25,9},{2,18},{10... | collective-permute-start | bytes 307208 | tf_op jit(solution)/shard_map/ppermute | solution.py:311
  60.6 6.9 %collective-permute-start.7 = (s16[400,128]{1,0:T(8,128)(2,1)S(1)}, s16[400,128]{1,0:T(8,128)(2,1)S(1)}, u32[]{:S(2)}, u32[]{:S(2)}) collective-permute-start(s16[400,128]{1,0:T(8,128)(2,1)S(1)} %shard_map.43.refs_0_), channel_id=1, source_target_pairs={{0,8},{8,0},{16,24},{24,16},{1,9},{9,1},{17,25},{25,17},{2,10},{10... | collective-permute-start | bytes 307208 | tf_op jit(solution)/shard_map/ppermute | solution.py:313
  66.7 5.0 %collective-permute-start.13 = (s16[400,128]{1,0:T(8,128)(2,1)S(1)}, s16[400,128]{1,0:T(8,128)(2,1)S(1)}, u32[]{:S(2)}, u32[]{:S(2)}) collective-permute-start(s16[400,128]{1,0:T(8,128)(2,1)S(1)} %shard_map.47.refs_2_), channel_id=1, source_target_pairs={{0,8},{8,0},{16,24},{24,16},{1,9},{9,1},{17,25},{25,17},{2,10},{10... | collective-permute-start | bytes 307208 | tf_op jit(solution)/shard_map/ppermute | solution.py:313

commit v4 on v3

--- a/solution.py
+++ b/solution.py
@@ -216,7 +216,8 @@
     )(pattern, near, *whole, *across, *earlier)
 
 
-def add_kernel(count, mine, other, coded, scales):
+def add_kernel(count, mine, other, *rest):
+    coded, scales = rest[-2:]
     rows = (coded.shape[0] - SCALE_ROWS) // count
     if mine.dtype == jnp.float32:
         held = [mine[t * rows : (t + 1) * rows, :] for t in range(count)]
@@ -225,16 +226,16 @@
     encode([a + b for a, b in zip(held, decode(other, rows, count))], coded, scales)
 
 
-def add_coded(count, mine, other):
+def add_coded(count, mine, other, *earlier):
     return pl.pallas_call(
         functools.partial(add_kernel, count),
         out_shape=jax.ShapeDtypeStruct(other.shape, other.dtype),
-        in_specs=[VMEM] * 2,
+        in_specs=[VMEM] * 2 + [ANY] * len(earlier),
         out_specs=VMEM,
         scratch_shapes=[pltpu.VMEM((SCALE_ROWS, other.shape[1]), jnp.float32)],
         compiler_params=params(8),
         cost_estimate=NO_COST,
-    )(mine, other)
+    )(mine, other, *earlier)
 
 
 def final_kernel(*refs):
@@ -300,16 +301,17 @@
         arrived[1].append(lax.ppermute(lax.ppermute(late, "bas", there), "bas", onward))
     beside = [lax.ppermute(piece, "bas", chip) for piece in whole]
     half = blocks * slots // 2
-    coded, earlier, opened = [], (), gate(arrived[0][0])
+    coded, earlier, summed, opened = [], (), (), gate(arrived[0][0])
     for start, stop, held in zip(cuts, cuts[1:], arrived):
         near = near_products(start, stop, whole, beside, opened)
         kept, sent = chunk_tiles(relays, pattern, near, whole, held, *earlier)
-        mine = add_coded(half, kept, lax.ppermute(sent, "aux", flipped(layers, 1)))
+        mine = add_coded(half, kept, lax.ppermute(sent, "aux", flipped(layers, 1)), *summed)
         earlier = (mine,)
         mask = 2
         while mask < layers:
             mine = add_coded(half, mine, lax.ppermute(mine, "aux", flipped(layers, mask)))
             mask *= 2
+        summed = (mine,)
         coded += [mine, lax.ppermute(mine, "aux", flipped(layers, 1))]
     return final_tiles((blocks, slots, width, width), coded)
 

time: 73 us -> 71.6 us (0.981)
  waiting for transfers between devices: 37.5 us -> 32.5 us
  starting transfers between devices: 23.4 us -> 27 us
    ppermute x2, waiting for transfers between devices: 6.57 us -> 3.34 us  [body(): lax.ppermute(mine, 'aux', flipped(layers, mask))]
    ppermute x1, waiting for transfers between devices: 11.5 us -> 8.41 us  [body(): lax.ppermute(lax.ppermute(late, 'bas', there), 'bas', onward)]
    ppermute x2, starting transfers between devices: 0.58 us -> 3.62 us  [body(): coded += [mine, lax.ppermute(mine, 'aux', flipped(layers, 1))]]
    ppermute x2, waiting for transfers between devices: 1.41 us -> 3.89 us  [body(): lax.ppermute(sent, 'aux', flipped(layers, 1))]
    ppermute x2, waiting for transfers between devices: 4.94 us -> 3.76 us  [body(): coded += [mine, lax.ppermute(mine, 'aux', flipped(layers, 1))]]
  transfers between devices with their start and end apart: 14 -> 14, of which waited for: 7 -> 6; matrix products, arithmetic and copies ran while one was open for 1% -> 1% of each run, Pallas kernels for 6% -> 7%
where the time goes in v4:
time: 71.6 us; the launch traced here: 71.3 us
  waiting for transfers between devices  32.5 us (45%)
  starting transfers between devices  27 us (38%)
  Pallas kernels  7.97 us (11%)
  local copies, waits for them, and re-layouts  3.7 us (5%)
    ppermute x1, waiting for transfers between devices, body(): lax.ppermute(late, 'bas', there)  13 us
    ppermute x1, waiting for transfers between devices, body(): lax.ppermute(lax.ppermute(late, 'bas', there), 'bas', onward)  8.41 us
    ppermute x2, starting transfers between devices, body(): beside = [lax.ppermute(piece, 'bas', chip) for piece in whole]  6.79 us
    ppermute x2, starting transfers between devices, body(): lax.ppermute(mine, 'aux', flipped(layers, mask))  6.2 us
    ppermute x2, starting transfers between devices, body(): lax.ppermute(sent, 'aux', flipped(layers, 1))  5.17 us
    ppermute x2, waiting for transfers between devices, body(): lax.ppermute(sent, 'aux', flipped(layers, 1))  3.89 us
    ppermute x2, waiting for transfers between devices, body(): coded += [mine, lax.ppermute(mine, 'aux', flipped(layers, 1))]  3.76 us
    ppermute x2, starting transfers between devices, body(): coded += [mine, lax.ppermute(mine, 'aux', flipped(layers, 1))]  3.62 us
  transfers between devices with their start and end apart: 14, of which 6 were waited for; matrix products, arithmetic and copies ran while one was open for 1% of the time, Pallas kernels for 7%

profile of v4, /device:TPU:0, one launch (start us, length us, event | category | flops | bytes accessed | tf_op | source)
XLA Modules:
  0.0 71.3 jit_solution(10989050515047249416)
XLA Ops:
  1.1 0.8 %copy.5 = s32[32,3]{1,0:T(8,128)S(1)} copy(s32[32,3]{0,1:T(4,128)} %param.5) | data formatting | bytes 768 | tf_op args[2]
  2.0 1.9 %copy-done = bf16[8,4,3,128,128]{4,3,2,1,0:T(8,128)(2,1)S(1)} copy-done((bf16[8,4,3,128,128]{4,3,2,1,0:T(8,128)(2,1)S(1)}, bf16[8,4,3,128,128]{4,3,2,1,0:T(8,128)(2,1)}, u32[]{:S(2)}) %copy-start) | copy-done | bytes 3145752
  3.9 0.9 %copy-done.1 = bf16[512,256]{1,0:T(8,128)(2,1)S(1)} copy-done((bf16[512,256]{1,0:T(8,128)(2,1)S(1)}, bf16[512,256]{1,0:T(8,128)(2,1)}, u32[]{:S(2)}) %copy-start.1) | copy-done | bytes 262168
  5.1 1.8 %shard_map.38 = (bf16[4,64,2048]{2,1,0:T(8,128)(2,1)S(1)}, bf16[4,64,2048]{2,1,0:T(8,128)(2,1)S(1)}, bf16[4,128,1024]{2,1,0:T(8,128)(2,1)S(1)}, bf16[4,128,1024]{2,1,0:T(8,128)(2,1)S(1)}) custom-call(s32[96]{0:T(128)S(1)} %reshape.3.pattern, bf16[512,256]{1,0:T(8,128)(2,1)S(1)} %get-tuple-element.15.own, bf16[512,256]{1,0:T(8,128)(2,1)S(1)} %collective-permute-done.beside, ...), custom_call_target="tpu_custom_call" | custom-call | tf_op jit(solution)/shard_map/pallas_call | solution.py:79
  6.9 1.3 %collective-permute-start.9 = (bf16[4,64,2048]{2,1,0:T(8,128)(2,1)S(1)}, bf16[4,64,2048]{2,1,0:T(8,128)(2,1)S(1)}, u32[]{:S(2)}, u32[]{:S(2)}) collective-permute-start(bf16[4,64,2048]{2,1,0:T(8,128)(2,1)S(1)} %get-tuple-element.22), channel_id=1, source_target_pairs={{3,7},{4,0},{11,15},{12,8},{19,23},{20,16},{27,31},{28,24}} | collective-permute-start | bytes 3145736 | tf_op jit(solution)/shard_map/ppermute | solution.py:301
  9.0 6.7 %collective-permute-start.2 = (bf16[4,128,1024]{2,1,0:T(8,128)(2,1)S(1)}, bf16[4,128,1024]{2,1,0:T(8,128)(2,1)S(1)}, u32[]{:S(2)}, u32[]{:S(2)}) collective-permute-start(bf16[4,128,1024]{2,1,0:T(8,128)(2,1)S(1)} %get-tuple-element.17.refs_0_), channel_id=1, source_target_pairs={{0,1},{1,0},{2,3},{3,2},{4,5},{5,4},{6,7},{7,6},{8,9},{9,8},{10,11... | collective-permute-start | bytes 3145736 | tf_op jit(solution)/shard_map/ppermute | solution.py:302
  16.5 13.0 %collective-permute-done.9 = bf16[4,64,2048]{2,1,0:T(8,128)(2,1)S(1)} collective-permute-done((bf16[4,64,2048]{2,1,0:T(8,128)(2,1)S(1)}, bf16[4,64,2048]{2,1,0:T(8,128)(2,1)S(1)}, u32[]{:S(2)}, u32[]{:S(2)}) %collective-permute-start.9) | collective-permute-done | bytes 1048608 | tf_op jit(solution)/shard_map/ppermute | solution.py:301
  29.5 1.3 %collective-permute-start.10 = (bf16[4,64,2048]{2,1,0:T(8,128)(2,1)S(1)}, bf16[4,64,2048]{2,1,0:T(8,128)(2,1)S(1)}, u32[]{:S(2)}, u32[]{:S(2)}) collective-permute-start(bf16[4,64,2048]{2,1,0:T(8,128)(2,1)S(1)} %collective-permute-done.9), channel_id=1, source_target_pairs={{7,4},{0,3},{15,12},{8,11},{23,20},{16,19},{31,28},{24,27}} | collective-permute-start | bytes 3145736 | tf_op jit(solution)/shard_map/ppermute | solution.py:301
  30.9 1.3 %shard_map.40.near = f32[512,512]{1,0:T(8,128)S(1)} custom-call(bf16[4,128,1024]{2,1,0:T(8,128)(2,1)S(1)} %get-tuple-element.17.refs_0_, bf16[4,128,1024]{2,1,0:T(8,128)(2,1)S(1)} %get-tuple-element.18.refs_1_, bf16[4,128,1024]{2,1,0:T(8,128)(2,1)S(1)} %collective-permute-done.2.refs_2_, bf16[4,128,1024]{2,1,0:T(8,128)(2,1)S(1)} %collective-permute-done.3.refs_3_, ...), custom_call_target="tpu_custom_call" | custom-call | tf_op jit(solution)/shard_map/pallas_call | solution.py:134
  32.2 1.0 %shard_map.41 = (f32[384,128]{1,0:T(8,128)S(1)}, s16[400,128]{1,0:T(8,128)(2,1)S(1)}) custom-call(s32[96]{0:T(128)S(1)} %reshape.3.pattern, f32[512,512]{1,0:T(8,128)S(1)} %shard_map.40.near, bf16[4,128,1024]{2,1,0:T(8,128)(2,1)S(1)} %get-tuple-element.17.refs_0_, bf16[4,128,1024]{2,1,0:T(8,128)(2,1)S(1)} %get-tuple-element.18.refs_1_, ...), custom_call_target="tpu_custom_call" | custom-call | tf_op jit(solution)/shard_map/pallas_call | solution.py:200
  33.2 2.3 %collective-permute-start.5 = (s16[400,128]{1,0:T(8,128)(2,1)S(1)}, s16[400,128]{1,0:T(8,128)(2,1)S(1)}, u32[]{:S(2)}, u32[]{:S(2)}) collective-permute-start(s16[400,128]{1,0:T(8,128)(2,1)S(1)} %get-tuple-element.21), channel_id=1, source_target_pairs={{0,8},{8,0},{16,24},{24,16},{1,9},{9,1},{17,25},{25,17},{2,10},{10... | collective-permute-start | bytes 307208 | tf_op jit(solution)/shard_map/ppermute | solution.py:308
  35.5 1.3 %shard_map.44.near = f32[512,512]{1,0:T(8,128)S(1)} custom-call(bf16[4,128,1024]{2,1,0:T(8,128)(2,1)S(1)} %get-tuple-element.17.refs_0_, bf16[4,128,1024]{2,1,0:T(8,128)(2,1)S(1)} %get-tuple-element.18.refs_1_, bf16[4,128,1024]{2,1,0:T(8,128)(2,1)S(1)} %collective-permute-done.2.refs_2_, bf16[4,128,1024]{2,1,0:T(8,128)(2,1)S(1)} %collective-permute-done.3.refs_3_, ...), custom_call_target="tpu_custom_call" | custom-call | tf_op jit(solution)/shard_map/pallas_call | solution.py:134
  36.7 1.4 %collective-permute-done.5.other = s16[400,128]{1,0:T(8,128)(2,1)S(1)} collective-permute-done((s16[400,128]{1,0:T(8,128)(2,1)S(1)}, s16[400,128]{1,0:T(8,128)(2,1)S(1)}, u32[]{:S(2)}, u32[]{:S(2)}) %collective-permute-start.5) | collective-permute-done | bytes 102432 | tf_op jit(solution)/shard_map/ppermute | solution.py:308
  38.2 3.1 %collective-permute-start.6 = (s16[400,128]{1,0:T(8,128)(2,1)S(1)}, s16[400,128]{1,0:T(8,128)(2,1)S(1)}, u32[]{:S(2)}, u32[]{:S(2)}) collective-permute-start(s16[400,128]{1,0:T(8,128)(2,1)S(1)} %shard_map.42.mine.refs_4_), channel_id=1, source_target_pairs={{0,16},{8,24},{16,0},{24,8},{1,17},{9,25},{17,1},{25,9},{2,18},{10... | collective-permute-start | bytes 307208 | tf_op jit(solution)/shard_map/ppermute | solution.py:312
  41.3 8.4 %collective-permute-done.10.refs_3_ = bf16[4,64,2048]{2,1,0:T(8,128)(2,1)S(1)} collective-permute-done((bf16[4,64,2048]{2,1,0:T(8,128)(2,1)S(1)}, bf16[4,64,2048]{2,1,0:T(8,128)(2,1)S(1)}, u32[]{:S(2)}, u32[]{:S(2)}) %collective-permute-start.10) | collective-permute-done | bytes 1048608 | tf_op jit(solution)/shard_map/ppermute | solution.py:301
  49.7 1.0 %shard_map.45 = (f32[384,128]{1,0:T(8,128)S(1)}, s16[400,128]{1,0:T(8,128)(2,1)S(1)}) custom-call(s32[96]{0:T(128)S(1)} %reshape.3.pattern, f32[512,512]{1,0:T(8,128)S(1)} %shard_map.44.near, bf16[4,128,1024]{2,1,0:T(8,128)(2,1)S(1)} %get-tuple-element.17.refs_0_, bf16[4,128,1024]{2,1,0:T(8,128)(2,1)S(1)} %get-tuple-element.18.refs_1_, ...), custom_call_target="tpu_custom_call" | custom-call | tf_op jit(solution)/shard_map/pallas_call | solution.py:200
  50.7 2.9 %collective-permute-start.11 = (s16[400,128]{1,0:T(8,128)(2,1)S(1)}, s16[400,128]{1,0:T(8,128)(2,1)S(1)}, u32[]{:S(2)}, u32[]{:S(2)}) collective-permute-start(s16[400,128]{1,0:T(8,128)(2,1)S(1)} %get-tuple-element.24), channel_id=1, source_target_pairs={{0,8},{8,0},{16,24},{24,16},{1,9},{9,1},{17,25},{25,17},{2,10},{10... | collective-permute-start | bytes 307208 | tf_op jit(solution)/shard_map/ppermute | solution.py:308
  53.7 2.5 %collective-permute-done.11.other = s16[400,128]{1,0:T(8,128)(2,1)S(1)} collective-permute-done((s16[400,128]{1,0:T(8,128)(2,1)S(1)}, s16[400,128]{1,0:T(8,128)(2,1)S(1)}, u32[]{:S(2)}, u32[]{:S(2)}) %collective-permute-start.11) | collective-permute-done | bytes 102432 | tf_op jit(solution)/shard_map/ppermute | solution.py:308
  56.3 3.1 %collective-permute-start.12 = (s16[400,128]{1,0:T(8,128)(2,1)S(1)}, s16[400,128]{1,0:T(8,128)(2,1)S(1)}, u32[]{:S(2)}, u32[]{:S(2)}) collective-permute-start(s16[400,128]{1,0:T(8,128)(2,1)S(1)} %shard_map.46.mine), channel_id=1, source_target_pairs={{0,16},{8,24},{16,0},{24,8},{1,17},{9,25},{17,1},{25,9},{2,18},{10... | collective-permute-start | bytes 307208 | tf_op jit(solution)/shard_map/ppermute | solution.py:312
  59.4 1.6 %collective-permute-start.7 = (s16[400,128]{1,0:T(8,128)(2,1)S(1)}, s16[400,128]{1,0:T(8,128)(2,1)S(1)}, u32[]{:S(2)}, u32[]{:S(2)}) collective-permute-start(s16[400,128]{1,0:T(8,128)(2,1)S(1)} %shard_map.43.rest_0_.refs_0_), channel_id=1, source_target_pairs={{0,8},{8,0},{16,24},{24,16},{1,9},{9,1},{17,25},{25,17},{2,10},{10... | collective-permute-start | bytes 307208 | tf_op jit(solution)/shard_map/ppermute | solution.py:315
  61.0 3.3 %collective-permute-done.12.other = s16[400,128]{1,0:T(8,128)(2,1)S(1)} collective-permute-done((s16[400,128]{1,0:T(8,128)(2,1)S(1)}, s16[400,128]{1,0:T(8,128)(2,1)S(1)}, u32[]{:S(2)}, u32[]{:S(2)}) %collective-permute-start.12) | collective-permute-done | bytes 102432 | tf_op jit(solution)/shard_map/ppermute | solution.py:312
  64.4 2.0 %collective-permute-start.13 = (s16[400,128]{1,0:T(8,128)(2,1)S(1)}, s16[400,128]{1,0:T(8,128)(2,1)S(1)}, u32[]{:S(2)}, u32[]{:S(2)}) collective-permute-start(s16[400,128]{1,0:T(8,128)(2,1)S(1)} %shard_map.47.refs_2_), channel_id=1, source_target_pairs={{0,8},{8,0},{16,24},{24,16},{1,9},{9,1},{17,25},{25,17},{2,10},{10... | collective-permute-start | bytes 307208 | tf_op jit(solution)/shard_map/ppermute | solution.py:315
  66.4 3.8 %collective-permute-done.13.refs_3_ = s16[400,128]{1,0:T(8,128)(2,1)S(1)} collective-permute-done((s16[400,128]{1,0:T(8,128)(2,1)S(1)}, s16[400,128]{1,0:T(8,128)(2,1)S(1)}, u32[]{:S(2)}, u32[]{:S(2)}) %collective-permute-start.13) | collective-permute-done | bytes 102432 | tf_op jit(solution)/shard_map/ppermute | solution.py:315
  70.2 1.1 %shard_map.48 = f32[4,3,128,128]{3,2,1,0:T(8,128)} custom-call(s16[400,128]{1,0:T(8,128)(2,1)S(1)} %shard_map.43.rest_0_.refs_0_, s16[400,128]{1,0:T(8,128)(2,1)S(1)} %collective-permute-done.7.refs_1_, s16[400,128]{1,0:T(8,128)(2,1)S(1)} %shard_map.47.refs_2_, s16[400,128]{1,0:T(8,128)(2,1)S(1)} %collective-permute-done.13.refs_3_), custom_call_target="tpu_custom_call" | custom-call | tf_op jit(solution)/shard_map/pallas_call | solution.py:264
  (22 shorter events, 3.4 us)
Async XLA Ops:
  0.0 5.1 %collective-permute-start = (bf16[512,256]{1,0:T(8,128)(2,1)}, bf16[512,256]{1,0:T(8,128)(2,1)S(1)}, u32[]{:S(2)}, u32[]{:S(2)}) collective-permute-start(bf16[512,256]{1,0:T(8,128)(2,1)} %own.1), channel_id=1, source_target_pairs={{0,1},{1,0},{2,3},{3,2},{4,5},{5,4},{6,7},{7,6},{8,9},{9,8},{10,11... | collective-permute-start | bytes 786440 | tf_op jit(solution)/shard_map/ppermute | solution.py:294
  0.5 4.7 %collective-permute-start.1 = (bf16[512,256]{1,0:T(8,128)(2,1)}, bf16[512,256]{1,0:T(8,128)(2,1)S(1)}, u32[]{:S(2)}, u32[]{:S(2)}) collective-permute-start(bf16[512,256]{1,0:T(8,128)(2,1)} %own.1), channel_id=1, source_target_pairs={{1,2},{2,1},{3,4},{4,3},{5,6},{6,5},{9,10},{10,9},{11,12},{12,11},... | collective-permute-start | bytes 786440 | tf_op jit(solution)/shard_map/ppermute | solution.py:293
  2.0 1.9 %copy-start = (bf16[8,4,3,128,128]{4,3,2,1,0:T(8,128)(2,1)S(1)}, bf16[8,4,3,128,128]{4,3,2,1,0:T(8,128)(2,1)}, u32[]{:S(2)}) copy-start(bf16[8,4,3,128,128]{4,3,2,1,0:T(8,128)(2,1)} %tensor.1) | copy-start | bytes 9437188
  3.9 0.9 %copy-start.1 = (bf16[512,256]{1,0:T(8,128)(2,1)S(1)}, bf16[512,256]{1,0:T(8,128)(2,1)}, u32[]{:S(2)}) copy-start(bf16[512,256]{1,0:T(8,128)(2,1)} %own.1) | copy-start | bytes 786436
  6.9 22.6 %collective-permute-start.9 = (bf16[4,64,2048]{2,1,0:T(8,128)(2,1)S(1)}, bf16[4,64,2048]{2,1,0:T(8,128)(2,1)S(1)}, u32[]{:S(2)}, u32[]{:S(2)}) collective-permute-start(bf16[4,64,2048]{2,1,0:T(8,128)(2,1)S(1)} %get-tuple-element.22), channel_id=1, source_target_pairs={{3,7},{4,0},{11,15},{12,8},{19,23},{20,16},{27,31},{28,24}} | collective-permute-start | bytes 3145736 | tf_op jit(solution)/shard_map/ppermute | solution.py:301
  8.2 22.7 %collective-permute-start.4 = (bf16[4,64,2048]{2,1,0:T(8,128)(2,1)S(1)}, bf16[4,64,2048]{2,1,0:T(8,128)(2,1)S(1)}, u32[]{:S(2)}, u32[]{:S(2)}) collective-permute-start(bf16[4,64,2048]{2,1,0:T(8,128)(2,1)S(1)} %get-tuple-element.19), channel_id=1, source_target_pairs={{1,2},{2,1},{3,4},{4,3},{5,6},{6,5},{9,10},{10,9},{11,12},{12,11},... | collective-permute-start | bytes 3145736 | tf_op jit(solution)/shard_map/ppermute | solution.py:299
  9.0 21.9 %collective-permute-start.2 = (bf16[4,128,1024]{2,1,0:T(8,128)(2,1)S(1)}, bf16[4,128,1024]{2,1,0:T(8,128)(2,1)S(1)}, u32[]{:S(2)}, u32[]{:S(2)}) collective-permute-start(bf16[4,128,1024]{2,1,0:T(8,128)(2,1)S(1)} %get-tuple-element.17.refs_0_), channel_id=1, source_target_pairs={{0,1},{1,0},{2,3},{3,2},{4,5},{5,4},{6,7},{7,6},{8,9},{9,8},{10,11... | collective-permute-start | bytes 3145736 | tf_op jit(solution)/shard_map/ppermute | solution.py:302
  15.7 15.2 %collective-permute-start.3 = (bf16[4,128,1024]{2,1,0:T(8,128)(2,1)S(1)}, bf16[4,128,1024]{2,1,0:T(8,128)(2,1)S(1)}, u32[]{:S(2)}, u32[]{:S(2)}) collective-permute-start(bf16[4,128,1024]{2,1,0:T(8,128)(2,1)S(1)} %get-tuple-element.18.refs_1_), channel_id=1, source_target_pairs={{0,1},{1,0},{2,3},{3,2},{4,5},{5,4},{6,7},{7,6},{8,9},{9,8},{10,11... | collective-permute-start | bytes 3145736 | tf_op jit(solution)/shard_map/ppermute | solution.py:302
  15.8 25.5 %collective-permute-start.8 = (bf16[4,64,2048]{2,1,0:T(8,128)(2,1)S(1)}, bf16[4,64,2048]{2,1,0:T(8,128)(2,1)S(1)}, u32[]{:S(2)}, u32[]{:S(2)}) collective-permute-start(bf16[4,64,2048]{2,1,0:T(8,128)(2,1)S(1)} %get-tuple-element.22), channel_id=1, source_target_pairs={{1,2},{2,1},{5,6},{6,5},{9,10},{10,9},{13,14},{14,13},{17,18},{18,... | collective-permute-start | bytes 3145736 | tf_op jit(solution)/shard_map/ppermute | solution.py:299
  29.5 20.2 %collective-permute-start.10 = (bf16[4,64,2048]{2,1,0:T(8,128)(2,1)S(1)}, bf16[4,64,2048]{2,1,0:T(8,128)(2,1)S(1)}, u32[]{:S(2)}, u32[]{:S(2)}) collective-permute-start(bf16[4,64,2048]{2,1,0:T(8,128)(2,1)S(1)} %collective-permute-done.9), channel_id=1, source_target_pairs={{7,4},{0,3},{15,12},{8,11},{23,20},{16,19},{31,28},{24,27}} | collective-permute-start | bytes 3145736 | tf_op jit(solution)/shard_map/ppermute | solution.py:301
  33.2 4.9 %collective-permute-start.5 = (s16[400,128]{1,0:T(8,128)(2,1)S(1)}, s16[400,128]{1,0:T(8,128)(2,1)S(1)}, u32[]{:S(2)}, u32[]{:S(2)}) collective-permute-start(s16[400,128]{1,0:T(8,128)(2,1)S(1)} %get-tuple-element.21), channel_id=1, source_target_pairs={{0,8},{8,0},{16,24},{24,16},{1,9},{9,1},{17,25},{25,17},{2,10},{10... | collective-permute-start | bytes 307208 | tf_op jit(solution)/shard_map/ppermute | solution.py:308
  38.2 15.4 %collective-permute-start.6 = (s16[400,128]{1,0:T(8,128)(2,1)S(1)}, s16[400,128]{1,0:T(8,128)(2,1)S(1)}, u32[]{:S(2)}, u32[]{:S(2)}) collective-permute-start(s16[400,128]{1,0:T(8,128)(2,1)S(1)} %shard_map.42.mine.refs_4_), channel_id=1, source_target_pairs={{0,16},{8,24},{16,0},{24,8},{1,17},{9,25},{17,1},{25,9},{2,18},{10... | collective-permute-start | bytes 307208 | tf_op jit(solution)/shard_map/ppermute | solution.py:312
  50.7 5.5 %collective-permute-start.11 = (s16[400,128]{1,0:T(8,128)(2,1)S(1)}, s16[400,128]{1,0:T(8,128)(2,1)S(1)}, u32[]{:S(2)}, u32[]{:S(2)}) collective-permute-start(s16[400,128]{1,0:T(8,128)(2,1)S(1)} %get-tuple-element.24), channel_id=1, source_target_pairs={{0,8},{8,0},{16,24},{24,16},{1,9},{9,1},{17,25},{25,17},{2,10},{10... | collective-permute-start | bytes 307208 | tf_op jit(solution)/shard_map/ppermute | solution.py:308
  56.3 8.0 %collective-permute-start.12 = (s16[400,128]{1,0:T(8,128)(2,1)S(1)}, s16[400,128]{1,0:T(8,128)(2,1)S(1)}, u32[]{:S(2)}, u32[]{:S(2)}) collective-permute-start(s16[400,128]{1,0:T(8,128)(2,1)S(1)} %shard_map.46.mine), channel_id=1, source_target_pairs={{0,16},{8,24},{16,0},{24,8},{1,17},{9,25},{17,1},{25,9},{2,18},{10... | collective-permute-start | bytes 307208 | tf_op jit(solution)/shard_map/ppermute | solution.py:312
  59.4 7.1 %collective-permute-start.7 = (s16[400,128]{1,0:T(8,128)(2,1)S(1)}, s16[400,128]{1,0:T(8,128)(2,1)S(1)}, u32[]{:S(2)}, u32[]{:S(2)}) collective-permute-start(s16[400,128]{1,0:T(8,128)(2,1)S(1)} %shard_map.43.rest_0_.refs_0_), channel_id=1, source_target_pairs={{0,8},{8,0},{16,24},{24,16},{1,9},{9,1},{17,25},{25,17},{2,10},{10... | collective-permute-start | bytes 307208 | tf_op jit(solution)/shard_map/ppermute | solution.py:315
  64.4 5.8 %collective-permute-start.13 = (s16[400,128]{1,0:T(8,128)(2,1)S(1)}, s16[400,128]{1,0:T(8,128)(2,1)S(1)}, u32[]{:S(2)}, u32[]{:S(2)}) collective-permute-start(s16[400,128]{1,0:T(8,128)(2,1)S(1)} %shard_map.47.refs_2_), channel_id=1, source_target_pairs={{0,8},{8,0},{16,24},{24,16},{1,9},{9,1},{17,25},{25,17},{2,10},{10... | collective-permute-start | bytes 307208 | tf_op jit(solution)/shard_map/ppermute | solution.py:315

commit v5 on v4

--- a/solution.py
+++ b/solution.py
@@ -47,7 +47,7 @@
     )(*arrays)
 
 
-def half_kernel(cuts, pattern, own, beside, across, tensor, *outs):
+def half_kernel(cuts, pattern, own, across, beside, tensor, *outs):
     parts, pieces = outs[: len(cuts) - 1], outs[len(cuts) - 1 :]
     aux, blocks, slots, width, _ = tensor.shape
     occupied = own.shape[1]
@@ -83,7 +83,7 @@
         out_specs=[VMEM] * len(shapes),
         compiler_params=params(24),
         cost_estimate=NO_COST,
-    )(pattern, own, beside, across, tensor)
+    )(pattern, own, across, beside, tensor)
     return outs[:-PIECES], outs[-PIECES:]
 
 
@@ -122,23 +122,21 @@
     return total
 
 
-def near_kernel(start, stop, *refs):
-    whole, beside, product = refs[:PIECES], refs[PIECES : 2 * PIECES], refs[-1]
-    half = product.shape[0] // 2
-    product[:half, :] = times(lambda k: whole[k][:, start:stop, :], whole)
-    product[half:, :] = times(lambda k: beside[k][:, start:stop, :], whole)
-
-
-def near_products(start, stop, whole, beside, *earlier):
+def product_kernel(start, stop, *refs):
+    rows, whole, product = refs[:PIECES], refs[PIECES : 2 * PIECES], refs[-1]
+    product[...] = times(lambda k: rows[k][:, start:stop, :], whole)
+
+
+def products(start, stop, rows, whole, *earlier):
     blocks, width, _ = whole[0].shape
     return pl.pallas_call(
-        functools.partial(near_kernel, start, stop),
-        out_shape=jax.ShapeDtypeStruct((2 * blocks * (stop - start), blocks * width), jnp.float32),
+        functools.partial(product_kernel, start, stop),
+        out_shape=jax.ShapeDtypeStruct((blocks * (stop - start), blocks * width), jnp.float32),
         in_specs=[VMEM] * (2 * PIECES) + [ANY] * len(earlier),
         out_specs=VMEM,
         compiler_params=params(24),
         cost_estimate=NO_COST,
-    )(*whole, *beside, *earlier)
+    )(*rows, *whole, *earlier)
 
 
 def gate_kernel(_, out):
@@ -156,8 +154,9 @@
     )(earlier)
 
 
-def tile_kernel(relays, count, pattern, near, *refs):
-    whole, across, (kept, sent, far, scales, places, sem) = refs[:PIECES], refs[PIECES : PIECES + count], refs[-6:]
+def tile_kernel(relays, count, start, pattern, own, *refs):
+    across, whole, near = refs[:count], refs[count : count + PIECES], refs[count + PIECES : -7]
+    kept, sent, far, close, scales, places, sem = refs[-7:]
     blocks, width, depth = whole[0].shape
     rows = across[0].shape[1]
     slots = pattern.shape[0] // (blocks * lax.axis_size("bas"))
@@ -175,17 +174,19 @@
         pl.when(jnp.logical_not(relayed))(lambda: multiply(across[0]))
     else:
         multiply(across[0])
+    if start is None:
+        close = near[0]
+    else:
+        close[...] = times(lambda k: near[k][:, start : start + rows, :], whole)
     copy.wait()
 
     def tile(t, parity):
         m = parity * (blocks // 2) + t // slots
         place = places[(device * blocks + m) * slots + t % slots]
         group, block = place // blocks, jnp.maximum(place, 0) % blocks
-        columns = pl.ds(pl.multiple_of(m * width, width), width)
-        close = block + jnp.where(group == device, 0, blocks)
-        inside = near[pl.ds(pl.multiple_of(close * rows, rows), rows), columns]
-        outside = far[pl.ds(pl.multiple_of(block * rows, rows), rows), columns]
-        value = jnp.where((group == device) | (group == device ^ 1), inside, outside)
+        part = pl.ds(pl.multiple_of(block * rows, rows), rows), pl.ds(pl.multiple_of(m * width, width), width)
+        value = jnp.where(group == device ^ 1, close[part], far[part])
+        value = jnp.where(group == device, own[part], value)
         return jnp.where(place < 0, 0.0, value)
 
     for t in range(half):
@@ -193,27 +194,34 @@
     encode([tile(t, 1 - layer % 2) for t in range(half)], sent, scales)
 
 
-def chunk_tiles(relays, pattern, near, whole, across, *earlier):
+def chunk_tiles(relays, start, pattern, own, across, whole, near, *earlier):
     blocks, width, _ = whole[0].shape
     rows, slots = across[0].shape[1], pattern.shape[0] // (blocks * lax.axis_size("bas"))
     half = blocks * slots // 2
-    return pl.pallas_call(
-        functools.partial(tile_kernel, relays, len(across)),
+    product = (blocks * rows, blocks * width)
+
+    def kernel(*refs):
+        given = 2 + len(across) + len(whole) + len(near)
+        tile_kernel(relays, len(across), start, *refs[:given], *refs[given + len(earlier) :])
+
+    return pl.pallas_call(
+        kernel,
         out_shape=[
             jax.ShapeDtypeStruct((half * rows, width), jnp.float32),
             jax.ShapeDtypeStruct((half * rows + SCALE_ROWS, width), jnp.int16),
         ],
-        in_specs=[ANY] + [VMEM] * (1 + PIECES + len(across)) + [ANY] * len(earlier),
+        in_specs=[ANY] + [VMEM] * (1 + len(across) + len(whole) + len(near)) + [ANY] * len(earlier),
         out_specs=[VMEM] * 2,
         scratch_shapes=[
-            pltpu.VMEM((blocks * rows, blocks * width), jnp.float32),
+            pltpu.VMEM(product, jnp.float32),
+            pltpu.VMEM((8, 128) if start is None else product, jnp.float32),
             pltpu.VMEM((SCALE_ROWS, width), jnp.float32),
             pltpu.SMEM(pattern.shape, pattern.dtype),
             pltpu.SemaphoreType.DMA,
         ],
         compiler_params=params(24),
         cost_estimate=NO_COST,
-    )(pattern, near, *whole, *across, *earlier)
+    )(pattern, own, *across, *whole, *near, *earlier)
 
 
 def add_kernel(count, mine, other, *rest):
@@ -295,16 +303,23 @@
     tensor, coefficients = fetch(tensor, coefficients)
     cuts = (0, CUT, width)
     pattern = pattern.reshape(-1)
-    (early, late), whole = half_forms(cuts, pattern, coefficients, beside, beyond, tensor)
-    arrived = [[lax.ppermute(early, "bas", across)], [lax.ppermute(late, "bas", direct)]]
+    (early, *late), whole = half_forms(cuts, pattern, coefficients, beside, beyond, tensor)
+    arrived = [[lax.ppermute(early, "bas", across)]] + [[lax.ppermute(part, "bas", direct)] for part in late]
     if detours:
-        arrived[1].append(lax.ppermute(lax.ppermute(late, "bas", there), "bas", onward))
+        halfway = [lax.ppermute(part, "bas", there) for part in late]
+        for held, part in zip(arrived[1:], halfway):
+            held.append(lax.ppermute(part, "bas", onward))
     beside = [lax.ppermute(piece, "bas", chip) for piece in whole]
     half = blocks * slots // 2
-    coded, earlier, summed, opened = [], (), (), gate(arrived[0][0])
-    for start, stop, held in zip(cuts, cuts[1:], arrived):
-        near = near_products(start, stop, whole, beside, opened)
-        kept, sent = chunk_tiles(relays, pattern, near, whole, held, *earlier)
+    opened = gate(arrived[0][0])
+    owned = [products(a, b, whole, whole, halfway[-1] if detours else opened) for a, b in zip(cuts, cuts[1:])]
+    coded, earlier, summed = [], (opened,), ()
+    for start, stop, own, held in zip(cuts, cuts[1:], owned, arrived):
+        if start == 0:
+            kept, sent = chunk_tiles(relays, 0, pattern, own, held, whole, beside, *earlier)
+        else:
+            near = products(start, stop, beside, whole, opened)
+            kept, sent = chunk_tiles(relays, None, pattern, own, held, whole, [near], *earlier)
         mine = add_coded(half, kept, lax.ppermute(sent, "aux", flipped(layers, 1)), *summed)
         earlier = (mine,)
         mask = 2

time: 71.6 us -> 70.7 us (0.987)
  starting transfers between devices: 27 us -> 23.1 us
  waiting for transfers between devices: 32.5 us -> 35.1 us
    ppermute x1, starting transfers between devices: 0.45 us -> 4.35 us  [body(): beside = lax.ppermute(coefficients, 'bas', chip)]
    ppermute x2, starting transfers between devices: 6.79 us -> 2.89 us  [body(): beside = [lax.ppermute(piece, 'bas', chip) for piece in whole]]
    ppermute x2, starting transfers between devices: 5.17 us -> 3.29 us  [body(): lax.ppermute(sent, 'aux', flipped(layers, 1))]
    ppermute x2, starting transfers between devices: 3.62 us -> 2.56 us  [body(): coded += [mine, lax.ppermute(mine, 'aux', flipped(layers, 1))]]
    ppermute x2, waiting for transfers between devices: 3.34 us -> 4.39 us  [body(): lax.ppermute(mine, 'aux', flipped(layers, mask))]
    ppermute x2, starting transfers between devices: 6.2 us -> 5.3 us  [body(): lax.ppermute(mine, 'aux', flipped(layers, mask))]
    pallas_call x4 -> x5, Pallas kernels: 4.45 us -> 4.7 us  [the longest x2 2.5 us: chunk_tiles(): pl.pallas_call(kernel, out_shape=[jax.ShapeDtypeStruct((half * rows, widt...]
where the time goes in v5:
time: 70.7 us; the launch traced here: 70.4 us
  waiting for transfers between devices  35.1 us (50%)
  starting transfers between devices  23.1 us (33%)
  Pallas kernels  8.22 us (12%)
  local copies, waits for them, and re-layouts  3.7 us (5%)
    ppermute x1, waiting for transfers between devices, body(): halfway = [lax.ppermute(part, 'bas', there) for part in late]  13.1 us
    ppermute x1, waiting for transfers between devices, body(): held.append(lax.ppermute(part, 'bas', onward))  9.03 us
    ppermute x2, starting transfers between devices, body(): lax.ppermute(mine, 'aux', flipped(layers, mask))  5.3 us
    ppermute x2, waiting for transfers between devices, body(): lax.ppermute(sent, 'aux', flipped(layers, 1))  4.57 us
    ppermute x2, waiting for transfers between devices, body(): lax.ppermute(mine, 'aux', flipped(layers, mask))  4.39 us
    ppermute x1, starting transfers between devices, body(): beside = lax.ppermute(coefficients, 'bas', chip)  4.35 us
    ppermute x2, waiting for transfers between devices, body(): coded += [mine, lax.ppermute(mine, 'aux', flipped(layers, 1))]  4.09 us
    unnamed x5, local copies, waits for them, and re-layouts  3.6 us
  transfers between devices with their start and end apart: 14, of which 6 were waited for; matrix products, arithmetic and copies ran while one was open for 1% of the time, Pallas kernels for 7%

profile of v5, /device:TPU:0, one launch (start us, length us, event | category | flops | bytes accessed | tf_op | source)
XLA Modules:
  0.0 70.4 jit_solution(13762550480348421736)
XLA Ops:
  0.7 4.4 %collective-permute-start.1 = (bf16[512,256]{1,0:T(8,128)(2,1)}, bf16[512,256]{1,0:T(8,128)(2,1)S(1)}, u32[]{:S(2)}, u32[]{:S(2)}) collective-permute-start(bf16[512,256]{1,0:T(8,128)(2,1)} %own.1), channel_id=1, source_target_pairs={{0,1},{1,0},{2,3},{3,2},{4,5},{5,4},{6,7},{7,6},{8,9},{9,8},{10,11... | collective-permute-start | bytes 786440 | tf_op jit(solution)/shard_map/ppermute | solution.py:302
  5.0 0.8 %copy.5 = s32[32,3]{1,0:T(8,128)S(1)} copy(s32[32,3]{0,1:T(4,128)} %param.5) | data formatting | bytes 768 | tf_op args[2]
  5.9 1.9 %copy-done = bf16[8,4,3,128,128]{4,3,2,1,0:T(8,128)(2,1)S(1)} copy-done((bf16[8,4,3,128,128]{4,3,2,1,0:T(8,128)(2,1)S(1)}, bf16[8,4,3,128,128]{4,3,2,1,0:T(8,128)(2,1)}, u32[]{:S(2)}) %copy-start) | copy-done | bytes 3145752
  7.8 0.9 %copy-done.1 = bf16[512,256]{1,0:T(8,128)(2,1)S(1)} copy-done((bf16[512,256]{1,0:T(8,128)(2,1)S(1)}, bf16[512,256]{1,0:T(8,128)(2,1)}, u32[]{:S(2)}) %copy-start.1) | copy-done | bytes 262168
  9.0 1.8 %shard_map.38 = (bf16[4,64,2048]{2,1,0:T(8,128)(2,1)S(1)}, bf16[4,64,2048]{2,1,0:T(8,128)(2,1)S(1)}, bf16[4,128,1024]{2,1,0:T(8,128)(2,1)S(1)}, bf16[4,128,1024]{2,1,0:T(8,128)(2,1)S(1)}) custom-call(s32[96]{0:T(128)S(1)} %reshape.3.pattern.refs_0_, bf16[512,256]{1,0:T(8,128)(2,1)S(1)} %get-tuple-element.15.own, ...), custom_call_target="tpu_custom_call" | custom-call | tf_op jit(solution)/shard_map/pallas_call | solution.py:79
  10.8 1.3 %collective-permute-start.2 = (bf16[4,64,2048]{2,1,0:T(8,128)(2,1)S(1)}, bf16[4,64,2048]{2,1,0:T(8,128)(2,1)S(1)}, u32[]{:S(2)}, u32[]{:S(2)}) collective-permute-start(bf16[4,64,2048]{2,1,0:T(8,128)(2,1)S(1)} %get-tuple-element.19), channel_id=1, source_target_pairs={{3,7},{4,0},{11,15},{12,8},{19,23},{20,16},{27,31},{28,24}} | collective-permute-start | bytes 3145736 | tf_op jit(solution)/shard_map/ppermute | solution.py:309
  12.9 2.8 %collective-permute-start.4 = (bf16[4,128,1024]{2,1,0:T(8,128)(2,1)S(1)}, bf16[4,128,1024]{2,1,0:T(8,128)(2,1)S(1)}, u32[]{:S(2)}, u32[]{:S(2)}) collective-permute-start(bf16[4,128,1024]{2,1,0:T(8,128)(2,1)S(1)} %get-tuple-element.17.refs_0_.refs_2_.refs_3_.refs_4_), channel_id=1, source_target_pairs={{0,1},{1,0},{2,3},{3,2},{4,5},{5,4},{6,7},{7,6},{8,9},{9,8},{10,11... | collective-permute-start | bytes 3145736 | tf_op jit(solution)/shard_map/ppermute | solution.py:312
  16.5 13.1 %collective-permute-done.2.refs_4_ = bf16[4,64,2048]{2,1,0:T(8,128)(2,1)S(1)} collective-permute-done((bf16[4,64,2048]{2,1,0:T(8,128)(2,1)S(1)}, bf16[4,64,2048]{2,1,0:T(8,128)(2,1)S(1)}, u32[]{:S(2)}, u32[]{:S(2)}) %collective-permute-start.2) | collective-permute-done | bytes 1048608 | tf_op jit(solution)/shard_map/ppermute | solution.py:309
  29.6 1.3 %collective-permute-start.10 = (bf16[4,64,2048]{2,1,0:T(8,128)(2,1)S(1)}, bf16[4,64,2048]{2,1,0:T(8,128)(2,1)S(1)}, u32[]{:S(2)}, u32[]{:S(2)}) collective-permute-start(bf16[4,64,2048]{2,1,0:T(8,128)(2,1)S(1)} %collective-permute-done.2.refs_4_), channel_id=1, source_target_pairs={{7,4},{0,3},{15,12},{8,11},{23,20},{16,19},{31,28},{24,27}} | collective-permute-start | bytes 3145736 | tf_op jit(solution)/shard_map/ppermute | solution.py:311
  30.9 0.7 %shard_map.39.refs_1_ = f32[256,512]{1,0:T(8,128)S(1)} custom-call(bf16[4,128,1024]{2,1,0:T(8,128)(2,1)S(1)} %get-tuple-element.17.refs_0_.refs_2_.refs_3_.refs_4_, bf16[4,128,1024]{2,1,0:T(8,128)(2,1)S(1)} %get-tuple-element.18.refs_1_.refs_3_.refs_4_.refs_5_, bf16[4,128,1024]{2,1,0:T(8,128)(2,1)S(1)} %get-tuple-element.17.refs_0_.refs_2_.refs_3_.refs_4_, ...), custom_call_target="tpu_custom_call" | custom-call | tf_op jit(solution)/shard_map/pallas_call | solution.py:132
  31.7 1.5 %shard_map.41 = (f32[384,128]{1,0:T(8,128)S(1)}, s16[400,128]{1,0:T(8,128)(2,1)S(1)}) custom-call(s32[96]{0:T(128)S(1)} %reshape.3.pattern.refs_0_, f32[256,512]{1,0:T(8,128)S(1)} %shard_map.39.refs_1_, bf16[4,64,2048]{2,1,0:T(8,128)(2,1)S(1)} %collective-permute-done.3._.refs_2_, ...), custom_call_target="tpu_custom_call" | custom-call | tf_op jit(solution)/shard_map/pallas_call | solution.py:207
  33.2 1.6 %collective-permute-start.6 = (s16[400,128]{1,0:T(8,128)(2,1)S(1)}, s16[400,128]{1,0:T(8,128)(2,1)S(1)}, u32[]{:S(2)}, u32[]{:S(2)}) collective-permute-start(s16[400,128]{1,0:T(8,128)(2,1)S(1)} %get-tuple-element.22), channel_id=1, source_target_pairs={{0,8},{8,0},{16,24},{24,16},{1,9},{9,1},{17,25},{25,17},{2,10},{10... | collective-permute-start | bytes 307208 | tf_op jit(solution)/shard_map/ppermute | solution.py:323
  36.3 1.6 %collective-permute-done.6.other = s16[400,128]{1,0:T(8,128)(2,1)S(1)} collective-permute-done((s16[400,128]{1,0:T(8,128)(2,1)S(1)}, s16[400,128]{1,0:T(8,128)(2,1)S(1)}, u32[]{:S(2)}, u32[]{:S(2)}) %collective-permute-start.6) | collective-permute-done | bytes 102432 | tf_op jit(solution)/shard_map/ppermute | solution.py:323
  38.0 2.6 %collective-permute-start.7 = (s16[400,128]{1,0:T(8,128)(2,1)S(1)}, s16[400,128]{1,0:T(8,128)(2,1)S(1)}, u32[]{:S(2)}, u32[]{:S(2)}) collective-permute-start(s16[400,128]{1,0:T(8,128)(2,1)S(1)} %shard_map.42.mine.refs_7_), channel_id=1, source_target_pairs={{0,16},{8,24},{16,0},{24,8},{1,17},{9,25},{17,1},{25,9},{2,18},{10... | collective-permute-start | bytes 307208 | tf_op jit(solution)/shard_map/ppermute | solution.py:327
  40.7 9.0 %collective-permute-done.10.refs_3_ = bf16[4,64,2048]{2,1,0:T(8,128)(2,1)S(1)} collective-permute-done((bf16[4,64,2048]{2,1,0:T(8,128)(2,1)S(1)}, bf16[4,64,2048]{2,1,0:T(8,128)(2,1)S(1)}, u32[]{:S(2)}, u32[]{:S(2)}) %collective-permute-start.10) | collective-permute-done | bytes 1048608 | tf_op jit(solution)/shard_map/ppermute | solution.py:311
  49.7 1.0 %shard_map.46 = (f32[384,128]{1,0:T(8,128)S(1)}, s16[400,128]{1,0:T(8,128)(2,1)S(1)}) custom-call(s32[96]{0:T(128)S(1)} %reshape.3.pattern.refs_0_, f32[256,512]{1,0:T(8,128)S(1)} %shard_map.44.refs_1_, bf16[4,64,2048]{2,1,0:T(8,128)(2,1)S(1)} %collective-permute-done.9.refs_2_, bf16[4,64,2048]{2,1,0:T(8,128)(2,1)S(1)} %collective-permute-done.10.refs_3_, ...), custom_call_target="tpu_custom_call" | custom-call | tf_op jit(solution)/shard_map/pallas_call | solution.py:207
  50.7 1.7 %collective-permute-start.11 = (s16[400,128]{1,0:T(8,128)(2,1)S(1)}, s16[400,128]{1,0:T(8,128)(2,1)S(1)}, u32[]{:S(2)}, u32[]{:S(2)}) collective-permute-start(s16[400,128]{1,0:T(8,128)(2,1)S(1)} %get-tuple-element.24), channel_id=1, source_target_pairs={{0,8},{8,0},{16,24},{24,16},{1,9},{9,1},{17,25},{25,17},{2,10},{10... | collective-permute-start | bytes 307208 | tf_op jit(solution)/shard_map/ppermute | solution.py:323
  52.5 3.0 %collective-permute-done.11.other = s16[400,128]{1,0:T(8,128)(2,1)S(1)} collective-permute-done((s16[400,128]{1,0:T(8,128)(2,1)S(1)}, s16[400,128]{1,0:T(8,128)(2,1)S(1)}, u32[]{:S(2)}, u32[]{:S(2)}) %collective-permute-start.11) | collective-permute-done | bytes 102432 | tf_op jit(solution)/shard_map/ppermute | solution.py:323
  55.5 2.7 %collective-permute-start.12 = (s16[400,128]{1,0:T(8,128)(2,1)S(1)}, s16[400,128]{1,0:T(8,128)(2,1)S(1)}, u32[]{:S(2)}, u32[]{:S(2)}) collective-permute-start(s16[400,128]{1,0:T(8,128)(2,1)S(1)} %shard_map.47.mine), channel_id=1, source_target_pairs={{0,16},{8,24},{16,0},{24,8},{1,17},{9,25},{17,1},{25,9},{2,18},{10... | collective-permute-start | bytes 307208 | tf_op jit(solution)/shard_map/ppermute | solution.py:327
  58.2 1.6 %collective-permute-start.8 = (s16[400,128]{1,0:T(8,128)(2,1)S(1)}, s16[400,128]{1,0:T(8,128)(2,1)S(1)}, u32[]{:S(2)}, u32[]{:S(2)}) collective-permute-start(s16[400,128]{1,0:T(8,128)(2,1)S(1)} %shard_map.43.rest_0_.refs_0_), channel_id=1, source_target_pairs={{0,8},{8,0},{16,24},{24,16},{1,9},{9,1},{17,25},{25,17},{2,10},{10... | collective-permute-start | bytes 307208 | tf_op jit(solution)/shard_map/ppermute | solution.py:330
  59.7 4.4 %collective-permute-done.12.other = s16[400,128]{1,0:T(8,128)(2,1)S(1)} collective-permute-done((s16[400,128]{1,0:T(8,128)(2,1)S(1)}, s16[400,128]{1,0:T(8,128)(2,1)S(1)}, u32[]{:S(2)}, u32[]{:S(2)}) %collective-permute-start.12) | collective-permute-done | bytes 102432 | tf_op jit(solution)/shard_map/ppermute | solution.py:327
  64.2 1.0 %collective-permute-start.13 = (s16[400,128]{1,0:T(8,128)(2,1)S(1)}, s16[400,128]{1,0:T(8,128)(2,1)S(1)}, u32[]{:S(2)}, u32[]{:S(2)}) collective-permute-start(s16[400,128]{1,0:T(8,128)(2,1)S(1)} %shard_map.48.refs_2_), channel_id=1, source_target_pairs={{0,8},{8,0},{16,24},{24,16},{1,9},{9,1},{17,25},{25,17},{2,10},{10... | collective-permute-start | bytes 307208 | tf_op jit(solution)/shard_map/ppermute | solution.py:330
  65.2 4.1 %collective-permute-done.13.refs_3_ = s16[400,128]{1,0:T(8,128)(2,1)S(1)} collective-permute-done((s16[400,128]{1,0:T(8,128)(2,1)S(1)}, s16[400,128]{1,0:T(8,128)(2,1)S(1)}, u32[]{:S(2)}, u32[]{:S(2)}) %collective-permute-start.13) | collective-permute-done | bytes 102432 | tf_op jit(solution)/shard_map/ppermute | solution.py:330
  69.3 1.1 %shard_map.49 = f32[4,3,128,128]{3,2,1,0:T(8,128)} custom-call(s16[400,128]{1,0:T(8,128)(2,1)S(1)} %shard_map.43.rest_0_.refs_0_, s16[400,128]{1,0:T(8,128)(2,1)S(1)} %collective-permute-done.8.refs_1_, s16[400,128]{1,0:T(8,128)(2,1)S(1)} %shard_map.48.refs_2_, s16[400,128]{1,0:T(8,128)(2,1)S(1)} %collective-permute-done.13.refs_3_), custom_call_target="tpu_custom_call" | custom-call | tf_op jit(solution)/shard_map/pallas_call | solution.py:272
  (23 shorter events, 4.4 us)
Async XLA Ops:
  0.0 9.0 %collective-permute-start = (bf16[512,256]{1,0:T(8,128)(2,1)}, bf16[512,256]{1,0:T(8,128)(2,1)S(1)}, u32[]{:S(2)}, u32[]{:S(2)}) collective-permute-start(bf16[512,256]{1,0:T(8,128)(2,1)} %own.1), channel_id=1, source_target_pairs={{1,2},{2,1},{3,4},{4,3},{5,6},{6,5},{9,10},{10,9},{11,12},{12,11},... | collective-permute-start | bytes 786440 | tf_op jit(solution)/shard_map/ppermute | solution.py:301
  0.7 8.3 %collective-permute-start.1 = (bf16[512,256]{1,0:T(8,128)(2,1)}, bf16[512,256]{1,0:T(8,128)(2,1)S(1)}, u32[]{:S(2)}, u32[]{:S(2)}) collective-permute-start(bf16[512,256]{1,0:T(8,128)(2,1)} %own.1), channel_id=1, source_target_pairs={{0,1},{1,0},{2,3},{3,2},{4,5},{5,4},{6,7},{7,6},{8,9},{9,8},{10,11... | collective-permute-start | bytes 786440 | tf_op jit(solution)/shard_map/ppermute | solution.py:302
  5.9 1.9 %copy-start = (bf16[8,4,3,128,128]{4,3,2,1,0:T(8,128)(2,1)S(1)}, bf16[8,4,3,128,128]{4,3,2,1,0:T(8,128)(2,1)}, u32[]{:S(2)}) copy-start(bf16[8,4,3,128,128]{4,3,2,1,0:T(8,128)(2,1)} %tensor.1) | copy-start | bytes 9437188
  7.8 0.9 %copy-start.1 = (bf16[512,256]{1,0:T(8,128)(2,1)S(1)}, bf16[512,256]{1,0:T(8,128)(2,1)}, u32[]{:S(2)}) copy-start(bf16[512,256]{1,0:T(8,128)(2,1)} %own.1) | copy-start | bytes 786436
  10.8 18.7 %collective-permute-start.2 = (bf16[4,64,2048]{2,1,0:T(8,128)(2,1)S(1)}, bf16[4,64,2048]{2,1,0:T(8,128)(2,1)S(1)}, u32[]{:S(2)}, u32[]{:S(2)}) collective-permute-start(bf16[4,64,2048]{2,1,0:T(8,128)(2,1)S(1)} %get-tuple-element.19), channel_id=1, source_target_pairs={{3,7},{4,0},{11,15},{12,8},{19,23},{20,16},{27,31},{28,24}} | collective-permute-start | bytes 3145736 | tf_op jit(solution)/shard_map/ppermute | solution.py:309
  12.1 19.5 %collective-permute-start.3 = (bf16[4,64,2048]{2,1,0:T(8,128)(2,1)S(1)}, bf16[4,64,2048]{2,1,0:T(8,128)(2,1)S(1)}, u32[]{:S(2)}, u32[]{:S(2)}) collective-permute-start(bf16[4,64,2048]{2,1,0:T(8,128)(2,1)S(1)} %get-tuple-element.20), channel_id=1, source_target_pairs={{1,2},{2,1},{3,4},{4,3},{5,6},{6,5},{9,10},{10,9},{11,12},{12,11},... | collective-permute-start | bytes 3145736 | tf_op jit(solution)/shard_map/ppermute | solution.py:307
  12.9 18.8 %collective-permute-start.4 = (bf16[4,128,1024]{2,1,0:T(8,128)(2,1)S(1)}, bf16[4,128,1024]{2,1,0:T(8,128)(2,1)S(1)}, u32[]{:S(2)}, u32[]{:S(2)}) collective-permute-start(bf16[4,128,1024]{2,1,0:T(8,128)(2,1)S(1)} %get-tuple-element.17.refs_0_.refs_2_.refs_3_.refs_4_), channel_id=1, source_target_pairs={{0,1},{1,0},{2,3},{3,2},{4,5},{5,4},{6,7},{7,6},{8,9},{9,8},{10,11... | collective-permute-start | bytes 3145736 | tf_op jit(solution)/shard_map/ppermute | solution.py:312
  15.7 16.0 %collective-permute-start.5 = (bf16[4,128,1024]{2,1,0:T(8,128)(2,1)S(1)}, bf16[4,128,1024]{2,1,0:T(8,128)(2,1)S(1)}, u32[]{:S(2)}, u32[]{:S(2)}) collective-permute-start(bf16[4,128,1024]{2,1,0:T(8,128)(2,1)S(1)} %get-tuple-element.18.refs_1_.refs_3_.refs_4_.refs_5_), channel_id=1, source_target_pairs={{0,1},{1,0},{2,3},{3,2},{4,5},{5,4},{6,7},{7,6},{8,9},{9,8},{10,11... | collective-permute-start | bytes 3145736 | tf_op jit(solution)/shard_map/ppermute | solution.py:312
  15.8 24.9 %collective-permute-start.9 = (bf16[4,64,2048]{2,1,0:T(8,128)(2,1)S(1)}, bf16[4,64,2048]{2,1,0:T(8,128)(2,1)S(1)}, u32[]{:S(2)}, u32[]{:S(2)}) collective-permute-start(bf16[4,64,2048]{2,1,0:T(8,128)(2,1)S(1)} %get-tuple-element.19), channel_id=1, source_target_pairs={{1,2},{2,1},{5,6},{6,5},{9,10},{10,9},{13,14},{14,13},{17,18},{18,... | collective-permute-start | bytes 3145736 | tf_op jit(solution)/shard_map/ppermute | solution.py:307
  29.6 20.2 %collective-permute-start.10 = (bf16[4,64,2048]{2,1,0:T(8,128)(2,1)S(1)}, bf16[4,64,2048]{2,1,0:T(8,128)(2,1)S(1)}, u32[]{:S(2)}, u32[]{:S(2)}) collective-permute-start(bf16[4,64,2048]{2,1,0:T(8,128)(2,1)S(1)} %collective-permute-done.2.refs_4_), channel_id=1, source_target_pairs={{7,4},{0,3},{15,12},{8,11},{23,20},{16,19},{31,28},{24,27}} | collective-permute-start | bytes 3145736 | tf_op jit(solution)/shard_map/ppermute | solution.py:311
  33.2 4.7 %collective-permute-start.6 = (s16[400,128]{1,0:T(8,128)(2,1)S(1)}, s16[400,128]{1,0:T(8,128)(2,1)S(1)}, u32[]{:S(2)}, u32[]{:S(2)}) collective-permute-start(s16[400,128]{1,0:T(8,128)(2,1)S(1)} %get-tuple-element.22), channel_id=1, source_target_pairs={{0,8},{8,0},{16,24},{24,16},{1,9},{9,1},{17,25},{25,17},{2,10},{10... | collective-permute-start | bytes 307208 | tf_op jit(solution)/shard_map/ppermute | solution.py:323
  38.0 14.3 %collective-permute-start.7 = (s16[400,128]{1,0:T(8,128)(2,1)S(1)}, s16[400,128]{1,0:T(8,128)(2,1)S(1)}, u32[]{:S(2)}, u32[]{:S(2)}) collective-permute-start(s16[400,128]{1,0:T(8,128)(2,1)S(1)} %shard_map.42.mine.refs_7_), channel_id=1, source_target_pairs={{0,16},{8,24},{16,0},{24,8},{1,17},{9,25},{17,1},{25,9},{2,18},{10... | collective-permute-start | bytes 307208 | tf_op jit(solution)/shard_map/ppermute | solution.py:327
  50.7 4.7 %collective-permute-start.11 = (s16[400,128]{1,0:T(8,128)(2,1)S(1)}, s16[400,128]{1,0:T(8,128)(2,1)S(1)}, u32[]{:S(2)}, u32[]{:S(2)}) collective-permute-start(s16[400,128]{1,0:T(8,128)(2,1)S(1)} %get-tuple-element.24), channel_id=1, source_target_pairs={{0,8},{8,0},{16,24},{24,16},{1,9},{9,1},{17,25},{25,17},{2,10},{10... | collective-permute-start | bytes 307208 | tf_op jit(solution)/shard_map/ppermute | solution.py:323
  55.5 8.6 %collective-permute-start.12 = (s16[400,128]{1,0:T(8,128)(2,1)S(1)}, s16[400,128]{1,0:T(8,128)(2,1)S(1)}, u32[]{:S(2)}, u32[]{:S(2)}) collective-permute-start(s16[400,128]{1,0:T(8,128)(2,1)S(1)} %shard_map.47.mine), channel_id=1, source_target_pairs={{0,16},{8,24},{16,0},{24,8},{1,17},{9,25},{17,1},{25,9},{2,18},{10... | collective-permute-start | bytes 307208 | tf_op jit(solution)/shard_map/ppermute | solution.py:327
  58.2 7.1 %collective-permute-start.8 = (s16[400,128]{1,0:T(8,128)(2,1)S(1)}, s16[400,128]{1,0:T(8,128)(2,1)S(1)}, u32[]{:S(2)}, u32[]{:S(2)}) collective-permute-start(s16[400,128]{1,0:T(8,128)(2,1)S(1)} %shard_map.43.rest_0_.refs_0_), channel_id=1, source_target_pairs={{0,8},{8,0},{16,24},{24,16},{1,9},{9,1},{17,25},{25,17},{2,10},{10... | collective-permute-start | bytes 307208 | tf_op jit(solution)/shard_map/ppermute | solution.py:330
  64.2 5.1 %collective-permute-start.13 = (s16[400,128]{1,0:T(8,128)(2,1)S(1)}, s16[400,128]{1,0:T(8,128)(2,1)S(1)}, u32[]{:S(2)}, u32[]{:S(2)}) collective-permute-start(s16[400,128]{1,0:T(8,128)(2,1)S(1)} %shard_map.48.refs_2_), channel_id=1, source_target_pairs={{0,8},{8,0},{16,24},{24,16},{1,9},{9,1},{17,25},{25,17},{2,10},{10... | collective-permute-start | bytes 307208 | tf_op jit(solution)/shard_map/ppermute | solution.py:330

commit v6 on v5

v6 whole, which is shorter than its diff:
```python
import functools
import itertools

import jax
import jax.numpy as jnp
import numpy as np
from jax import lax
from jax.experimental import pallas as pl
from jax.experimental.pallas import tpu as pltpu
from jax.sharding import PartitionSpec as P

CUT = 64
FEW = 3
SCALE_ROWS = 16
FULL = 32752.0
VMEM = pl.BlockSpec(memory_space=pltpu.VMEM)
ANY = pl.BlockSpec(memory_space=pl.ANY)
SMEM = pl.BlockSpec(memory_space=pltpu.SMEM)


def params(mib):
    return pltpu.CompilerParams(vmem_limit_bytes=mib << 20)


NO_COST = pl.CostEstimate(flops=0, bytes_accessed=0, transcendentals=0)


def piece_sizes(aux, count):
    return [aux // count + (k < aux % count) for k in range(count)]


def neighbour(device):
    return device + 2 * (device % 2) - 1


def most_needed(pattern, devices):
    rows = np.arange(pattern.shape[1])
    blocks = len(rows) // devices
    other = neighbour(np.arange(devices))
    wanted = other[:, None] * blocks + np.arange(blocks)
    wanted = np.where(((other >= 0) & (other < devices))[:, None], wanted, -2).astype(np.int32)
    own = rows // blocks == np.arange(devices)[:, None]
    listed = (pattern == wanted[:, :, None, None]) & own[:, None, None, :]
    return jnp.max(jnp.sum(jnp.any(listed, axis=(2, 3)), axis=1))


def needed(pattern, blocks, of, by):
    listed = [pattern[j, by * blocks + m] for j in range(pattern.shape[0]) for m in range(blocks)]
    return [functools.reduce(jnp.logical_or, [one == of * blocks + block for one in listed]) for block in range(blocks)]


def fetch_kernel(tensor, own, tensor_out, own_out, sems):
    copies = [
        pltpu.make_async_copy(own, own_out, sems.at[0]),
        pltpu.make_async_copy(tensor, tensor_out, sems.at[1]),
    ]
    for copy in copies:
        copy.start()
    for copy in copies:
        copy.wait()


def fetch(tensor, own):
    arrays = (tensor, own)
    return pl.pallas_call(
        fetch_kernel,
        out_shape=[jax.ShapeDtypeStruct(a.shape, a.dtype) for a in arrays],
        in_specs=[ANY] * 2,
        out_specs=[VMEM] * 2,
        scratch_shapes=[pltpu.SemaphoreType.DMA((2,))],
        compiler_params=params(8),
        cost_estimate=NO_COST,
    )(*(pltpu.with_memory_space_constraint(a, pltpu.HBM) for a in arrays))


def half_kernel(cuts, count, relays, pattern, own, *refs):
    outs = refs[-(len(cuts) - 1 + count) :]
    parts, pieces = outs[: len(cuts) - 1], outs[len(cuts) - 1 :]
    *across, beside, tensor = refs[: -len(outs)]
    aux, blocks, slots, width, _ = tensor.shape
    occupied = own.shape[1]
    sizes = piece_sizes(aux, count)
    owner = [(k, i) for k, size in enumerate(sizes) for i in range(size)]
    device = lax.axis_index("bas")
    relayed = functools.reduce(jnp.logical_or, [device == target for target in relays], False)
    held = parts[0].shape[0]
    other = neighbour(device)
    there = (other >= 0) & (other < lax.axis_size("bas"))
    if held < blocks:
        asked = needed(pattern, blocks, device, jnp.clip(other, 0, lax.axis_size("bas") - 1))
    packed = jnp.int32(0)
    for m in range(blocks):
        chosen = []
        for j in range(slots):
            place = pattern[j, device * blocks + m]
            group = place // blocks
            rows = pl.ds(pl.multiple_of(jnp.maximum(place, 0) % blocks * width, width), width)
            value = across[0][rows, :]
            if relays:
                value = jnp.where(relayed, across[1][rows, :], value)
            value = jnp.where(group == device ^ 1, beside[rows, :], value)
            value = jnp.where(group == device, own[rows, :], value)
            chosen.append(jnp.where(place < 0, jnp.zeros_like(value), value))
        chosen = jnp.concatenate(chosen, axis=0)
        for p in range(aux):
            row = jnp.concatenate([tensor[p, m, j] for j in range(slots)], axis=1)
            half = jnp.dot(row, chosen, preferred_element_type=jnp.float32).astype(jnp.bfloat16)
            piece, column = owner[p]
            pieces[piece][m, :, column * occupied : (column + 1) * occupied] = half
            for part, start, stop in zip(parts, cuts, cuts[1:]):
                if held == blocks:
                    part[m, :, p * occupied : (p + 1) * occupied] = half[start:stop]
                elif m < held:
                    part[packed, :, p * occupied : (p + 1) * occupied] = half[start:stop]
        if held <= m:

            @pl.when(packed < held)
            def _():
                for part, start, stop in zip(parts, cuts, cuts[1:]):
                    at = 0
                    for piece in pieces:
                        part[packed, :, at : at + piece.shape[2]] = piece[m, start:stop, :]
                        at += piece.shape[2]

        if held < blocks:
            packed += (asked[m] & there).astype(jnp.int32)


def half_forms(held, count, cuts, relays, pattern, own, beside, across, tensor):
    aux, blocks, slots, width, _ = tensor.shape
    depth = aux * own.shape[1]
    shapes = [(held, b - a, depth) for a, b in zip(cuts, cuts[1:])]
    shapes += [(blocks, width, size * own.shape[1]) for size in piece_sizes(aux, count)]
    outs = pl.pallas_call(
        functools.partial(half_kernel, cuts, count, relays),
        out_shape=[jax.ShapeDtypeStruct(shape, jnp.bfloat16) for shape in shapes],
        in_specs=[SMEM] + [VMEM] * (3 + len(across)),
        out_specs=[VMEM] * len(shapes),
        compiler_params=params(24),
        cost_estimate=NO_COST,
    )(pattern, own, *across, beside, tensor)
    return outs[:-count], outs[-count:]


def encode(tiles, coded, scales):
    rows = tiles[0].shape[0]
    scales[...] = jnp.zeros_like(scales)
    for t, tile in enumerate(tiles):
        most = jnp.max(jnp.abs(tile), axis=0, keepdims=True)
        power = jnp.ceil(jnp.log2(jnp.maximum(most, 2.0**-90)))
        scales[t : t + 1, :] = power
        whole = jnp.round(tile * (FULL * jnp.exp2(-power)))
        coded[t * rows : (t + 1) * rows, :] = whole.astype(jnp.int32).astype(jnp.int16)
    end = len(tiles) * rows
    coded[end : end + SCALE_ROWS, :] = scales[...].astype(jnp.int32).astype(jnp.int16)


def decode(coded, rows, count):
    end = count * rows
    scales = coded[end : end + SCALE_ROWS, :].astype(jnp.int32).astype(jnp.float32)
    scales = jnp.exp2(scales) * (1.0 / FULL)
    for t in range(count):
        value = coded[t * rows : (t + 1) * rows, :].astype(jnp.int32).astype(jnp.float32)
        yield value * scales[t : t + 1, :]


def times(rows, pieces):
    total = 0.0
    for k, piece in enumerate(pieces):
        left, right = rows(k), piece[...]
        total += lax.dot_general(
            left.reshape(-1, left.shape[2]),
            right.reshape(-1, right.shape[2]),
            (((1,), (1,)), ((), ())),
            preferred_element_type=jnp.float32,
        )
    return total


def product_kernel(count, start, stop, *refs):
    rows, whole, product = refs[:count], refs[count : 2 * count], refs[-1]
    product[...] = times(lambda k: rows[k][:, start:stop, :], whole)


def products(start, stop, rows, whole, *earlier):
    blocks, width, _ = whole[0].shape
    return pl.pallas_call(
        functools.partial(product_kernel, len(whole), start, stop),
        out_shape=jax.ShapeDtypeStruct((blocks * (stop - start), blocks * width), jnp.float32),
        in_specs=[VMEM] * (2 * len(whole)) + [ANY] * len(earlier),
        out_specs=VMEM,
        compiler_params=params(24),
        cost_estimate=NO_COST,
    )(*rows, *whole, *earlier)


def gate_kernel(_, out):
    out[...] = jnp.zeros_like(out)


def gate(earlier):
    return pl.pallas_call(
        gate_kernel,
        out_shape=jax.ShapeDtypeStruct((8, 128), jnp.float32),
        in_specs=[ANY],
        out_specs=VMEM,
        compiler_params=params(4),
        cost_estimate=NO_COST,
    )(earlier)


def tile_kernel(relays, count, pieces, start, pattern, own, *refs):
    across, whole, near = refs[:count], refs[count : count + pieces], refs[count + pieces : -7]
    kept, sent, far, close, scales, places, sem = refs[-7:]
    blocks, width, _ = whole[0].shape
    ends = list(itertools.accumulate([piece.shape[2] for piece in whole], initial=0))
    rows = across[0].shape[1]
    slots = pattern.shape[0]
    device, layer = lax.axis_index("bas"), lax.axis_index("aux")
    half = blocks * slots // 2
    copy = pltpu.make_async_copy(pattern, places, sem)
    copy.start()

    def multiply(source):
        far[...] = times(lambda k: source[:, :, ends[k] : ends[k + 1]], whole)

    if count > 1:
        relayed = functools.reduce(jnp.logical_or, [device == target for target in relays])
        pl.when(relayed)(lambda: multiply(across[1]))
        pl.when(jnp.logical_not(relayed))(lambda: multiply(across[0]))
    else:
        multiply(across[0])
    if start is None:
        close = near[0]
    else:
        close[...] = times(lambda k: near[k][:, start : start + rows, :], whole)
    copy.wait()
    held = far.shape[0] // rows
    if held < blocks:
        asked = needed(places, blocks, neighbour(device), device)

    def tile(t, parity):
        m = parity * (blocks // 2) + t // slots
        place = places[t % slots, device * blocks + m]
        group, block = place // blocks, jnp.maximum(place, 0) % blocks
        columns = pl.ds(pl.multiple_of(m * width, width), width)
        part = pl.ds(pl.multiple_of(block * rows, rows), rows), columns
        if held < blocks:
            before = [jnp.where(asked[i] & (i < block), 1, 0) for i in range(blocks)]
            block = jnp.minimum(sum(before), held - 1)
        value = far[pl.ds(pl.multiple_of(block * rows, rows), rows), columns]
        value = jnp.where(group == device ^ 1, close[part], value)
        value = jnp.where(group == device, own[part], value)
        return jnp.where(place < 0, 0.0, value)

    for t in range(half):
        kept[t * rows : (t + 1) * rows, :] = tile(t, layer % 2)
    encode([tile(t, 1 - layer % 2) for t in range(half)], sent, scales)


def chunk_tiles(relays, start, pattern, own, across, whole, near, *earlier):
    blocks, width, _ = whole[0].shape
    rows, slots = across[0].shape[1], pattern.shape[0]
    half = blocks * slots // 2
    product = (blocks * rows, blocks * width)
    held = across[0].shape[0]

    def kernel(*refs):
        given = 2 + len(across) + len(whole) + len(near)
        tile_kernel(relays, len(across), len(whole), start, *refs[:given], *refs[given + len(earlier) :])

    return pl.pallas_call(
        kernel,
        out_shape=[
            jax.ShapeDtypeStruct((half * rows, width), jnp.float32),
            jax.ShapeDtypeStruct((half * rows + SCALE_ROWS, width), jnp.int16),
        ],
        in_specs=[ANY] + [VMEM] * (1 + len(across) + len(whole) + len(near)) + [ANY] * len(earlier),
        out_specs=[VMEM] * 2,
        scratch_shapes=[
            pltpu.VMEM((held * rows, blocks * width), jnp.float32),
            pltpu.VMEM((8, 128) if start is None else product, jnp.float32),
            pltpu.VMEM((SCALE_ROWS, width), jnp.float32),
            pltpu.SMEM(pattern.shape, pattern.dtype),
            pltpu.SemaphoreType.DMA,
        ],
        compiler_params=params(24),
        cost_estimate=NO_COST,
    )(pattern, own, *across, *whole, *near, *earlier)


def add_kernel(count, mine, other, *rest):
    coded, scales = rest[-2:]
    rows = (coded.shape[0] - SCALE_ROWS) // count
    if mine.dtype == jnp.float32:
        held = [mine[t * rows : (t + 1) * rows, :] for t in range(count)]
    else:
        held = decode(mine, rows, count)
    encode([a + b for a, b in zip(held, decode(other, rows, count))], coded, scales)


def add_coded(count, mine, other, *earlier):
    return pl.pallas_call(
        functools.partial(add_kernel, count),
        out_shape=jax.ShapeDtypeStruct(other.shape, other.dtype),
        in_specs=[VMEM] * 2 + [ANY] * len(earlier),
        out_specs=VMEM,
        scratch_shapes=[pltpu.VMEM((SCALE_ROWS, other.shape[1]), jnp.float32)],
        compiler_params=params(8),
        cost_estimate=NO_COST,
    )(mine, other, *earlier)


def final_kernel(*refs):
    coded, out = refs[:-1], refs[-1]
    blocks, slots, width, _ = out.shape
    half = blocks * slots // 2
    layer = lax.axis_index("aux")
    for mine in range(2):
        base = jnp.where(layer % 2 == mine, 0, half)
        chunks = [list(decode(part, (part.shape[0] - SCALE_ROWS) // half, half)) for part in coded[mine::2]]
        for t in range(half):
            place = base + t
            out[place // slots, place % slots] = jnp.concatenate([chunk[t] for chunk in chunks], axis=0).T


def final_tiles(shape, coded):
    return pl.pallas_call(
        final_kernel,
        out_shape=jax.ShapeDtypeStruct(shape, jnp.float32),
        in_specs=[VMEM] * len(coded),
        out_specs=VMEM,
        compiler_params=params(8),
        cost_estimate=NO_COST,
    )(*coded)


def flipped(size, mask):
    return [(i, i ^ mask) for i in range(size)]


def body(coefficients, tensor, pattern):
    devices, layers = lax.axis_size("bas"), lax.axis_size("aux")
    _, blocks, slots, width, _ = tensor.shape
    chip = flipped(devices, 1)
    across = [pair for i in range(1, devices - 1, 2) for pair in ((i, i + 1), (i + 1, i))]
    detours = ((3, 4, 7), (4, 3, 0)) if devices == 8 else ()
    direct = [pair for pair in across if pair not in [d[:2] for d in detours]]
    there = [(source, via) for source, _, via in detours]
    onward = [(via, target) for _, target, via in detours]
    relays = tuple(target for _, target, _ in detours)

    beyond = [lax.ppermute(coefficients, "bas", direct)]
    if detours:
        beyond.append(lax.ppermute(coefficients, "bas", [pair for pair in across if pair not in direct]))
    beside = lax.ppermute(coefficients, "bas", chip)
    tensor, coefficients = fetch(tensor, coefficients)
    cuts = (0, CUT, width)
    pattern = pattern.T
    few = most_needed(pattern, devices) <= FEW

    def exchange(held, count, pattern, coefficients, beside, beyond, tensor):
        (early, *late), whole = half_forms(held, count, cuts, relays, pattern, coefficients, beside, beyond, tensor)
        arrived = [[lax.ppermute(early, "bas", across)]] + [[lax.ppermute(part, "bas", direct)] for part in late]
        if detours:
            halfway = [lax.ppermute(part, "bas", there) for part in late]
            for got, part in zip(arrived[1:], halfway):
                got.append(lax.ppermute(part, "bas", onward))
        beside = [lax.ppermute(piece, "bas", chip) for piece in whole]
        half = blocks * slots // 2
        opened = gate(arrived[0][0])
        owned = [products(a, b, whole, whole, halfway[-1] if detours else opened) for a, b in zip(cuts, cuts[1:])]
        coded, earlier, summed = [], (opened,), ()
        for start, stop, own, got in zip(cuts, cuts[1:], owned, arrived):
            if start == 0:
                kept, sent = chunk_tiles(relays, 0, pattern, own, got, whole, beside, *earlier)
            else:
                near = products(start, stop, beside, whole, opened)
                kept, sent = chunk_tiles(relays, None, pattern, own, got, whole, [near], *earlier)
            mine = add_coded(half, kept, lax.ppermute(sent, "aux", flipped(layers, 1)), *summed)
            earlier = (mine,)
            mask = 2
            while mask < layers:
                mine = add_coded(half, mine, lax.ppermute(mine, "aux", flipped(layers, mask)))
                mask *= 2
            summed = (mine,)
            coded += [mine, lax.ppermute(mine, "aux", flipped(layers, 1))]
        return final_tiles((blocks, slots, width, width), coded)

    operands = (pattern, coefficients, beside, beyond, tensor)
    if blocks <= FEW:
        return exchange(blocks, 2, *operands)
    return lax.cond(few, functools.partial(exchange, FEW, 2), functools.partial(exchange, blocks, 2), *operands)


def solution(mesh):
    return jax.shard_map(
        body,
        mesh=mesh,
        in_specs=(P("bas", None), P("aux", "bas", None, None, None), P()),
        out_specs=P("bas", None, None, None),
        check_vma=False,
    )
```

time: 70.7 us -> 67.7 us (0.958)
  waiting for transfers between devices: 35.1 us -> 31.7 us
  local copies, waits for them, and re-layouts: 3.7 us -> 0.88 us
  Pallas kernels: 8.22 us -> 10.2 us
  other arithmetic: 0 us -> 1.59 us
  starting transfers between devices: 23.1 us -> 22.1 us
    ppermute x13 -> x14, waiting for transfers between devices: 35.1 us -> 31.6 us  [the longest x1 11 us: exchange(): halfway = [lax.ppermute(part, 'bas', there) for part in late]]
    unnamed x5 -> x4, local copies, waits for them, and re-layouts: 3.6 us -> 0.88 us
    pallas_call x1, Pallas kernels: 0.25 us -> 2.01 us  [fetch(): pl.pallas_call(fetch_kernel, out_shape=[jax.ShapeDtypeStruct(a.shape, a.d...]
    ppermute x13 -> x14, starting transfers between devices: 18.8 us -> 17.8 us  [the longest x2 5.32 us: exchange(): lax.ppermute(mine, 'aux', flipped(layers, mask))]
    reduce_or x0 -> x1, other arithmetic: none -> 0.93 us  [most_needed(): return jnp.max(jnp.sum(jnp.any(listed, axis=(2, 3)), axis=1))]
    pallas_call x1, Pallas kernels: 1.08 us -> 0.28 us  [final_tiles(): pl.pallas_call(final_kernel, out_shape=jax.ShapeDtypeStruct(shape, jnp.fl...]
  transfers between devices with their start and end apart: 14 -> 15, of which waited for: 6 -> 6; matrix products, arithmetic and copies ran while one was open for 1% -> 2% of each run, Pallas kernels for 7% -> 11%
where the time goes in v6:
time: 67.7 us; the launch traced here: 67.5 us
  waiting for transfers between devices  31.7 us (47%)
  starting transfers between devices  22.1 us (33%)
  Pallas kernels  10.2 us (15%)
  other arithmetic  1.59 us (2%)
  local copies, waits for them, and re-layouts  0.88 us (1%)
  between operations  0.72 us (1%)
    ppermute x1, waiting for transfers between devices, exchange(): halfway = [lax.ppermute(part, 'bas', there) for part in late]  11 us
    ppermute x1, waiting for transfers between devices, exchange(): got.append(lax.ppermute(part, 'bas', onward))  7.13 us
    ppermute x2, waiting for transfers between devices, exchange(): lax.ppermute(sent, 'aux', flipped(layers, 1))  5.55 us
    ppermute x2, starting transfers between devices, exchange(): lax.ppermute(mine, 'aux', flipped(layers, mask))  5.32 us
    ppermute x1, starting transfers between devices, body(): beside = lax.ppermute(coefficients, 'bas', chip)  4.29 us
    ppermute x2, waiting for transfers between devices, exchange(): coded += [mine, lax.ppermute(mine, 'aux', flipped(layers, 1))]  4.08 us
    ppermute x2, waiting for transfers between devices, exchange(): lax.ppermute(mine, 'aux', flipped(layers, mask))  3.83 us
    ppermute x2, starting transfers between devices, exchange(): lax.ppermute(sent, 'aux', flipped(layers, 1))  3.3 us
  transfers between devices with their start and end apart: 15, of which 6 were waited for; matrix products, arithmetic and copies ran while one was open for 2% of the time, Pallas kernels for 11%

profile of v6, /device:TPU:0, one launch (start us, length us, event | category | flops | bytes accessed | tf_op | source)
XLA Modules:
  0.0 67.5 jit_solution(16769323796029590021)
XLA Ops:
  0.0 0.8 %collective-permute-start.24 = (bf16[512,256]{1,0:T(8,128)(2,1)}, bf16[512,256]{1,0:T(8,128)(2,1)S(1)}, u32[]{:S(2)}, u32[]{:S(2)}) collective-permute-start(bf16[512,256]{1,0:T(8,128)(2,1)} %own.1), channel_id=1, source_target_pairs={{1,2},{2,1},{5,6},{6,5},{9,10},{10,9},{13,14},{14,13},{17,18},{18,... | collective-permute-start | bytes 786440 | tf_op jit(solution)/shard_map/ppermute | solution.py:353
  0.8 1.4 %collective-permute-start.25 = (bf16[512,256]{1,0:T(8,128)(2,1)}, bf16[512,256]{1,0:T(8,128)(2,1)}, u32[]{:S(2)}, u32[]{:S(2)}) collective-permute-start(bf16[512,256]{1,0:T(8,128)(2,1)} %own.1), channel_id=1, source_target_pairs={{3,4},{4,3},{11,12},{12,11},{19,20},{20,19},{27,28},{28,27}} | collective-permute-start | bytes 786440 | tf_op jit(solution)/shard_map/ppermute | solution.py:355
  2.2 4.3 %collective-permute-start.26 = (bf16[512,256]{1,0:T(8,128)(2,1)}, bf16[512,256]{1,0:T(8,128)(2,1)}, u32[]{:S(2)}, u32[]{:S(2)}) collective-permute-start(bf16[512,256]{1,0:T(8,128)(2,1)} %own.1), channel_id=1, source_target_pairs={{0,1},{1,0},{2,3},{3,2},{4,5},{5,4},{6,7},{7,6},{8,9},{9,8},{10,11... | collective-permute-start | bytes 786440 | tf_op jit(solution)/shard_map/ppermute | solution.py:356
  6.5 0.9 %and_reduce_fusion = pred[8,4]{0,1:T(4,128)(4,1)S(1)} fusion(s32[8,4]{0,1:T(4,128)} %constant.15, s32[3,32]{1,0:T(4,128)} %bitcast.1, pred[8,32]{1,0:T(8,128)(4,1)} %constant.16), kind=kLoop, calls=%fused_computation | loop fusion | flops 9184 | bytes 800 | tf_op jit(solution)/shard_map/reduce_or | solution.py:44
  8.7 2.0 %shard_map.57 = (bf16[8,4,3,128,128]{4,3,2,1,0:T(8,128)(2,1)S(1)}, bf16[512,256]{1,0:T(8,128)(2,1)S(1)}) custom-call(bf16[8,4,3,128,128]{4,3,2,1,0:T(8,128)(2,1)} %tensor.1, bf16[512,256]{1,0:T(8,128)(2,1)} %own.1), custom_call_target="tpu_custom_call" | custom-call | tf_op jit(solution)/shard_map/pallas_call | solution.py:65
  10.8 55.8 %conditional.1 = (f32[4,3,128,128]{3,2,1,0:T(8,128)S(1)}) conditional(s32[]{:T(128)} %convert_element_type.7, (s32[3,32]{1,0:T(4,128)S(1)}, bf16[512,256]{1,0:T(8,128)(2,1)S(1)}, bf16[512,256]{1,0:T(8,128)(2,1)S(1)}, bf16[512,256]{1,0:T(8,128)(2,1)}, bf16[512,256]{1,0:T(8,128)(2,1)}, /*index=5*/bf16[8,4,3,128,128]{4,3,2,1,0:T(8,128)(2,1)S(1)}) %tuple.17, ...), branch_computations={%region_3.0_spmd, %region_4.0_spmd} | conditional | bytes 27623912 | solution.py:393
  10.8 2.4 %branch_1_fun.12 = (bf16[3,64,2048]{2,1,0:T(8,128)(2,1)S(1)}, bf16[3,64,2048]{2,1,0:T(8,128)(2,1)S(1)}, bf16[4,128,1024]{2,1,0:T(8,128)(2,1)S(1)}, bf16[4,128,1024]{2,1,0:T(8,128)(2,1)S(1)}) custom-call(s32[3,32]{1,0:T(4,128)S(1)} %get-tuple-element.46.pattern.refs_0_, bf16[512,256]{1,0:T(8,128)(2,1)S(1)} %get-tuple-element.47.own, ...), custom_call_target="tpu_custom_call" | custom-call | tf_op jit(solution)/shard_map/cond/branch_1_fun/pallas_call | solution.py:134
  13.2 1.3 %collective-permute-start.12 = (bf16[3,64,2048]{2,1,0:T(8,128)(2,1)S(1)}, bf16[3,64,2048]{2,1,0:T(8,128)(2,1)S(1)}, u32[]{:S(2)}, u32[]{:S(2)}) collective-permute-start(bf16[3,64,2048]{2,1,0:T(8,128)(2,1)S(1)} %get-tuple-element.54), channel_id=1, source_target_pairs={{3,7},{4,0},{11,15},{12,8},{19,23},{20,16},{27,31},{28,24}} | collective-permute-start | bytes 2359304 | tf_op jit(solution)/shard_map/cond/branch_1_fun/ppermute | solution.py:366
  16.5 11.0 %collective-permute-done.12.refs_4_ = bf16[3,64,2048]{2,1,0:T(8,128)(2,1)S(1)} collective-permute-done((bf16[3,64,2048]{2,1,0:T(8,128)(2,1)S(1)}, bf16[3,64,2048]{2,1,0:T(8,128)(2,1)S(1)}, u32[]{:S(2)}, u32[]{:S(2)}) %collective-permute-start.12) | collective-permute-done | bytes 786464 | tf_op jit(solution)/shard_map/cond/branch_1_fun/ppermute | solution.py:366
  27.5 1.5 %collective-permute-start.20 = (bf16[3,64,2048]{2,1,0:T(8,128)(2,1)S(1)}, bf16[3,64,2048]{2,1,0:T(8,128)(2,1)S(1)}, u32[]{:S(2)}, u32[]{:S(2)}) collective-permute-start(bf16[3,64,2048]{2,1,0:T(8,128)(2,1)S(1)} %collective-permute-done.12.refs_4_), channel_id=1, source_target_pairs={{7,4},{0,3},{15,12},{8,11},{23,20},{16,19},{31,28},{24,27}} | collective-permute-start | bytes 2359304 | tf_op jit(solution)/shard_map/cond/branch_1_fun/ppermute | solution.py:368
  29.0 0.7 %branch_1_fun.13.refs_1_ = f32[256,512]{1,0:T(8,128)S(1)} custom-call(bf16[4,128,1024]{2,1,0:T(8,128)(2,1)S(1)} %get-tuple-element.52.refs_0_.refs_2_.refs_3_.refs_4_, bf16[4,128,1024]{2,1,0:T(8,128)(2,1)S(1)} %get-tuple-element.53.refs_1_.refs_3_.refs_4_.refs_5_, bf16[4,128,1024]{2,1,0:T(8,128)(2,1)S(1)} %get-tuple-element.52.refs_0_.refs_2_.refs_3_.refs_4_, ...), custom_call_target="tpu_custom_call" | custom-call | tf_op jit(solution)/shard_map/cond/branch_1_fun/pallas_call | solution.py:187
  29.8 1.8 %branch_1_fun.15 = (f32[384,128]{1,0:T(8,128)S(1)}, s16[400,128]{1,0:T(8,128)(2,1)S(1)}) custom-call(s32[3,32]{1,0:T(4,128)S(1)} %get-tuple-element.46.pattern.refs_0_, f32[256,512]{1,0:T(8,128)S(1)} %branch_1_fun.13.refs_1_, bf16[3,64,2048]{2,1,0:T(8,128)(2,1)S(1)} %collective-permute-done.13._.refs_2_, ...), custom_call_target="tpu_custom_call" | custom-call | tf_op jit(solution)/shard_map/cond/branch_1_fun/pallas_call | solution.py:272
  31.6 1.6 %collective-permute-start.16 = (s16[400,128]{1,0:T(8,128)(2,1)S(1)}, s16[400,128]{1,0:T(8,128)(2,1)S(1)}, u32[]{:S(2)}, u32[]{:S(2)}) collective-permute-start(s16[400,128]{1,0:T(8,128)(2,1)S(1)} %get-tuple-element.57), channel_id=1, source_target_pairs={{0,8},{8,0},{16,24},{24,16},{1,9},{9,1},{17,25},{25,17},{2,10},{10... | collective-permute-start | bytes 307208 | tf_op jit(solution)/shard_map/cond/branch_1_fun/ppermute | solution.py:380
  34.7 1.6 %collective-permute-done.16.other = s16[400,128]{1,0:T(8,128)(2,1)S(1)} collective-permute-done((s16[400,128]{1,0:T(8,128)(2,1)S(1)}, s16[400,128]{1,0:T(8,128)(2,1)S(1)}, u32[]{:S(2)}, u32[]{:S(2)}) %collective-permute-start.16) | collective-permute-done | bytes 102432 | tf_op jit(solution)/shard_map/cond/branch_1_fun/ppermute | solution.py:380
  36.4 2.7 %collective-permute-start.17 = (s16[400,128]{1,0:T(8,128)(2,1)S(1)}, s16[400,128]{1,0:T(8,128)(2,1)S(1)}, u32[]{:S(2)}, u32[]{:S(2)}) collective-permute-start(s16[400,128]{1,0:T(8,128)(2,1)S(1)} %branch_1_fun.16.mine.refs_7_), channel_id=1, source_target_pairs={{0,16},{8,24},{16,0},{24,8},{1,17},{9,25},{17,1},{25,9},{2,18},{10... | collective-permute-start | bytes 307208 | tf_op jit(solution)/shard_map/cond/branch_1_fun/ppermute | solution.py:384
  39.1 7.1 %collective-permute-done.20.refs_3_ = bf16[3,64,2048]{2,1,0:T(8,128)(2,1)S(1)} collective-permute-done((bf16[3,64,2048]{2,1,0:T(8,128)(2,1)S(1)}, bf16[3,64,2048]{2,1,0:T(8,128)(2,1)S(1)}, u32[]{:S(2)}, u32[]{:S(2)}) %collective-permute-start.20) | collective-permute-done | bytes 786464 | tf_op jit(solution)/shard_map/cond/branch_1_fun/ppermute | solution.py:368
  46.2 1.2 %branch_1_fun.20 = (f32[384,128]{1,0:T(8,128)S(1)}, s16[400,128]{1,0:T(8,128)(2,1)S(1)}) custom-call(s32[3,32]{1,0:T(4,128)S(1)} %get-tuple-element.46.pattern.refs_0_, f32[256,512]{1,0:T(8,128)S(1)} %branch_1_fun.18.refs_1_, bf16[3,64,2048]{2,1,0:T(8,128)(2,1)S(1)} %collective-permute-done.19.refs_2_, ...), custom_call_target="tpu_custom_call" | custom-call | tf_op jit(solution)/shard_map/cond/branch_1_fun/pallas_call | solution.py:272
  47.4 1.7 %collective-permute-start.21 = (s16[400,128]{1,0:T(8,128)(2,1)S(1)}, s16[400,128]{1,0:T(8,128)(2,1)S(1)}, u32[]{:S(2)}, u32[]{:S(2)}) collective-permute-start(s16[400,128]{1,0:T(8,128)(2,1)S(1)} %get-tuple-element.59), channel_id=1, source_target_pairs={{0,8},{8,0},{16,24},{24,16},{1,9},{9,1},{17,25},{25,17},{2,10},{10... | collective-permute-start | bytes 307208 | tf_op jit(solution)/shard_map/cond/branch_1_fun/ppermute | solution.py:380
  49.2 3.9 %collective-permute-done.21.other = s16[400,128]{1,0:T(8,128)(2,1)S(1)} collective-permute-done((s16[400,128]{1,0:T(8,128)(2,1)S(1)}, s16[400,128]{1,0:T(8,128)(2,1)S(1)}, u32[]{:S(2)}, u32[]{:S(2)}) %collective-permute-start.21) | collective-permute-done | bytes 102432 | tf_op jit(solution)/shard_map/cond/branch_1_fun/ppermute | solution.py:380
  53.2 2.7 %collective-permute-start.22 = (s16[400,128]{1,0:T(8,128)(2,1)S(1)}, s16[400,128]{1,0:T(8,128)(2,1)S(1)}, u32[]{:S(2)}, u32[]{:S(2)}) collective-permute-start(s16[400,128]{1,0:T(8,128)(2,1)S(1)} %branch_1_fun.21.mine), channel_id=1, source_target_pairs={{0,16},{8,24},{16,0},{24,8},{1,17},{9,25},{17,1},{25,9},{2,18},{10... | collective-permute-start | bytes 307208 | tf_op jit(solution)/shard_map/cond/branch_1_fun/ppermute | solution.py:384
  55.9 1.6 %collective-permute-start.18 = (s16[400,128]{1,0:T(8,128)(2,1)S(1)}, s16[400,128]{1,0:T(8,128)(2,1)S(1)}, u32[]{:S(2)}, u32[]{:S(2)}) collective-permute-start(s16[400,128]{1,0:T(8,128)(2,1)S(1)} %branch_1_fun.17.rest_0_.refs_0_), channel_id=1, source_target_pairs={{0,8},{8,0},{16,24},{24,16},{1,9},{9,1},{17,25},{25,17},{2,10},{10... | collective-permute-start | bytes 307208 | tf_op jit(solution)/shard_map/cond/branch_1_fun/ppermute | solution.py:387
  57.4 3.8 %collective-permute-done.22.other = s16[400,128]{1,0:T(8,128)(2,1)S(1)} collective-permute-done((s16[400,128]{1,0:T(8,128)(2,1)S(1)}, s16[400,128]{1,0:T(8,128)(2,1)S(1)}, u32[]{:S(2)}, u32[]{:S(2)}) %collective-permute-start.22) | collective-permute-done | bytes 102432 | tf_op jit(solution)/shard_map/cond/branch_1_fun/ppermute | solution.py:384
  62.0 4.1 %collective-permute-done.23.refs_3_ = s16[400,128]{1,0:T(8,128)(2,1)S(1)} collective-permute-done((s16[400,128]{1,0:T(8,128)(2,1)S(1)}, s16[400,128]{1,0:T(8,128)(2,1)S(1)}, u32[]{:S(2)}, u32[]{:S(2)}) %collective-permute-start.23) | collective-permute-done | bytes 102432 | tf_op jit(solution)/shard_map/cond/branch_1_fun/ppermute | solution.py:387
  66.6 0.9 %copy-done = f32[4,3,128,128]{3,2,1,0:T(8,128)} copy-done((f32[4,3,128,128]{3,2,1,0:T(8,128)}, f32[4,3,128,128]{3,2,1,0:T(8,128)S(1)}, u32[]{:S(2)}) %copy-start) | copy-done | bytes 786456
  (27 shorter events, 5.4 us)
Async XLA Ops:
  0.0 10.8 %copy-start.1 = (s32[32,3]{0,1:T(4,128)S(1)}, s32[32,3]{0,1:T(4,128)}, u32[]{:S(2)}) copy-start(s32[32,3]{0,1:T(4,128)} %param.9) | copy-start | bytes 1156
  0.0 10.7 %collective-permute-start.24 = (bf16[512,256]{1,0:T(8,128)(2,1)}, bf16[512,256]{1,0:T(8,128)(2,1)S(1)}, u32[]{:S(2)}, u32[]{:S(2)}) collective-permute-start(bf16[512,256]{1,0:T(8,128)(2,1)} %own.1), channel_id=1, source_target_pairs={{1,2},{2,1},{5,6},{6,5},{9,10},{10,9},{13,14},{14,13},{17,18},{18,... | collective-permute-start | bytes 786440 | tf_op jit(solution)/shard_map/ppermute | solution.py:353
  0.8 9.9 %collective-permute-start.25 = (bf16[512,256]{1,0:T(8,128)(2,1)}, bf16[512,256]{1,0:T(8,128)(2,1)}, u32[]{:S(2)}, u32[]{:S(2)}) collective-permute-start(bf16[512,256]{1,0:T(8,128)(2,1)} %own.1), channel_id=1, source_target_pairs={{3,4},{4,3},{11,12},{12,11},{19,20},{20,19},{27,28},{28,27}} | collective-permute-start | bytes 786440 | tf_op jit(solution)/shard_map/ppermute | solution.py:355
  2.2 8.6 %collective-permute-start.26 = (bf16[512,256]{1,0:T(8,128)(2,1)}, bf16[512,256]{1,0:T(8,128)(2,1)}, u32[]{:S(2)}, u32[]{:S(2)}) collective-permute-start(bf16[512,256]{1,0:T(8,128)(2,1)} %own.1), channel_id=1, source_target_pairs={{0,1},{1,0},{2,3},{3,2},{4,5},{5,4},{6,7},{7,6},{8,9},{9,8},{10,11... | collective-permute-start | bytes 786440 | tf_op jit(solution)/shard_map/ppermute | solution.py:356
  13.2 14.4 %collective-permute-start.12 = (bf16[3,64,2048]{2,1,0:T(8,128)(2,1)S(1)}, bf16[3,64,2048]{2,1,0:T(8,128)(2,1)S(1)}, u32[]{:S(2)}, u32[]{:S(2)}) collective-permute-start(bf16[3,64,2048]{2,1,0:T(8,128)(2,1)S(1)} %get-tuple-element.54), channel_id=1, source_target_pairs={{3,7},{4,0},{11,15},{12,8},{19,23},{20,16},{27,31},{28,24}} | collective-permute-start | bytes 2359304 | tf_op jit(solution)/shard_map/cond/branch_1_fun/ppermute | solution.py:366
  14.5 15.3 %collective-permute-start.14 = (bf16[4,128,1024]{2,1,0:T(8,128)(2,1)S(1)}, bf16[4,128,1024]{2,1,0:T(8,128)(2,1)S(1)}, u32[]{:S(2)}, u32[]{:S(2)}) collective-permute-start(bf16[4,128,1024]{2,1,0:T(8,128)(2,1)S(1)} %get-tuple-element.52.refs_0_.refs_2_.refs_3_.refs_4_), channel_id=1, source_target_pairs={{0,1},{1,0},{2,3},{3,2},{4,5},{5,4},{6,7},{7,6},{8,9},{9,8},{10,11... | collective-permute-start | bytes 3145736 | tf_op jit(solution)/shard_map/cond/branch_1_fun/ppermute | solution.py:369
  14.6 15.3 %collective-permute-start.15 = (bf16[4,128,1024]{2,1,0:T(8,128)(2,1)S(1)}, bf16[4,128,1024]{2,1,0:T(8,128)(2,1)S(1)}, u32[]{:S(2)}, u32[]{:S(2)}) collective-permute-start(bf16[4,128,1024]{2,1,0:T(8,128)(2,1)S(1)} %get-tuple-element.53.refs_1_.refs_3_.refs_4_.refs_5_), channel_id=1, source_target_pairs={{0,1},{1,0},{2,3},{3,2},{4,5},{5,4},{6,7},{7,6},{8,9},{9,8},{10,11... | collective-permute-start | bytes 3145736 | tf_op jit(solution)/shard_map/cond/branch_1_fun/ppermute | solution.py:369
  15.1 14.7 %collective-permute-start.13 = (bf16[3,64,2048]{2,1,0:T(8,128)(2,1)S(1)}, bf16[3,64,2048]{2,1,0:T(8,128)(2,1)S(1)}, u32[]{:S(2)}, u32[]{:S(2)}) collective-permute-start(bf16[3,64,2048]{2,1,0:T(8,128)(2,1)S(1)} %get-tuple-element.55), channel_id=1, source_target_pairs={{1,2},{2,1},{3,4},{4,3},{5,6},{6,5},{9,10},{10,9},{11,12},{12,11},... | collective-permute-start | bytes 2359304 | tf_op jit(solution)/shard_map/cond/branch_1_fun/ppermute | solution.py:364
  15.8 23.3 %collective-permute-start.19 = (bf16[3,64,2048]{2,1,0:T(8,128)(2,1)S(1)}, bf16[3,64,2048]{2,1,0:T(8,128)(2,1)S(1)}, u32[]{:S(2)}, u32[]{:S(2)}) collective-permute-start(bf16[3,64,2048]{2,1,0:T(8,128)(2,1)S(1)} %get-tuple-element.54), channel_id=1, source_target_pairs={{1,2},{2,1},{5,6},{6,5},{9,10},{10,9},{13,14},{14,13},{17,18},{18,... | collective-permute-start | bytes 2359304 | tf_op jit(solution)/shard_map/cond/branch_1_fun/ppermute | solution.py:364
  27.5 18.7 %collective-permute-start.20 = (bf16[3,64,2048]{2,1,0:T(8,128)(2,1)S(1)}, bf16[3,64,2048]{2,1,0:T(8,128)(2,1)S(1)}, u32[]{:S(2)}, u32[]{:S(2)}) collective-permute-start(bf16[3,64,2048]{2,1,0:T(8,128)(2,1)S(1)} %collective-permute-done.12.refs_4_), channel_id=1, source_target_pairs={{7,4},{0,3},{15,12},{8,11},{23,20},{16,19},{31,28},{24,27}} | collective-permute-start | bytes 2359304 | tf_op jit(solution)/shard_map/cond/branch_1_fun/ppermute | solution.py:368
  31.6 4.7 %collective-permute-start.16 = (s16[400,128]{1,0:T(8,128)(2,1)S(1)}, s16[400,128]{1,0:T(8,128)(2,1)S(1)}, u32[]{:S(2)}, u32[]{:S(2)}) collective-permute-start(s16[400,128]{1,0:T(8,128)(2,1)S(1)} %get-tuple-element.57), channel_id=1, source_target_pairs={{0,8},{8,0},{16,24},{24,16},{1,9},{9,1},{17,25},{25,17},{2,10},{10... | collective-permute-start | bytes 307208 | tf_op jit(solution)/shard_map/cond/branch_1_fun/ppermute | solution.py:380
  36.4 12.6 %collective-permute-start.17 = (s16[400,128]{1,0:T(8,128)(2,1)S(1)}, s16[400,128]{1,0:T(8,128)(2,1)S(1)}, u32[]{:S(2)}, u32[]{:S(2)}) collective-permute-start(s16[400,128]{1,0:T(8,128)(2,1)S(1)} %branch_1_fun.16.mine.refs_7_), channel_id=1, source_target_pairs={{0,16},{8,24},{16,0},{24,8},{1,17},{9,25},{17,1},{25,9},{2,18},{10... | collective-permute-start | bytes 307208 | tf_op jit(solution)/shard_map/cond/branch_1_fun/ppermute | solution.py:384
  47.4 5.7 %collective-permute-start.21 = (s16[400,128]{1,0:T(8,128)(2,1)S(1)}, s16[400,128]{1,0:T(8,128)(2,1)S(1)}, u32[]{:S(2)}, u32[]{:S(2)}) collective-permute-start(s16[400,128]{1,0:T(8,128)(2,1)S(1)} %get-tuple-element.59), channel_id=1, source_target_pairs={{0,8},{8,0},{16,24},{24,16},{1,9},{9,1},{17,25},{25,17},{2,10},{10... | collective-permute-start | bytes 307208 | tf_op jit(solution)/shard_map/cond/branch_1_fun/ppermute | solution.py:380
  53.2 8.1 %collective-permute-start.22 = (s16[400,128]{1,0:T(8,128)(2,1)S(1)}, s16[400,128]{1,0:T(8,128)(2,1)S(1)}, u32[]{:S(2)}, u32[]{:S(2)}) collective-permute-start(s16[400,128]{1,0:T(8,128)(2,1)S(1)} %branch_1_fun.21.mine), channel_id=1, source_target_pairs={{0,16},{8,24},{16,0},{24,8},{1,17},{9,25},{17,1},{25,9},{2,18},{10... | collective-permute-start | bytes 307208 | tf_op jit(solution)/shard_map/cond/branch_1_fun/ppermute | solution.py:384
  55.9 6.2 %collective-permute-start.18 = (s16[400,128]{1,0:T(8,128)(2,1)S(1)}, s16[400,128]{1,0:T(8,128)(2,1)S(1)}, u32[]{:S(2)}, u32[]{:S(2)}) collective-permute-start(s16[400,128]{1,0:T(8,128)(2,1)S(1)} %branch_1_fun.17.rest_0_.refs_0_), channel_id=1, source_target_pairs={{0,8},{8,0},{16,24},{24,16},{1,9},{9,1},{17,25},{25,17},{2,10},{10... | collective-permute-start | bytes 307208 | tf_op jit(solution)/shard_map/cond/branch_1_fun/ppermute | solution.py:387
  61.4 4.7 %collective-permute-start.23 = (s16[400,128]{1,0:T(8,128)(2,1)S(1)}, s16[400,128]{1,0:T(8,128)(2,1)S(1)}, u32[]{:S(2)}, u32[]{:S(2)}) collective-permute-start(s16[400,128]{1,0:T(8,128)(2,1)S(1)} %branch_1_fun.22.refs_2_), channel_id=1, source_target_pairs={{0,8},{8,0},{16,24},{24,16},{1,9},{9,1},{17,25},{25,17},{2,10},{10... | collective-permute-start | bytes 307208 | tf_op jit(solution)/shard_map/cond/branch_1_fun/ppermute | solution.py:387
  66.6 0.9 %copy-start = (f32[4,3,128,128]{3,2,1,0:T(8,128)}, f32[4,3,128,128]{3,2,1,0:T(8,128)S(1)}, u32[]{:S(2)}) copy-start(f32[4,3,128,128]{3,2,1,0:T(8,128)S(1)} %get-tuple-element.116) | copy-start | bytes 2359300

commit v7 on v6

--- a/solution.py
+++ b/solution.py
@@ -23,6 +23,7 @@
 
 
 NO_COST = pl.CostEstimate(flops=0, bytes_accessed=0, transcendentals=0)
+LONG = pl.CostEstimate(flops=6 * 10**9, bytes_accessed=0, transcendentals=0)
 
 
 def piece_sizes(aux, count):
@@ -205,7 +206,7 @@
         in_specs=[ANY],
         out_specs=VMEM,
         compiler_params=params(4),
-        cost_estimate=NO_COST,
+        cost_estimate=LONG,
     )(earlier)
 
 

time: 67.7 us -> 66.3 us (0.979)
  the two profiles are of different devices: /device:TPU:0 before, /device:TPU:12 now
where the time goes in v7:
time: 66.3 us; the launch traced here: 66.1 us
  waiting for transfers between devices  33.2 us (50%)
  starting transfers between devices  19.2 us (29%)
  Pallas kernels  10.2 us (15%)
  other arithmetic  1.59 us (2%)
  local copies, waits for them, and re-layouts  0.88 us (1%)
  between operations  0.71 us (1%)
    ppermute x1, waiting for transfers between devices, exchange(): lax.ppermute(early, 'bas', across)  11 us
    ppermute x2, waiting for transfers between devices, exchange(): lax.ppermute(sent, 'aux', flipped(layers, 1))  6.95 us
    ppermute x2, starting transfers between devices, exchange(): lax.ppermute(mine, 'aux', flipped(layers, mask))  5.36 us
    ppermute x2, waiting for transfers between devices, exchange(): lax.ppermute(mine, 'aux', flipped(layers, mask))  4.86 us
    ppermute x1, waiting for transfers between devices, exchange(): halfway = [lax.ppermute(part, 'bas', there) for part in late]  4.42 us
    ppermute x2, waiting for transfers between devices, exchange(): coded += [mine, lax.ppermute(mine, 'aux', flipped(layers, 1))]  4.28 us
    ppermute x1, starting transfers between devices, exchange(): lax.ppermute(early, 'bas', across)  3.73 us
    pallas_call x2, Pallas kernels, chunk_tiles(): pl.pallas_call(kernel, out_shape=[jax.ShapeDtypeStruct((half * rows, widt...  2.94 us
  transfers between devices with their start and end apart: 15, of which 9 were waited for; matrix products, arithmetic and copies ran while one was open for 2% of the time, Pallas kernels for 11%

profile of v7, /device:TPU:12, one launch (start us, length us, event | category | flops | bytes accessed | tf_op | source)
XLA Modules:
  0.0 66.1 jit_solution(12195207155763627817)
XLA Ops:
  0.0 0.8 %collective-permute-start.24 = (bf16[512,256]{1,0:T(8,128)(2,1)}, bf16[512,256]{1,0:T(8,128)(2,1)S(1)}, u32[]{:S(2)}, u32[]{:S(2)}) collective-permute-start(bf16[512,256]{1,0:T(8,128)(2,1)} %own.1), channel_id=1, source_target_pairs={{1,2},{2,1},{5,6},{6,5},{9,10},{10,9},{13,14},{14,13},{17,18},{18,... | collective-permute-start | bytes 786440 | tf_op jit(solution)/shard_map/ppermute | solution.py:354
  0.8 2.8 %collective-permute-start.25 = (bf16[512,256]{1,0:T(8,128)(2,1)}, bf16[512,256]{1,0:T(8,128)(2,1)}, u32[]{:S(2)}, u32[]{:S(2)}) collective-permute-start(bf16[512,256]{1,0:T(8,128)(2,1)} %own.1), channel_id=1, source_target_pairs={{3,4},{4,3},{11,12},{12,11},{19,20},{20,19},{27,28},{28,27}} | collective-permute-start | bytes 786440 | tf_op jit(solution)/shard_map/ppermute | solution.py:356
  3.6 1.4 %collective-permute-start.26 = (bf16[512,256]{1,0:T(8,128)(2,1)}, bf16[512,256]{1,0:T(8,128)(2,1)}, u32[]{:S(2)}, u32[]{:S(2)}) collective-permute-start(bf16[512,256]{1,0:T(8,128)(2,1)} %own.1), channel_id=1, source_target_pairs={{0,1},{1,0},{2,3},{3,2},{4,5},{5,4},{6,7},{7,6},{8,9},{9,8},{10,11... | collective-permute-start | bytes 786440 | tf_op jit(solution)/shard_map/ppermute | solution.py:357
  5.0 0.9 %and_reduce_fusion = pred[8,4]{0,1:T(4,128)(4,1)S(1)} fusion(s32[8,4]{0,1:T(4,128)} %constant.15, s32[3,32]{1,0:T(4,128)} %bitcast.1, pred[8,32]{1,0:T(8,128)(4,1)} %constant.16), kind=kLoop, calls=%fused_computation | loop fusion | flops 9184 | bytes 800 | tf_op jit(solution)/shard_map/reduce_or | solution.py:45
  7.3 2.0 %shard_map.57 = (bf16[8,4,3,128,128]{4,3,2,1,0:T(8,128)(2,1)S(1)}, bf16[512,256]{1,0:T(8,128)(2,1)S(1)}) custom-call(bf16[8,4,3,128,128]{4,3,2,1,0:T(8,128)(2,1)} %tensor.1, bf16[512,256]{1,0:T(8,128)(2,1)} %own.1), custom_call_target="tpu_custom_call" | custom-call | tf_op jit(solution)/shard_map/pallas_call | solution.py:66
  9.3 1.6 %collective-permute-done.25 = bf16[512,256]{1,0:T(8,128)(2,1)} collective-permute-done((bf16[512,256]{1,0:T(8,128)(2,1)}, bf16[512,256]{1,0:T(8,128)(2,1)}, u32[]{:S(2)}, u32[]{:S(2)}) %collective-permute-start.25) | collective-permute-done | bytes 262176 | tf_op jit(solution)/shard_map/ppermute | solution.py:356
  10.9 54.3 %conditional.1 = (f32[4,3,128,128]{3,2,1,0:T(8,128)S(1)}) conditional(s32[]{:T(128)} %convert_element_type.7, (s32[3,32]{1,0:T(4,128)S(1)}, bf16[512,256]{1,0:T(8,128)(2,1)S(1)}, bf16[512,256]{1,0:T(8,128)(2,1)S(1)}, bf16[512,256]{1,0:T(8,128)(2,1)}, bf16[512,256]{1,0:T(8,128)(2,1)}, /*index=5*/bf16[8,4,3,128,128]{4,3,2,1,0:T(8,128)(2,1)S(1)}) %tuple.17, ...), branch_computations={%region_3.0_spmd, %region_4.0_spmd} | conditional | flops 6000000000 | bytes 27623912 | solution.py:394
  10.9 2.4 %branch_1_fun.12 = (bf16[3,64,2048]{2,1,0:T(8,128)(2,1)S(1)}, bf16[3,64,2048]{2,1,0:T(8,128)(2,1)S(1)}, bf16[4,128,1024]{2,1,0:T(8,128)(2,1)S(1)}, bf16[4,128,1024]{2,1,0:T(8,128)(2,1)S(1)}) custom-call(s32[3,32]{1,0:T(4,128)S(1)} %get-tuple-element.46.pattern.refs_0_, bf16[512,256]{1,0:T(8,128)(2,1)S(1)} %get-tuple-element.47.own, ...), custom_call_target="tpu_custom_call" | custom-call | tf_op jit(solution)/shard_map/cond/branch_1_fun/pallas_call | solution.py:135
  13.3 1.3 %collective-permute-start.12 = (bf16[3,64,2048]{2,1,0:T(8,128)(2,1)S(1)}, bf16[3,64,2048]{2,1,0:T(8,128)(2,1)S(1)}, u32[]{:S(2)}, u32[]{:S(2)}) collective-permute-start(bf16[3,64,2048]{2,1,0:T(8,128)(2,1)S(1)} %get-tuple-element.54), channel_id=1, source_target_pairs={{3,7},{4,0},{11,15},{12,8},{19,23},{20,16},{27,31},{28,24}} | collective-permute-start | bytes 2359304 | tf_op jit(solution)/shard_map/cond/branch_1_fun/ppermute | solution.py:367
  14.7 3.7 %collective-permute-start.13 = (bf16[3,64,2048]{2,1,0:T(8,128)(2,1)S(1)}, bf16[3,64,2048]{2,1,0:T(8,128)(2,1)S(1)}, u32[]{:S(2)}, u32[]{:S(2)}) collective-permute-start(bf16[3,64,2048]{2,1,0:T(8,128)(2,1)S(1)} %get-tuple-element.55), channel_id=1, source_target_pairs={{1,2},{2,1},{3,4},{4,3},{5,6},{6,5},{9,10},{10,9},{11,12},{12,11},... | collective-permute-start | bytes 2359304 | tf_op jit(solution)/shard_map/cond/branch_1_fun/ppermute | solution.py:365
  19.7 4.4 %collective-permute-done.12.refs_4_ = bf16[3,64,2048]{2,1,0:T(8,128)(2,1)S(1)} collective-permute-done((bf16[3,64,2048]{2,1,0:T(8,128)(2,1)S(1)}, bf16[3,64,2048]{2,1,0:T(8,128)(2,1)S(1)}, u32[]{:S(2)}, u32[]{:S(2)}) %collective-permute-start.12) | collective-permute-done | bytes 786464 | tf_op jit(solution)/shard_map/cond/branch_1_fun/ppermute | solution.py:367
  24.1 1.5 %collective-permute-start.20 = (bf16[3,64,2048]{2,1,0:T(8,128)(2,1)S(1)}, bf16[3,64,2048]{2,1,0:T(8,128)(2,1)S(1)}, u32[]{:S(2)}, u32[]{:S(2)}) collective-permute-start(bf16[3,64,2048]{2,1,0:T(8,128)(2,1)S(1)} %collective-permute-done.12.refs_4_), channel_id=1, source_target_pairs={{7,4},{0,3},{15,12},{8,11},{23,20},{16,19},{31,28},{24,27}} | collective-permute-start | bytes 2359304 | tf_op jit(solution)/shard_map/cond/branch_1_fun/ppermute | solution.py:369
  25.6 0.7 %branch_1_fun.13.refs_1_ = f32[256,512]{1,0:T(8,128)S(1)} custom-call(bf16[4,128,1024]{2,1,0:T(8,128)(2,1)S(1)} %get-tuple-element.52.refs_0_.refs_2_.refs_3_.refs_4_, bf16[4,128,1024]{2,1,0:T(8,128)(2,1)S(1)} %get-tuple-element.53.refs_1_.refs_3_.refs_4_.refs_5_, bf16[4,128,1024]{2,1,0:T(8,128)(2,1)S(1)} %get-tuple-element.52.refs_0_.refs_2_.refs_3_.refs_4_, ...), custom_call_target="tpu_custom_call" | custom-call | tf_op jit(solution)/shard_map/cond/branch_1_fun/pallas_call | solution.py:188
  26.3 11.0 %collective-permute-done.13._.refs_2_ = bf16[3,64,2048]{2,1,0:T(8,128)(2,1)S(1)} collective-permute-done((bf16[3,64,2048]{2,1,0:T(8,128)(2,1)S(1)}, bf16[3,64,2048]{2,1,0:T(8,128)(2,1)S(1)}, u32[]{:S(2)}, u32[]{:S(2)}) %collective-permute-start.13) | collective-permute-done | bytes 786464 | tf_op jit(solution)/shard_map/cond/branch_1_fun/ppermute | solution.py:365
  37.4 1.8 %branch_1_fun.15 = (f32[384,128]{1,0:T(8,128)S(1)}, s16[400,128]{1,0:T(8,128)(2,1)S(1)}) custom-call(s32[3,32]{1,0:T(4,128)S(1)} %get-tuple-element.46.pattern.refs_0_, f32[256,512]{1,0:T(8,128)S(1)} %branch_1_fun.13.refs_1_, bf16[3,64,2048]{2,1,0:T(8,128)(2,1)S(1)} %collective-permute-done.13._.refs_2_, ...), custom_call_target="tpu_custom_call" | custom-call | tf_op jit(solution)/shard_map/cond/branch_1_fun/pallas_call | solution.py:273
  41.2 2.7 %collective-permute-done.16.other = s16[400,128]{1,0:T(8,128)(2,1)S(1)} collective-permute-done((s16[400,128]{1,0:T(8,128)(2,1)S(1)}, s16[400,128]{1,0:T(8,128)(2,1)S(1)}, u32[]{:S(2)}, u32[]{:S(2)}) %collective-permute-start.16) | collective-permute-done | bytes 102432 | tf_op jit(solution)/shard_map/cond/branch_1_fun/ppermute | solution.py:381
  43.9 3.2 %collective-permute-start.17 = (s16[400,128]{1,0:T(8,128)(2,1)S(1)}, s16[400,128]{1,0:T(8,128)(2,1)S(1)}, u32[]{:S(2)}, u32[]{:S(2)}) collective-permute-start(s16[400,128]{1,0:T(8,128)(2,1)S(1)} %branch_1_fun.16.mine.refs_7_), channel_id=1, source_target_pairs={{0,16},{8,24},{16,0},{24,8},{1,17},{9,25},{17,1},{25,9},{2,18},{10... | collective-permute-start | bytes 307208 | tf_op jit(solution)/shard_map/cond/branch_1_fun/ppermute | solution.py:385
  47.2 1.2 %branch_1_fun.20 = (f32[384,128]{1,0:T(8,128)S(1)}, s16[400,128]{1,0:T(8,128)(2,1)S(1)}) custom-call(s32[3,32]{1,0:T(4,128)S(1)} %get-tuple-element.46.pattern.refs_0_, f32[256,512]{1,0:T(8,128)S(1)} %branch_1_fun.18.refs_1_, bf16[3,64,2048]{2,1,0:T(8,128)(2,1)S(1)} %collective-permute-done.19.refs_2_, ...), custom_call_target="tpu_custom_call" | custom-call | tf_op jit(solution)/shard_map/cond/branch_1_fun/pallas_call | solution.py:273
  48.4 1.4 %collective-permute-done.17.other = s16[400,128]{1,0:T(8,128)(2,1)S(1)} collective-permute-done((s16[400,128]{1,0:T(8,128)(2,1)S(1)}, s16[400,128]{1,0:T(8,128)(2,1)S(1)}, u32[]{:S(2)}, u32[]{:S(2)}) %collective-permute-start.17) | collective-permute-done | bytes 102432 | tf_op jit(solution)/shard_map/cond/branch_1_fun/ppermute | solution.py:385
  49.9 4.2 %collective-permute-done.21.other = s16[400,128]{1,0:T(8,128)(2,1)S(1)} collective-permute-done((s16[400,128]{1,0:T(8,128)(2,1)S(1)}, s16[400,128]{1,0:T(8,128)(2,1)S(1)}, u32[]{:S(2)}, u32[]{:S(2)}) %collective-permute-start.21) | collective-permute-done | bytes 102432 | tf_op jit(solution)/shard_map/cond/branch_1_fun/ppermute | solution.py:381
  54.2 2.1 %collective-permute-start.22 = (s16[400,128]{1,0:T(8,128)(2,1)S(1)}, s16[400,128]{1,0:T(8,128)(2,1)S(1)}, u32[]{:S(2)}, u32[]{:S(2)}) collective-permute-start(s16[400,128]{1,0:T(8,128)(2,1)S(1)} %branch_1_fun.21.mine), channel_id=1, source_target_pairs={{0,16},{8,24},{16,0},{24,8},{1,17},{9,25},{17,1},{25,9},{2,18},{10... | collective-permute-start | bytes 307208 | tf_op jit(solution)/shard_map/cond/branch_1_fun/ppermute | solution.py:385
  56.4 3.5 %collective-permute-done.22.other = s16[400,128]{1,0:T(8,128)(2,1)S(1)} collective-permute-done((s16[400,128]{1,0:T(8,128)(2,1)S(1)}, s16[400,128]{1,0:T(8,128)(2,1)S(1)}, u32[]{:S(2)}, u32[]{:S(2)}) %collective-permute-start.22) | collective-permute-done | bytes 102432 | tf_op jit(solution)/shard_map/cond/branch_1_fun/ppermute | solution.py:385
  61.0 3.7 %collective-permute-done.23.refs_3_ = s16[400,128]{1,0:T(8,128)(2,1)S(1)} collective-permute-done((s16[400,128]{1,0:T(8,128)(2,1)S(1)}, s16[400,128]{1,0:T(8,128)(2,1)S(1)}, u32[]{:S(2)}, u32[]{:S(2)}) %collective-permute-start.23) | collective-permute-done | bytes 102432 | tf_op jit(solution)/shard_map/cond/branch_1_fun/ppermute | solution.py:388
  65.2 0.9 %copy-done = f32[4,3,128,128]{3,2,1,0:T(8,128)} copy-done((f32[4,3,128,128]{3,2,1,0:T(8,128)}, f32[4,3,128,128]{3,2,1,0:T(8,128)S(1)}, u32[]{:S(2)}) %copy-start) | copy-done | bytes 786456
  (27 shorter events, 5.7 us)
Async XLA Ops:
  0.0 10.9 %copy-start.1 = (s32[32,3]{0,1:T(4,128)S(1)}, s32[32,3]{0,1:T(4,128)}, u32[]{:S(2)}) copy-start(s32[32,3]{0,1:T(4,128)} %param.9) | copy-start | bytes 1156
  0.0 9.3 %collective-permute-start.24 = (bf16[512,256]{1,0:T(8,128)(2,1)}, bf16[512,256]{1,0:T(8,128)(2,1)S(1)}, u32[]{:S(2)}, u32[]{:S(2)}) collective-permute-start(bf16[512,256]{1,0:T(8,128)(2,1)} %own.1), channel_id=1, source_target_pairs={{1,2},{2,1},{5,6},{6,5},{9,10},{10,9},{13,14},{14,13},{17,18},{18,... | collective-permute-start | bytes 786440 | tf_op jit(solution)/shard_map/ppermute | solution.py:354
  0.8 10.1 %collective-permute-start.25 = (bf16[512,256]{1,0:T(8,128)(2,1)}, bf16[512,256]{1,0:T(8,128)(2,1)}, u32[]{:S(2)}, u32[]{:S(2)}) collective-permute-start(bf16[512,256]{1,0:T(8,128)(2,1)} %own.1), channel_id=1, source_target_pairs={{3,4},{4,3},{11,12},{12,11},{19,20},{20,19},{27,28},{28,27}} | collective-permute-start | bytes 786440 | tf_op jit(solution)/shard_map/ppermute | solution.py:356
  3.6 7.3 %collective-permute-start.26 = (bf16[512,256]{1,0:T(8,128)(2,1)}, bf16[512,256]{1,0:T(8,128)(2,1)}, u32[]{:S(2)}, u32[]{:S(2)}) collective-permute-start(bf16[512,256]{1,0:T(8,128)(2,1)} %own.1), channel_id=1, source_target_pairs={{0,1},{1,0},{2,3},{3,2},{4,5},{5,4},{6,7},{7,6},{8,9},{9,8},{10,11... | collective-permute-start | bytes 786440 | tf_op jit(solution)/shard_map/ppermute | solution.py:357
  13.3 10.8 %collective-permute-start.12 = (bf16[3,64,2048]{2,1,0:T(8,128)(2,1)S(1)}, bf16[3,64,2048]{2,1,0:T(8,128)(2,1)S(1)}, u32[]{:S(2)}, u32[]{:S(2)}) collective-permute-start(bf16[3,64,2048]{2,1,0:T(8,128)(2,1)S(1)} %get-tuple-element.54), channel_id=1, source_target_pairs={{3,7},{4,0},{11,15},{12,8},{19,23},{20,16},{27,31},{28,24}} | collective-permute-start | bytes 2359304 | tf_op jit(solution)/shard_map/cond/branch_1_fun/ppermute | solution.py:367
  14.7 22.7 %collective-permute-start.13 = (bf16[3,64,2048]{2,1,0:T(8,128)(2,1)S(1)}, bf16[3,64,2048]{2,1,0:T(8,128)(2,1)S(1)}, u32[]{:S(2)}, u32[]{:S(2)}) collective-permute-start(bf16[3,64,2048]{2,1,0:T(8,128)(2,1)S(1)} %get-tuple-element.55), channel_id=1, source_target_pairs={{1,2},{2,1},{3,4},{4,3},{5,6},{6,5},{9,10},{10,9},{11,12},{12,11},... | collective-permute-start | bytes 2359304 | tf_op jit(solution)/shard_map/cond/branch_1_fun/ppermute | solution.py:365
  18.4 19.0 %collective-permute-start.14 = (bf16[4,128,1024]{2,1,0:T(8,128)(2,1)S(1)}, bf16[4,128,1024]{2,1,0:T(8,128)(2,1)S(1)}, u32[]{:S(2)}, u32[]{:S(2)}) collective-permute-start(bf16[4,128,1024]{2,1,0:T(8,128)(2,1)S(1)} %get-tuple-element.52.refs_0_.refs_2_.refs_3_.refs_4_), channel_id=1, source_target_pairs={{0,1},{1,0},{2,3},{3,2},{4,5},{5,4},{6,7},{7,6},{8,9},{9,8},{10,11... | collective-permute-start | bytes 3145736 | tf_op jit(solution)/shard_map/cond/branch_1_fun/ppermute | solution.py:370
  18.5 18.9 %collective-permute-start.15 = (bf16[4,128,1024]{2,1,0:T(8,128)(2,1)S(1)}, bf16[4,128,1024]{2,1,0:T(8,128)(2,1)S(1)}, u32[]{:S(2)}, u32[]{:S(2)}) collective-permute-start(bf16[4,128,1024]{2,1,0:T(8,128)(2,1)S(1)} %get-tuple-element.53.refs_1_.refs_3_.refs_4_.refs_5_), channel_id=1, source_target_pairs={{0,1},{1,0},{2,3},{3,2},{4,5},{5,4},{6,7},{7,6},{8,9},{9,8},{10,11... | collective-permute-start | bytes 3145736 | tf_op jit(solution)/shard_map/cond/branch_1_fun/ppermute | solution.py:370
  19.0 28.2 %collective-permute-start.19 = (bf16[3,64,2048]{2,1,0:T(8,128)(2,1)S(1)}, bf16[3,64,2048]{2,1,0:T(8,128)(2,1)S(1)}, u32[]{:S(2)}, u32[]{:S(2)}) collective-permute-start(bf16[3,64,2048]{2,1,0:T(8,128)(2,1)S(1)} %get-tuple-element.54), channel_id=1, source_target_pairs={{1,2},{2,1},{5,6},{6,5},{9,10},{10,9},{13,14},{14,13},{17,18},{18,... | collective-permute-start | bytes 2359304 | tf_op jit(solution)/shard_map/cond/branch_1_fun/ppermute | solution.py:365
  24.1 23.1 %collective-permute-start.20 = (bf16[3,64,2048]{2,1,0:T(8,128)(2,1)S(1)}, bf16[3,64,2048]{2,1,0:T(8,128)(2,1)S(1)}, u32[]{:S(2)}, u32[]{:S(2)}) collective-permute-start(bf16[3,64,2048]{2,1,0:T(8,128)(2,1)S(1)} %collective-permute-done.12.refs_4_), channel_id=1, source_target_pairs={{7,4},{0,3},{15,12},{8,11},{23,20},{16,19},{31,28},{24,27}} | collective-permute-start | bytes 2359304 | tf_op jit(solution)/shard_map/cond/branch_1_fun/ppermute | solution.py:369
  39.1 4.7 %collective-permute-start.16 = (s16[400,128]{1,0:T(8,128)(2,1)S(1)}, s16[400,128]{1,0:T(8,128)(2,1)S(1)}, u32[]{:S(2)}, u32[]{:S(2)}) collective-permute-start(s16[400,128]{1,0:T(8,128)(2,1)S(1)} %get-tuple-element.57), channel_id=1, source_target_pairs={{0,8},{8,0},{16,24},{24,16},{1,9},{9,1},{17,25},{25,17},{2,10},{10... | collective-permute-start | bytes 307208 | tf_op jit(solution)/shard_map/cond/branch_1_fun/ppermute | solution.py:381
  43.9 5.9 %collective-permute-start.17 = (s16[400,128]{1,0:T(8,128)(2,1)S(1)}, s16[400,128]{1,0:T(8,128)(2,1)S(1)}, u32[]{:S(2)}, u32[]{:S(2)}) collective-permute-start(s16[400,128]{1,0:T(8,128)(2,1)S(1)} %branch_1_fun.16.mine.refs_7_), channel_id=1, source_target_pairs={{0,16},{8,24},{16,0},{24,8},{1,17},{9,25},{17,1},{25,9},{2,18},{10... | collective-permute-start | bytes 307208 | tf_op jit(solution)/shard_map/cond/branch_1_fun/ppermute | solution.py:385
  48.4 5.8 %collective-permute-start.21 = (s16[400,128]{1,0:T(8,128)(2,1)S(1)}, s16[400,128]{1,0:T(8,128)(2,1)S(1)}, u32[]{:S(2)}, u32[]{:S(2)}) collective-permute-start(s16[400,128]{1,0:T(8,128)(2,1)S(1)} %get-tuple-element.59), channel_id=1, source_target_pairs={{0,8},{8,0},{16,24},{24,16},{1,9},{9,1},{17,25},{25,17},{2,10},{10... | collective-permute-start | bytes 307208 | tf_op jit(solution)/shard_map/cond/branch_1_fun/ppermute | solution.py:381
  54.2 5.6 %collective-permute-start.22 = (s16[400,128]{1,0:T(8,128)(2,1)S(1)}, s16[400,128]{1,0:T(8,128)(2,1)S(1)}, u32[]{:S(2)}, u32[]{:S(2)}) collective-permute-start(s16[400,128]{1,0:T(8,128)(2,1)S(1)} %branch_1_fun.21.mine), channel_id=1, source_target_pairs={{0,16},{8,24},{16,0},{24,8},{1,17},{9,25},{17,1},{25,9},{2,18},{10... | collective-permute-start | bytes 307208 | tf_op jit(solution)/shard_map/cond/branch_1_fun/ppermute | solution.py:385
  56.4 4.7 %collective-permute-start.18 = (s16[400,128]{1,0:T(8,128)(2,1)S(1)}, s16[400,128]{1,0:T(8,128)(2,1)S(1)}, u32[]{:S(2)}, u32[]{:S(2)}) collective-permute-start(s16[400,128]{1,0:T(8,128)(2,1)S(1)} %branch_1_fun.17.rest_0_.refs_0_), channel_id=1, source_target_pairs={{0,8},{8,0},{16,24},{24,16},{1,9},{9,1},{17,25},{25,17},{2,10},{10... | collective-permute-start | bytes 307208 | tf_op jit(solution)/shard_map/cond/branch_1_fun/ppermute | solution.py:388
  60.0 4.7 %collective-permute-start.23 = (s16[400,128]{1,0:T(8,128)(2,1)S(1)}, s16[400,128]{1,0:T(8,128)(2,1)S(1)}, u32[]{:S(2)}, u32[]{:S(2)}) collective-permute-start(s16[400,128]{1,0:T(8,128)(2,1)S(1)} %branch_1_fun.22.refs_2_), channel_id=1, source_target_pairs={{0,8},{8,0},{16,24},{24,16},{1,9},{9,1},{17,25},{25,17},{2,10},{10... | collective-permute-start | bytes 307208 | tf_op jit(solution)/shard_map/cond/branch_1_fun/ppermute | solution.py:388
  65.2 0.9 %copy-start = (f32[4,3,128,128]{3,2,1,0:T(8,128)}, f32[4,3,128,128]{3,2,1,0:T(8,128)S(1)}, u32[]{:S(2)}) copy-start(f32[4,3,128,128]{3,2,1,0:T(8,128)S(1)} %get-tuple-element.116) | copy-start | bytes 2359300
